TPU v7x, 32 devices: a whole 2x2x4 slice. The times are simulated.
32 devices in a mesh: groups: 2 (over y), ctx: 4 (over z), dp: 2 (over x), mp: 2 (over core).
Axes of the slice: x: 2, y: 2, z: 4, core: 2. Of those that a mesh axis runs over, the one named last changes fastest.
Arguments:
- positions: int32 [4, 512], P(('groups', 'dp')), parts along dimension 0, may hold values from 0 to 4095, as said below
- queries: bfloat16 [4, 1024, 4096], P(('groups', 'dp'), 'ctx', 'mp'), parts along dimension 0, may hold values from -4 to 4
- keys: bfloat16 [4, 1024, 512], P(('groups', 'dp'), 'ctx', 'mp'), parts along dimension 0, may hold values from -36 to 36
- values: bfloat16 [4, 1024, 512], P(('groups', 'dp'), 'ctx', 'mp'), parts along dimension 0, may hold values from -6 to 6
- out_grad: bfloat16 [4, 1024, 4096], P(('groups', 'dp'), 'ctx', 'mp'), parts along dimension 0, may hold values from -6 to 6
Outputs:
- query_grad: bfloat16 [4, 1024, 4096], P(('groups', 'dp'), 'ctx', 'mp'), parts along dimension 0
- key_grad: bfloat16 [4, 1024, 512], P(('groups', 'dp'), 'ctx', 'mp'), parts along dimension 0
- value_grad: bfloat16 [4, 1024, 512], P(('groups', 'dp'), 'ctx', 'mp'), parts along dimension 0
There are 2 independent parts, one for each index of `groups`. A program takes and returns all parts, laid end to end along the dimension named above; each array names one. Nothing has to cross between parts.
Inputs may be any that keep to these rules, and one draw needn't show every extreme that they name: In each sequence the positions rise strictly with the rank; the shard k * 1024 to (k + 1) * 1024 - 1 holds at most 256 of them, and some shard holds exactly 256.
All inputs are finite; a program needn't handle non-finite values.
Results may differ from a plain program's by a relative error of at most 0.007.
The roundings to bfloat16 on the way count: a program that leaves them out, or rounds other values in their place, can miss the bound.
Values may be sent and summed in bfloat16 or wider, within the bound.
No kernel may reach another device: no remote copies, remote signals or barrier semaphores. Data moves between devices by JAX's collectives and lax.ppermute only.
A program may use at most 128 MiB of HBM per device.

v0:
```python
import functools
import math

import jax
import jax.numpy as jnp
import numpy as np
from jax import lax
from jax.experimental import pallas as pl
from jax.experimental.pallas import tpu as pltpu
from jax.sharding import PartitionSpec as P

HEAD_DIM = 128
HALF_DIM = HEAD_DIM // 2
TOK_SHARD = 1024
ROPE_BASE = 500000.0
SCORE_SCALE = 1.0 / math.sqrt(HEAD_DIM)
EXP2_SCALE = SCORE_SCALE * math.log2(math.e)
HIDDEN = -1e30
ALIGN = 16
CHUNK = 288
MIB = 1024 * 1024

VMEM = pl.BlockSpec(memory_space=pltpu.VMEM)
SMEM = pl.BlockSpec(memory_space=pltpu.SMEM)
HBM = pl.BlockSpec(memory_space=pltpu.HBM)


def vmem(routed, small, large):
    return pltpu.CompilerParams(vmem_limit_bytes=(small if routed <= 512 else large) * MIB)


def dot(left, right, contract):
    return lax.dot_general(left, right, (contract, ((), ())), preferred_element_type=jnp.float32)


def turn(field, cos_full, sin_full):
    return field * cos_full + pltpu.roll(field, HALF_DIM, 1) * sin_full


def turn_back(field, cos_full, sin_full):
    return field * cos_full - pltpu.roll(field, HALF_DIM, 1) * sin_full


def frequencies():
    ladder = np.arange(HALF_DIM, dtype=np.float32)
    exponent = ladder * np.float32(-2.0 * math.log(ROPE_BASE) / HEAD_DIM)
    freq = np.exp(exponent.astype(np.float64)).astype(np.float32)
    entry = lax.broadcasted_iota(jnp.int32, (1, HEAD_DIM), 1) % HALF_DIM
    row = jnp.zeros((1, HEAD_DIM), jnp.float32)
    for index in range(HALF_DIM):
        row = jnp.where(entry == index, float(freq[index]), row)
    return row


def shard_layout(ctx_size, me, pos, meta_ref):
    shard_of = pos // TOK_SHARD
    for hop in range(2 * ctx_size):
        meta_ref[hop] = 0
    start = jnp.int32(0)
    first = jnp.int32(0)
    my_first = jnp.int32(0)
    for shard in range(ctx_size):
        count = jnp.sum(jnp.where(shard_of == shard, 1.0, 0.0)).astype(jnp.int32)
        my_first = jnp.where(me == shard, first, my_first)

        @pl.when(me >= shard)
        def _():
            meta_ref[me - shard] = start
            meta_ref[ctx_size + me - shard] = count

        first = first + count
        start = start + (count + ALIGN - 1) // ALIGN * ALIGN
    return my_first


def prepare_kernel(
    ctx_size, pos_hbm, keys_hbm, values_hbm, meta_ref, cos_ref, sin_ref, sent_ref, *refs
):
    pos_ref, keys_ref, values_ref, sems = refs
    sources = (pos_hbm, keys_hbm, values_hbm)
    targets = (pos_ref, keys_ref, values_ref)
    copies = [
        pltpu.make_async_copy(source, target, sems.at[index])
        for index, (source, target) in enumerate(zip(sources, targets))
    ]
    for copy in copies:
        copy.start()
    copies[0].wait()
    slots = keys_ref.shape[0]
    pos = pos_ref[...]
    my_first = shard_layout(ctx_size, lax.axis_index("ctx"), pos, meta_ref)
    shape = (slots, pos.shape[1])
    gap = lax.broadcasted_iota(jnp.int32, shape, 1) - lax.broadcasted_iota(jnp.int32, shape, 0)
    named = jnp.where(gap == my_first, pos.astype(jnp.float32), 0.0)
    angles = jnp.sum(named, axis=1, keepdims=True) * frequencies()
    cos_full = jnp.cos(angles)
    front = lax.broadcasted_iota(jnp.int32, angles.shape, 1) < HALF_DIM
    sin_full = jnp.where(front, -jnp.sin(angles), jnp.sin(angles))
    cos_ref[...] = cos_full
    sin_ref[...] = sin_full
    copies[1].wait()
    copies[2].wait()
    for lane in range(0, keys_ref.shape[1], HEAD_DIM):
        lanes = slice(lane, lane + HEAD_DIM)
        key = turn(keys_ref[:, lanes].astype(jnp.float32), cos_full, sin_full)
        middle = 2 * lane + HEAD_DIM
        sent_ref[:, 2 * lane : middle] = key.astype(jnp.bfloat16)
        sent_ref[:, middle : middle + HEAD_DIM] = values_ref[:, lanes]


def prepare(positions, keys, values, ctx_size):
    slots, width = keys.shape
    table = jax.ShapeDtypeStruct((slots, HEAD_DIM), jnp.float32)
    sent = jax.ShapeDtypeStruct((slots, 2 * width), jnp.bfloat16)
    operands = (positions, keys, values)
    return pl.pallas_call(
        functools.partial(prepare_kernel, ctx_size),
        out_shape=(
            jax.ShapeDtypeStruct((2 * ctx_size,), jnp.int32),
            table,
            table,
            sent,
        ),
        in_specs=[HBM] * 3,
        out_specs=(SMEM, VMEM, VMEM, VMEM),
        scratch_shapes=[pltpu.VMEM(operand.shape, operand.dtype) for operand in operands]
        + [pltpu.SemaphoreType.DMA((3,))],
        compiler_params=vmem(positions.shape[1], 60, 60),
        name="prepare",
    )(*operands)


def queries_kernel(
    cos_ref,
    sin_ref,
    query_ref,
    grad_ref,
    sent_ref,
    turned_ref,
    turned_t_ref,
    grad_t_ref,
    sent_again_ref,
):
    sent_again_ref[...] = sent_ref[...]
    for lane in range(0, query_ref.shape[1], HEAD_DIM):
        lanes = slice(lane, lane + HEAD_DIM)
        query = turn(query_ref[:, lanes].astype(jnp.float32), cos_ref[...], sin_ref[...])
        turned_ref[:, lanes] = query.astype(jnp.bfloat16)
        turned_t_ref[lanes, :] = query.T.astype(jnp.bfloat16)
        grad_t_ref[lanes, :] = grad_ref[:, lanes].astype(jnp.float32).T.astype(jnp.bfloat16)


def rotate_queries(cos_full, sin_full, queries, out_grad, sent):
    slots, width = queries.shape
    straight = jax.ShapeDtypeStruct((slots, width), jnp.bfloat16)
    across = jax.ShapeDtypeStruct((width, slots), jnp.bfloat16)
    return pl.pallas_call(
        queries_kernel,
        out_shape=(straight, across, across, jax.ShapeDtypeStruct(sent.shape, sent.dtype)),
        in_specs=[VMEM] * 5,
        out_specs=(VMEM,) * 4,
        compiler_params=vmem(0, 16, 16),
        cost_estimate=pl.CostEstimate(
            flops=3 * 10**9, bytes_accessed=4 * 1024 * 1024, transcendentals=0
        ),
        name="rotate_queries",
    )(cos_full, sin_full, queries, out_grad, sent)


def stacked(ref, lane, heads, width):
    parts = [ref[:width, lane + h * HEAD_DIM : lane + (h + 1) * HEAD_DIM] for h in range(heads)]
    return jnp.concatenate(parts, axis=0)


def beside(ref, rows, heads, slots, width):
    if width == slots:
        return ref[:rows, :]
    columns = [head * slots for head in range(heads)]
    return jnp.concatenate([ref[:rows, start : start + width] for start in columns], axis=1)


def terms_of(probs, score_grads, queries, grads):
    key_term = dot(score_grads, queries, ((1,), (0,))) * SCORE_SCALE
    return jnp.concatenate([key_term, dot(probs, grads, ((1,), (0,)))], axis=1)


def fold(field, join, reduce):
    while field.shape[0] % 16 == 0:
        half = field.shape[0] // 2
        field = join(field[:half], field[half:])
    return reduce(field, axis=0, keepdims=True)


def head_lanes(head):
    return slice(head * HEAD_DIM, (head + 1) * HEAD_DIM)


def key_lanes(key_head):
    return slice(2 * key_head * HEAD_DIM, (2 * key_head + 1) * HEAD_DIM)


def value_lanes(key_head):
    return slice((2 * key_head + 1) * HEAD_DIM, 2 * (key_head + 1) * HEAD_DIM)


def own_kernel(step_heads, sent_ref, turned_t_ref, grad_t_ref, weight_ref, product_ref, sums_ref, bias_ref):
    slots = sent_ref.shape[0]
    key_heads = sent_ref.shape[1] // HEAD_DIM // 2
    heads = turned_t_ref.shape[0] // HEAD_DIM // key_heads
    key_id = lax.broadcasted_iota(jnp.int32, (slots, slots), 0)
    slot_id = lax.broadcasted_iota(jnp.int32, (slots, slots), 1)
    bias_ref[...] = jnp.where(key_id <= slot_id, 0.0, HIDDEN)
    for key_head in range(key_heads):

        def step(index, carry):
            for part in range(step_heads):
                head = key_head * heads + index * step_heads + part
                rows = pl.ds(pl.multiple_of(head * HEAD_DIM, HEAD_DIM), HEAD_DIM)
                scores = dot(sent_ref[:, key_lanes(key_head)], turned_t_ref[rows, :], ((1,), (0,)))
                scores = scores + bias_ref[...]
                prob_grad = dot(sent_ref[:, value_lanes(key_head)], grad_t_ref[rows, :], ((1,), (0,)))
                peak = fold(scores, jnp.maximum, jnp.max)
                weights = jnp.exp2((scores - peak) * EXP2_SCALE)
                weight_ref[head] = weights
                product_ref[head] = prob_grad
                sums_ref[head, 0:1, :] = peak
                sums_ref[head, 1:2, :] = fold(weights, jnp.add, jnp.sum)
                sums_ref[head, 2:3, :] = fold(weights * prob_grad, jnp.add, jnp.sum)
            return carry

        lax.fori_loop(0, heads // step_heads, step, 0)


def own_scores(sent, turned_t, grad_t):
    slots = sent.shape[0]
    heads = turned_t.shape[0] // HEAD_DIM
    square = jax.ShapeDtypeStruct((heads, slots, slots), jnp.float32)
    return pl.pallas_call(
        functools.partial(own_kernel, 4),
        out_shape=(square, square, jax.ShapeDtypeStruct((heads, 8, slots), jnp.float32)),
        in_specs=[VMEM] * 3,
        out_specs=(VMEM,) * 3,
        scratch_shapes=[pltpu.VMEM((slots, slots), jnp.float32)],
        compiler_params=vmem(0, 16, 16),
        cost_estimate=pl.CostEstimate(
            flops=5 * 10**9, bytes_accessed=10 * 1024 * 1024, transcendentals=0
        ),
        name="own_scores",
    )(sent, turned_t, grad_t)


def scores_kernel(
    ctx_size,
    sizes,
    step_units,
    key_head,
    meta_ref,
    turned_ref,
    grad_ref,
    turned_t_ref,
    grad_t_ref,
    sums_ref,
    *refs,
):
    count = 4 if relayed(ctx_size) else ctx_size - 1
    inputs, before = refs[:count], refs[count : -6 - ctx_size]
    refs = refs[-6 - ctx_size :]
    terms, refs = refs[: ctx_size - 1], refs[ctx_size - 1 :]
    score_grad_ref, joined_ref, key_ref, value_ref, bias_ref, prob_ref, acc_ref = refs
    slots = turned_ref.shape[0]
    span = bias_ref.shape[0]
    heads = joined_ref.shape[0]
    starts = [pl.multiple_of(meta_ref[hop], ALIGN) for hop in range(ctx_size)]
    my_start, my_count = starts[0], meta_ref[ctx_size]
    sent_hops = list(range(1, ctx_size))
    if relayed(ctx_size):
        last = lax.axis_index("ctx") == ctx_size - 1
        sent_hops = [jnp.where(last, 3, 1), 2, jnp.where(last, 1, 2)]

    def blocks_of(lanes):
        blocks = [block[:, lanes] for block in inputs]
        if relayed(ctx_size):
            alpha, beta, gamma, delta = blocks
            blocks = [jnp.where(last, alpha, gamma), jnp.where(last, beta, alpha), delta]
        return blocks

    for ref, lanes in ((key_ref, key_lanes(key_head)), (value_ref, value_lanes(key_head))):
        ref[slots:span, :] = jnp.zeros((span - slots, HEAD_DIM), jnp.bfloat16)
        blocks = blocks_of(lanes)
        for hop in range(ctx_size - 1, 0, -1):
            ref[pl.ds(starts[hop], slots), :] = blocks[hop - 1]
    place = lax.broadcasted_iota(jnp.int32, bias_ref.shape, 0)
    seen = place < 0
    for hop in range(1, ctx_size):
        end = starts[hop] + meta_ref[ctx_size + hop]
        seen = seen | ((place >= starts[hop]) & (place < end))
    bias_ref[...] = jnp.where(seen, 0.0, HIDDEN)
    live = lax.broadcasted_iota(jnp.int32, (1, slots), 1) < my_count
    acc_ref[...] = jnp.zeros_like(acc_ref)

    def joint(ref, places, rows, width):
        return jnp.concatenate([ref[rows(place) + (slice(0, width),)] for place in places], axis=1)

    def head_rows(place):
        return (pl.ds(pl.multiple_of((key_head * heads + place) * HEAD_DIM, HEAD_DIM), HEAD_DIM),)

    def units(groups, rows, width):
        side = slots // width
        bias = jnp.concatenate([bias_ref[:rows, :]] * (slots // HEAD_DIM), axis=1)
        alive = jnp.concatenate([live[:, :width]] * side, axis=1)
        queries = [joint(turned_t_ref, group, head_rows, width) for group in groups]
        grads = [joint(grad_t_ref, group, head_rows, width) for group in groups]

        def sums(row):
            index = lambda place: (key_head * heads + place, slice(row, row + 1))
            return [joint(sums_ref, group, index, width) for group in groups]

        own_peaks, own_totals, own_products = sums(0), sums(1), sums(2)
        scores = [dot(key_ref[:rows, :], query, ((1,), (0,))) + bias for query in queries]
        prob_grads = [dot(value_ref[:rows, :], grad, ((1,), (0,))) for grad in grads]
        peaks = [
            jnp.maximum(own, fold(score, jnp.maximum, jnp.max))
            for own, score in zip(own_peaks, scores)
        ]
        weights = [jnp.exp2((score - peak) * EXP2_SCALE) for score, peak in zip(scores, peaks)]
        shares = [jnp.exp2((own - peak) * EXP2_SCALE) for own, peak in zip(own_peaks, peaks)]
        totals = [
            own * share + fold(weight, jnp.add, jnp.sum)
            for own, share, weight in zip(own_totals, shares, weights)
        ]
        products = [
            own * share + fold(weight * prob_grad, jnp.add, jnp.sum)
            for own, share, weight, prob_grad in zip(own_products, shares, weights, prob_grads)
        ]
        inverses = [1.0 / total for total in totals]
        deltas = [product * inverse for product, inverse in zip(products, inverses)]
        inverses = [jnp.where(alive, inverse, 0.0) for inverse in inverses]
        factors = [share * inverse for share, inverse in zip(shares, inverses)]
        probs = [weight * inverse for weight, inverse in zip(weights, inverses)]
        score_grads = [
            (prob * (prob_grad - delta)).astype(jnp.bfloat16)
            for prob, prob_grad, delta in zip(probs, prob_grads, deltas)
        ]
        probs = [prob.astype(jnp.bfloat16) for prob in probs]
        for group, prob, score_grad, factor, delta in zip(
            groups, probs, score_grads, factors, deltas
        ):
            for index, place in enumerate(group):
                part = slice(index * width, (index + 1) * width)
                columns = pl.ds(pl.multiple_of(place * slots, slots), width)
                prob_ref[:rows, columns] = prob[:, part]
                score_grad_ref[:rows, columns] = score_grad[:, part]
                joined_ref[place, 0:1, :width] = factor[:, part]
                joined_ref[place, 1:2, :width] = delta[:, part]
                if width < slots:
                    rest = pl.ds(pl.multiple_of(place * slots + width, HEAD_DIM), slots - width)
                    score_grad_ref[:rows, rest] = jnp.zeros((rows, slots - width), jnp.bfloat16)
                    joined_ref[place, 0:2, width:] = jnp.zeros((2, slots - width), jnp.float32)

    above = {}
    for rows, width in sizes:
        fits = (my_start > above.get(width, 0)) & (my_start <= rows)
        above[width] = rows
        if len(sizes) > 1:
            fits = fits & ((my_count > slots // 2) if width == slots else (my_count <= width))

        @pl.when(fits)
        def _():
            side = slots // width

            def step(index, carry):
                base = index * step_units * side
                units(
                    [[base + part * side + item for item in range(side)] for part in range(step_units)],
                    rows,
                    width,
                )
                return carry

            lax.fori_loop(0, heads // side // step_units, step, 0)
            if rows % CHUNK:
                beyond = slice(rows, rows + CHUNK - rows % CHUNK)
                none = jnp.zeros((CHUNK - rows % CHUNK, heads * slots), jnp.bfloat16)
                score_grad_ref[beyond, :] = none
            lane = key_head * heads * HEAD_DIM
            acc_ref[:rows, :] = terms_of(
                beside(prob_ref, rows, heads, slots, width),
                beside(score_grad_ref, rows, heads, slots, width),
                stacked(turned_ref, lane, heads, width),
                stacked(grad_ref, lane, heads, width),
            )

    @pl.when(my_start == 0)
    def _():
        for place in range(heads):
            inverse = 1.0 / sums_ref[key_head * heads + place, 1:2, :]
            joined_ref[place, 0:1, :] = jnp.where(live, inverse, 0.0)
            joined_ref[place, 1:2, :] = sums_ref[key_head * heads + place, 2:3, :] * inverse

    for hop, term_ref in zip(sent_hops, terms):
        start = pl.multiple_of(meta_ref[hop], ALIGN)
        term = acc_ref[pl.ds(start, slots), :].astype(term_ref.dtype)
        if term_ref.shape == term.shape:
            term_ref[...] = term
        else:
            term_ref[:, : -2 * HEAD_DIM] = before[0][...]
            term_ref[:, -2 * HEAD_DIM :] = term


def relayed(ctx_size):
    return ctx_size == 4


def scores(key_head, meta, turned, out_grad, turned_t, grad_t, sums, blocks, after, routed, ctx_size):
    slots, width = blocks[0].shape
    heads = turned.shape[1] // (width // 2)
    span = -(-(routed + ctx_size * ALIGN) // CHUNK) * CHUNK
    sizes, step_units = [(span, slots)], 1
    if span == 2 * CHUNK and routed - slots // 2 + ctx_size * ALIGN <= 3 * CHUNK // 2 + ALIGN:
        sizes = [(CHUNK, slots), (3 * CHUNK // 2, slots), (CHUNK, slots // 2), (span, slots // 2)]
        step_units = 4
    terms = [jax.ShapeDtypeStruct((slots, 2 * HEAD_DIM), jnp.bfloat16)] * (ctx_size - 1)
    if relayed(ctx_size):
        terms[1] = jax.ShapeDtypeStruct((slots, 2 * (key_head + 1) * HEAD_DIM), jnp.bfloat16)
        terms[2] = jax.ShapeDtypeStruct((slots, 2 * HEAD_DIM), jnp.float32)
    outs = pl.pallas_call(
        functools.partial(scores_kernel, ctx_size, sizes, step_units, key_head),
        out_shape=(
            *terms,
            jax.ShapeDtypeStruct((span, heads * slots), jnp.bfloat16),
            jax.ShapeDtypeStruct((heads, 8, slots), jnp.float32),
            jax.ShapeDtypeStruct((span + slots, HEAD_DIM), jnp.bfloat16),
        ),
        in_specs=[SMEM] + [VMEM] * (5 + len(blocks) + len(after)),
        out_specs=(VMEM,) * (ctx_size + 2),
        scratch_shapes=[
            pltpu.VMEM((span + slots, HEAD_DIM), jnp.bfloat16),
            pltpu.VMEM((span, HEAD_DIM), jnp.float32),
            pltpu.VMEM((span, heads * slots), jnp.bfloat16),
            pltpu.VMEM((span + slots, 2 * HEAD_DIM), jnp.float32),
        ],
        compiler_params=vmem(routed, 20, 60),
        cost_estimate=pl.CostEstimate(
            flops=4 * 10**9, bytes_accessed=6 * 1024 * 1024, transcendentals=0
        ),
        name="scores",
    )(meta, turned, out_grad, turned_t, grad_t, sums, *blocks, *after)
    return outs[: ctx_size - 1], outs[ctx_size - 1 :]


def local_kernel(
    key_head,
    meta_ref,
    cos_ref,
    sin_ref,
    turned_ref,
    grad_ref,
    sent_ref,
    weight_ref,
    product_ref,
    score_grad_ref,
    joined_ref,
    key_ref,
    *refs,
):
    dq_ref, own_ref, prob_ref, own_grad_ref, sum_ref = refs[-5:]
    slots = turned_ref.shape[0]
    heads = joined_ref.shape[0]
    span = score_grad_ref.shape[0]
    my_start = meta_ref[0]
    own_key_t = sent_ref[:, key_lanes(key_head)].astype(jnp.float32).T.astype(jnp.bfloat16)
    for head in range(heads):
        columns = slice(head * slots, (head + 1) * slots)
        prob = weight_ref[key_head * heads + head] * joined_ref[head, 0:1, :]
        prob_ref[:, columns] = prob.astype(jnp.bfloat16)
        product = product_ref[key_head * heads + head] - joined_ref[head, 1:2, :]
        score_grad = (prob * product).astype(jnp.bfloat16)
        own_grad_ref[:, columns] = score_grad
        sum_ref[head] = dot(own_key_t, score_grad, ((1,), (0,)))
    for chunk in range(0, span, CHUNK):

        @pl.when(chunk < my_start)
        def _():
            rows = slice(chunk, chunk + CHUNK)
            key_t = key_ref[rows, :].astype(jnp.float32).T.astype(jnp.bfloat16)
            for head in range(heads):
                score_grad = score_grad_ref[rows, head * slots : (head + 1) * slots]
                sum_ref[head] += dot(key_t, score_grad, ((1,), (0,)))

    lane = key_head * heads * HEAD_DIM
    for head in range(heads):
        grad = turn_back((sum_ref[head] * SCORE_SCALE).T, cos_ref[...], sin_ref[...])
        dq_ref[:, head * HEAD_DIM : (head + 1) * HEAD_DIM] = grad.astype(jnp.bfloat16)
    own_ref[...] = terms_of(
        prob_ref[...],
        own_grad_ref[...],
        stacked(turned_ref, lane, heads, slots),
        stacked(grad_ref, lane, heads, slots),
    )


def local_terms(key_head, meta, cos_full, sin_full, turned, out_grad, sent, own, joined, dq, after):
    slots = turned.shape[0]
    heads = joined[1].shape[0]
    weight, product, _ = own
    operands = [meta, cos_full, sin_full, turned, out_grad, sent, weight, product, *joined, *after]
    in_specs = [SMEM] + [VMEM] * (len(operands) - 1)
    aliases = {}
    if dq is not None:
        aliases = {len(operands): 0}
        operands.append(dq)
        in_specs.append(pl.BlockSpec(memory_space=pl.ANY))
    return pl.pallas_call(
        functools.partial(local_kernel, key_head),
        grid=(1,),
        out_shape=(
            jax.ShapeDtypeStruct(turned.shape, jnp.bfloat16),
            jax.ShapeDtypeStruct((slots, 2 * HEAD_DIM), jnp.float32),
        ),
        in_specs=in_specs,
        out_specs=(pl.BlockSpec((slots, heads * HEAD_DIM), lambda step: (0, key_head)), VMEM),
        scratch_shapes=[
            pltpu.VMEM((slots, heads * slots), jnp.bfloat16),
            pltpu.VMEM((slots, heads * slots), jnp.bfloat16),
            pltpu.VMEM((heads, HEAD_DIM, slots), jnp.float32),
        ],
        input_output_aliases=aliases,
        compiler_params=vmem(joined[0].shape[0] // 2, 16, 48),
        cost_estimate=pl.CostEstimate(
            flops=4 * 10**9, bytes_accessed=10 * 1024 * 1024, transcendentals=0
        ),
        name="local_terms",
    )(*operands)


def add_kernel(own_ref, arrived_ref, *refs):
    refs[-1][...] = (own_ref[...] + arrived_ref[...].astype(jnp.float32)).astype(jnp.bfloat16)


def add_terms(own, arrived, after):
    return pl.pallas_call(
        add_kernel,
        out_shape=jax.ShapeDtypeStruct(arrived.shape, jnp.bfloat16),
        in_specs=[VMEM] * (2 + len(after)),
        out_specs=VMEM,
        compiler_params=vmem(0, 16, 16),
        cost_estimate=pl.CostEstimate(flops=10**6, bytes_accessed=10**6, transcendentals=0),
        name="add_terms",
    )(own, arrived, *after)


def finish_kernel(ctx_size, key_heads, meta_ref, cos_ref, sin_ref, *refs):
    key_grad_ref, value_grad_ref = refs[-2:]
    owns, terms = refs[:key_heads], list(refs[key_heads:-2])
    slots = cos_ref.shape[0]
    live = lax.broadcasted_iota(jnp.int32, (slots, HEAD_DIM), 0) < meta_ref[ctx_size]
    totals = [own[...] for own in owns]
    for index in range(ctx_size - 1):
        parts = [terms.pop(0)]
        if parts[0].shape[1] == 2 * HEAD_DIM:
            parts += [terms.pop(0) for _ in range(key_heads - 1)]
        term = jnp.concatenate([part[...] for part in parts], axis=1).astype(jnp.float32)
        if index == 0 and relayed(ctx_size):
            term = jnp.where(lax.axis_index("ctx") == 2, 0.0, term)
        for head in range(key_heads):
            totals[head] += term[:, 2 * head * HEAD_DIM : 2 * (head + 1) * HEAD_DIM]
    for head, total in enumerate(totals):
        lanes = head_lanes(head)
        key_term = turn_back(total[:, :HEAD_DIM], cos_ref[...], sin_ref[...])
        key_grad_ref[:, lanes] = jnp.where(live, key_term, 0.0).astype(jnp.bfloat16)
        value_grad_ref[:, lanes] = jnp.where(live, total[:, HEAD_DIM:], 0.0).astype(jnp.bfloat16)


def finish(meta, cos_full, sin_full, owns, terms, ctx_size):
    slots = cos_full.shape[0]
    key_heads = len(owns)
    grad = jax.ShapeDtypeStruct((slots, key_heads * HEAD_DIM), jnp.bfloat16)
    return pl.pallas_call(
        functools.partial(finish_kernel, ctx_size, key_heads),
        out_shape=(grad, grad),
        in_specs=[SMEM] + [VMEM] * (2 + len(owns) + len(terms)),
        out_specs=(VMEM, VMEM),
        compiler_params=vmem(0, 16, 16),
        name="finish",
    )(meta, cos_full, sin_full, *owns, *terms)


def spread(sent, sent_again, ctx_size):
    if relayed(ctx_size):
        alpha = lax.ppermute(sent, "ctx", [(0, 2), (2, 3)])
        beta = lax.ppermute(sent, "ctx", [(1, 3)])
        gamma = lax.ppermute(sent_again, "ctx", [(0, 1), (1, 2)])
        return [alpha, beta, gamma, lax.ppermute(alpha, "ctx", [(2, 3)])]
    blocks = [sent]
    for hop in range(1, ctx_size):
        pairs = [(shard, shard + 1) for shard in range(hop - 1, ctx_size - 1)]
        blocks.append(lax.ppermute(blocks[-1], "ctx", pairs))
    return blocks[1:]


def relay(terms):
    firsts, thirds, after = [], [], []
    for first, _, third in terms:
        firsts.append(lax.ppermute(first, "ctx", [(3, 2), (2, 1), (1, 0)]))
        third = add_terms(third, firsts[-1], after)
        thirds.append(lax.ppermute(third, "ctx", [(3, 2), (2, 0)]))
        after = [third]
    return firsts + thirds + [lax.ppermute(terms[-1][1], "ctx", [(3, 1)])]


def descend(terms, ctx_size):
    arrived = []
    for hop, term in enumerate(terms, 1):
        pairs = [(shard + hop, shard) for shard in range(ctx_size - hop)]
        arrived.append(lax.ppermute(term, "ctx", pairs))
    return arrived


def body(positions, queries, keys, values, out_grad):
    ctx_size = lax.axis_size("ctx")
    routed = positions.shape[1]
    key_heads = keys.shape[2] // HEAD_DIM
    meta, cos_full, sin_full, sent = prepare(positions, keys[0], values[0], ctx_size)
    turned, turned_t, grad_t, sent_again = rotate_queries(
        cos_full, sin_full, queries[0], out_grad[0], sent
    )
    blocks = spread(sent, sent_again, ctx_size)
    own = own_scores(sent, turned_t, grad_t)
    terms, joined, owns = [], [], []
    for head in range(key_heads):
        after = [terms[-1][1]] if terms else []
        outs = scores(
            head,
            meta,
            turned,
            out_grad[0],
            turned_t,
            grad_t,
            own[2],
            blocks,
            after,
            routed,
            ctx_size,
        )
        terms.append(outs[0])
        joined.append(outs[1])
    if relayed(ctx_size):
        arrived = relay(terms)
    else:
        arrived = [part for hop in zip(*[descend(term, ctx_size) for term in terms]) for part in hop]
    dq = None
    for head in range(key_heads):
        after = [arrived[0]] if relayed(ctx_size) and head > 0 else []
        dq, own_terms = local_terms(
            head, meta, cos_full, sin_full, turned, out_grad[0], sent, own, joined[head], dq, after
        )
        owns.append(own_terms)
    key_grad, value_grad = finish(meta, cos_full, sin_full, owns, arrived, ctx_size)
    return (dq[None], key_grad[None], value_grad[None])


def solution(mesh):
    split = P(("groups", "dp"), "ctx", "mp")
    return jax.shard_map(
        body,
        mesh=mesh,
        in_specs=(P(("groups", "dp"), None), split, split, split, split),
        out_specs=(split, split, split),
        check_vma=False,
    )
```

profile of v0, /device:TPU:0, one launch (start us, length us, event | category | flops | bytes accessed | tf_op | source)
XLA Modules:
  0.0 58.7 jit_solution(10034057855783440489)
XLA Ops:
  0.6 2.3 %prepare.1 = (s32[8]{0:T(128)}, f32[256,128]{1,0:T(8,128)}, f32[256,128]{1,0:T(8,128)}, bf16[256,512]{1,0:T(8,128)(2,1)}) custom-call(s32[1,512]{1,0:T(1,128)} %pos_hbm.1, bf16[256,256]{1,0:T(8,128)(2,1)} %bitcast.14, bf16[256,256]{1,0:T(8,128)(2,1)} %bitcast.15), custom_call_target="tpu_custom_call" | custom-call | tf_op jit(solution)/shard_map/prepare/pallas_call | solution.py:116
  2.9 6.0 %collective-permute-start = (bf16[256,512]{1,0:T(8,128)(2,1)}, bf16[256,512]{1,0:T(8,128)(2,1)S(1)}, u32[]{:S(2)}, u32[]{:S(2)}) collective-permute-start(bf16[256,512]{1,0:T(8,128)(2,1)} %get-tuple-element.35.sent_ref), channel_id=1, source_target_pairs={{0,8},{8,12},{1,9},{9,13},{2,10},{10,14},{3,11},{11,15},{16,24},{2... | collective-permute-start | bytes 786440 | tf_op jit(solution)/shard_map/ppermute | solution.py:590
  8.9 0.7 %collective-permute-start.1 = (bf16[256,512]{1,0:T(8,128)(2,1)}, bf16[256,512]{1,0:T(8,128)(2,1)S(1)}, u32[]{:S(2)}, u32[]{:S(2)}) collective-permute-start(bf16[256,512]{1,0:T(8,128)(2,1)} %get-tuple-element.35.sent_ref), channel_id=1, source_target_pairs={{4,12},{5,13},{6,14},{7,15},{20,28},{21,29},{22,30},{23,31}} | collective-permute-start | bytes 786440 | tf_op jit(solution)/shard_map/ppermute | solution.py:591
  9.5 0.0 copy-start
  9.6 1.2 %copy-done = bf16[1,256,2048]{2,1,0:T(8,128)(2,1)S(1)} copy-done((bf16[1,256,2048]{2,1,0:T(8,128)(2,1)S(1)}, bf16[1,256,2048]{2,1,0:T(8,128)(2,1)}, u32[]{:S(2)}) %copy-start) | copy-done | bytes 1048600
  10.8 0.9 %copy-done.2 = f32[256,128]{1,0:T(8,128)S(1)} copy-done((f32[256,128]{1,0:T(8,128)S(1)}, f32[256,128]{1,0:T(8,128)}, u32[]{:S(2)}) %copy-start.2) | copy-done | bytes 131096
  11.7 0.9 %copy-done.4 = f32[256,128]{1,0:T(8,128)S(1)} copy-done((f32[256,128]{1,0:T(8,128)S(1)}, f32[256,128]{1,0:T(8,128)}, u32[]{:S(2)}) %copy-start.4) | copy-done | bytes 131096
  12.6 0.9 %copy-done.6 = bf16[256,512]{1,0:T(8,128)(2,1)S(1)} copy-done((bf16[256,512]{1,0:T(8,128)(2,1)S(1)}, bf16[256,512]{1,0:T(8,128)(2,1)}, u32[]{:S(2)}) %copy-start.6) | copy-done | bytes 262168
  13.5 1.2 %copy-done.9 = bf16[1,256,2048]{2,1,0:T(8,128)(2,1)S(1)} copy-done((bf16[1,256,2048]{2,1,0:T(8,128)(2,1)S(1)}, bf16[1,256,2048]{2,1,0:T(8,128)(2,1)}, u32[]{:S(2)}) %copy-start.9) | copy-done | bytes 1048600
  14.8 1.1 %rotate_queries.1 = (bf16[256,2048]{1,0:T(8,128)(2,1)S(1)}, bf16[2048,256]{1,0:T(8,128)(2,1)S(1)}, bf16[2048,256]{1,0:T(8,128)(2,1)S(1)}, bf16[256,512]{1,0:T(8,128)(2,1)S(1)}) custom-call(f32[256,128]{1,0:T(8,128)S(1)} %copy-done.2, f32[256,128]{1,0:T(8,128)S(1)} %copy-done.4, bf16[256,2048]{1,0:T(8,128)(2,1)S(1)} %bitcast.12, ...), custom_call_target="tpu_custom_call" | custom-call | flops 3000000000 | bytes 4194304 | tf_op jit(solution)/shard_map/rotate_queries/pallas_call | solution.py:157
  15.9 4.1 %collective-permute-start.2 = (bf16[256,512]{1,0:T(8,128)(2,1)S(1)}, bf16[256,512]{1,0:T(8,128)(2,1)S(1)}, u32[]{:S(2)}, u32[]{:S(2)}) collective-permute-start(bf16[256,512]{1,0:T(8,128)(2,1)S(1)} %get-tuple-element.42), channel_id=1, source_target_pairs={{0,4},{4,8},{1,5},{5,9},{2,6},{6,10},{3,7},{7,11},{16,20},{20,24},... | collective-permute-start | bytes 786440 | tf_op jit(solution)/shard_map/ppermute | solution.py:592
  20.0 0.7 %collective-permute-start.3 = (bf16[256,512]{1,0:T(8,128)(2,1)S(1)}, bf16[256,512]{1,0:T(8,128)(2,1)S(1)}, u32[]{:S(2)}, u32[]{:S(2)}) collective-permute-start(bf16[256,512]{1,0:T(8,128)(2,1)S(1)} %collective-permute-done.refs_0_), channel_id=1, source_target_pairs={{8,12},{9,13},{10,14},{11,15},{24,28},{25,29},{26,30},{27,31}} | collective-permute-start | bytes 786440 | tf_op jit(solution)/shard_map/ppermute | solution.py:593
  20.7 0.0 copy-start.1
  20.7 2.2 %own_scores.1 = (f32[16,256,256]{2,1,0:T(8,128)S(1)}, f32[16,256,256]{2,1,0:T(8,128)S(1)}, f32[16,8,256]{2,1,0:T(8,128)S(1)}) custom-call(bf16[256,512]{1,0:T(8,128)(2,1)S(1)} %copy-done.7, bf16[2048,256]{1,0:T(8,128)(2,1)S(1)} %get-tuple-element.37.turned_t_ref, bf16[2048,256]{1,0:T(8,128)(2,1)S(1)} %get-tuple-element.38.grad_t_ref), custom_call_target="tpu_custom_call" | custom-call | flops 5000000000 | bytes 10485760 | tf_op jit(solution)/shard_map/own_scores/pallas_call | solution.py:238
  22.9 2.3 %collective-permute-done.2.refs_2_ = bf16[256,512]{1,0:T(8,128)(2,1)S(1)} collective-permute-done((bf16[256,512]{1,0:T(8,128)(2,1)S(1)}, bf16[256,512]{1,0:T(8,128)(2,1)S(1)}, u32[]{:S(2)}, u32[]{:S(2)}) %collective-permute-start.2) | collective-permute-done | bytes 262176 | tf_op jit(solution)/shard_map/ppermute | solution.py:592
  25.3 0.0 collective-permute-done.1.refs_1_
  25.3 0.0 collective-permute-done.3.refs_3_
  25.3 1.0 %scores.2 = (bf16[256,256]{1,0:T(8,128)(2,1)S(1)}, bf16[256,256]{1,0:T(8,128)(2,1)S(1)}, f32[256,256]{1,0:T(8,128)S(1)}, bf16[576,2048]{1,0:T(8,128)(2,1)S(1)}, ...) custom-call(s32[8]{0:T(128)S(1)} %copy-done.8, bf16[256,2048]{1,0:T(8,128)(2,1)S(1)} %get-tuple-element.36.turned_ref, ...), custom_call_target="tpu_custom_call" | custom-call | flops 4000000000 | bytes 6291456 | tf_op jit(solution)/shard_map/scores/pallas_call | solution.py:426
  26.3 1.3 %collective-permute-start.4 = (bf16[256,256]{1,0:T(8,128)(2,1)S(1)}, bf16[256,256]{1,0:T(8,128)(2,1)S(1)}, u32[]{:S(2)}, u32[]{:S(2)}) collective-permute-start(bf16[256,256]{1,0:T(8,128)(2,1)S(1)} %get-tuple-element.47), channel_id=1, source_target_pairs={{12,8},{8,4},{4,0},{13,9},{9,5},{5,1},{14,10},{10,6},{6,2},{15,11}... | collective-permute-start | bytes 393224 | tf_op jit(solution)/shard_map/ppermute | solution.py:604
  27.6 0.0 copy-start.3
  27.6 0.0 copy-start.5
  27.6 1.2 %scores.3 = (bf16[256,256]{1,0:T(8,128)(2,1)S(1)}, bf16[256,512]{1,0:T(8,128)(2,1)S(1)}, f32[256,256]{1,0:T(8,128)S(1)}, bf16[576,2048]{1,0:T(8,128)(2,1)S(1)}, ...) custom-call(s32[8]{0:T(128)S(1)} %copy-done.8, bf16[256,2048]{1,0:T(8,128)(2,1)S(1)} %get-tuple-element.36.turned_ref, ...), custom_call_target="tpu_custom_call" | custom-call | flops 4000000000 | bytes 6291456 | tf_op jit(solution)/shard_map/scores/pallas_call | solution.py:426
  28.8 1.3 %collective-permute-start.5 = (bf16[256,256]{1,0:T(8,128)(2,1)S(1)}, bf16[256,256]{1,0:T(8,128)(2,1)S(1)}, u32[]{:S(2)}, u32[]{:S(2)}) collective-permute-start(bf16[256,256]{1,0:T(8,128)(2,1)S(1)} %get-tuple-element.55), channel_id=1, source_target_pairs={{12,8},{8,4},{4,0},{13,9},{9,5},{5,1},{14,10},{10,6},{6,2},{15,11}... | collective-permute-start | bytes 393224 | tf_op jit(solution)/shard_map/ppermute | solution.py:604
  30.1 0.7 %collective-permute-start.8 = (bf16[256,512]{1,0:T(8,128)(2,1)S(1)}, bf16[256,512]{1,0:T(8,128)(2,1)S(1)}, u32[]{:S(2)}, u32[]{:S(2)}) collective-permute-start(bf16[256,512]{1,0:T(8,128)(2,1)S(1)} %get-tuple-element.58), channel_id=1, source_target_pairs={{12,4},{13,5},{14,6},{15,7},{28,20},{29,21},{30,22},{31,23}} | collective-permute-start | bytes 786440 | tf_op jit(solution)/shard_map/ppermute | solution.py:608
  30.8 2.7 %local_terms.2 = (bf16[256,2048]{1,0:T(8,128)(2,1)}, f32[256,256]{1,0:T(8,128)S(1)}) custom-call(s32[8]{0:T(128)S(1)} %copy-done.8, f32[256,128]{1,0:T(8,128)S(1)} %copy-done.3, f32[256,128]{1,0:T(8,128)S(1)} %copy-done.5, bf16[256,2048]{1,0:T(8,128)(2,1)S(1)} %get-tuple-element.36.turned_ref, bf16[256,2048]{1,0:T(8,128)(2,1)S(1)} %bitcast.10, ...), custom_call_target="tpu_custom_call" | custom-call | flops 4000000000 | bytes 10485760 | tf_op jit(solution)/shard_map/local_terms/pallas_call | solution.py:513
  33.5 0.4 collective-permute-done.4.refs_0_.arrived_ref.refs_2_
  33.9 1.3 %collective-permute-start.6 = (bf16[256,256]{1,0:T(8,128)(2,1)S(1)}, bf16[256,256]{1,0:T(8,128)(2,1)S(1)}, u32[]{:S(2)}, u32[]{:S(2)}) collective-permute-start(bf16[256,256]{1,0:T(8,128)(2,1)S(1)} %add_terms.2.refs_0_), channel_id=1, source_target_pairs={{12,8},{8,0},{13,9},{9,1},{14,10},{10,2},{15,11},{11,3},{28,24},{2... | collective-permute-start | bytes 393224 | tf_op jit(solution)/shard_map/ppermute | solution.py:606
  35.2 1.8 %collective-permute-done.5.arrived_ref.refs_3_ = bf16[256,256]{1,0:T(8,128)(2,1)S(1)} collective-permute-done((bf16[256,256]{1,0:T(8,128)(2,1)S(1)}, bf16[256,256]{1,0:T(8,128)(2,1)S(1)}, u32[]{:S(2)}, u32[]{:S(2)}) %collective-permute-start.5) | collective-permute-done | bytes 131104 | tf_op jit(solution)/shard_map/ppermute | solution.py:604
  37.1 1.3 %collective-permute-start.7 = (bf16[256,256]{1,0:T(8,128)(2,1)S(1)}, bf16[256,256]{1,0:T(8,128)(2,1)S(1)}, u32[]{:S(2)}, u32[]{:S(2)}) collective-permute-start(bf16[256,256]{1,0:T(8,128)(2,1)S(1)} %add_terms.3), channel_id=1, source_target_pairs={{12,8},{8,0},{13,9},{9,1},{14,10},{10,2},{15,11},{11,3},{28,24},{2... | collective-permute-start | bytes 393224 | tf_op jit(solution)/shard_map/ppermute | solution.py:606
  38.4 2.7 %local_terms.3 = (bf16[256,2048]{1,0:T(8,128)(2,1)}, f32[256,256]{1,0:T(8,128)S(1)}) custom-call(s32[8]{0:T(128)S(1)} %copy-done.8, f32[256,128]{1,0:T(8,128)S(1)} %copy-done.3, f32[256,128]{1,0:T(8,128)S(1)} %copy-done.5, bf16[256,2048]{1,0:T(8,128)(2,1)S(1)} %get-tuple-element.36.turned_ref, ...), custom_call_target="tpu_custom_call", output_to_operand_aliasing={{0}: (12, {})} | custom-call | flops 4000000000 | bytes 10485760 | tf_op jit(solution)/shard_map/local_terms/pallas_call | solution.py:513
  41.1 16.2 %collective-permute-done.7.refs_5_ = bf16[256,256]{1,0:T(8,128)(2,1)S(1)} collective-permute-done((bf16[256,256]{1,0:T(8,128)(2,1)S(1)}, bf16[256,256]{1,0:T(8,128)(2,1)S(1)}, u32[]{:S(2)}, u32[]{:S(2)}) %collective-permute-start.7) | collective-permute-done | bytes 131104 | tf_op jit(solution)/shard_map/ppermute | solution.py:606
  57.3 1.4 %finish.1 = (bf16[256,256]{1,0:T(8,128)(2,1)}, bf16[256,256]{1,0:T(8,128)(2,1)}) custom-call(s32[8]{0:T(128)S(1)} %copy-done.8, f32[256,128]{1,0:T(8,128)S(1)} %copy-done.3, f32[256,128]{1,0:T(8,128)S(1)} %copy-done.5, f32[256,256]{1,0:T(8,128)S(1)} %get-tuple-element.53.refs_0_, f32[256,256]{1,0:T(8,128)S(1)} %get-tuple-element.54.refs_1_, ...), custom_call_target="tpu_custom_call" | custom-call | tf_op jit(solution)/shard_map/finish/pallas_call | solution.py:578
  (16 shorter events, 0.1 us)
Async XLA Ops:
  2.9 17.1 %collective-permute-start = (bf16[256,512]{1,0:T(8,128)(2,1)}, bf16[256,512]{1,0:T(8,128)(2,1)S(1)}, u32[]{:S(2)}, u32[]{:S(2)}) collective-permute-start(bf16[256,512]{1,0:T(8,128)(2,1)} %get-tuple-element.35.sent_ref), channel_id=1, source_target_pairs={{0,8},{8,12},{1,9},{9,13},{2,10},{10,14},{3,11},{11,15},{16,24},{2... | collective-permute-start | bytes 786440 | tf_op jit(solution)/shard_map/ppermute | solution.py:590
  8.9 16.4 %collective-permute-start.1 = (bf16[256,512]{1,0:T(8,128)(2,1)}, bf16[256,512]{1,0:T(8,128)(2,1)S(1)}, u32[]{:S(2)}, u32[]{:S(2)}) collective-permute-start(bf16[256,512]{1,0:T(8,128)(2,1)} %get-tuple-element.35.sent_ref), channel_id=1, source_target_pairs={{4,12},{5,13},{6,14},{7,15},{20,28},{21,29},{22,30},{23,31}} | collective-permute-start | bytes 786440 | tf_op jit(solution)/shard_map/ppermute | solution.py:591
  9.5 1.2 %copy-start = (bf16[1,256,2048]{2,1,0:T(8,128)(2,1)S(1)}, bf16[1,256,2048]{2,1,0:T(8,128)(2,1)}, u32[]{:S(2)}) copy-start(bf16[1,256,2048]{2,1,0:T(8,128)(2,1)} %param.9) | copy-start | bytes 3145732
  10.8 0.9 %copy-start.2 = (f32[256,128]{1,0:T(8,128)S(1)}, f32[256,128]{1,0:T(8,128)}, u32[]{:S(2)}) copy-start(f32[256,128]{1,0:T(8,128)} %get-tuple-element.33.cos_ref) | copy-start | bytes 393220
  11.7 0.9 %copy-start.4 = (f32[256,128]{1,0:T(8,128)S(1)}, f32[256,128]{1,0:T(8,128)}, u32[]{:S(2)}) copy-start(f32[256,128]{1,0:T(8,128)} %get-tuple-element.34.sin_ref) | copy-start | bytes 393220
  12.6 0.9 %copy-start.6 = (bf16[256,512]{1,0:T(8,128)(2,1)S(1)}, bf16[256,512]{1,0:T(8,128)(2,1)}, u32[]{:S(2)}) copy-start(bf16[256,512]{1,0:T(8,128)(2,1)} %get-tuple-element.35.sent_ref) | copy-start | bytes 786436
  13.5 1.2 %copy-start.9 = (bf16[1,256,2048]{2,1,0:T(8,128)(2,1)S(1)}, bf16[1,256,2048]{2,1,0:T(8,128)(2,1)}, u32[]{:S(2)}) copy-start(bf16[1,256,2048]{2,1,0:T(8,128)(2,1)} %param.6) | copy-start | bytes 3145732
  14.8 6.0 %copy-start.7 = (bf16[256,512]{1,0:T(8,128)(2,1)S(1)}, bf16[256,512]{1,0:T(8,128)(2,1)}, u32[]{:S(2)}) copy-start(bf16[256,512]{1,0:T(8,128)(2,1)} %get-tuple-element.35.sent_ref) | copy-start | bytes 786436
  15.9 9.4 %collective-permute-start.2 = (bf16[256,512]{1,0:T(8,128)(2,1)S(1)}, bf16[256,512]{1,0:T(8,128)(2,1)S(1)}, u32[]{:S(2)}, u32[]{:S(2)}) collective-permute-start(bf16[256,512]{1,0:T(8,128)(2,1)S(1)} %get-tuple-element.42), channel_id=1, source_target_pairs={{0,4},{4,8},{1,5},{5,9},{2,6},{6,10},{3,7},{7,11},{16,20},{20,24},... | collective-permute-start | bytes 786440 | tf_op jit(solution)/shard_map/ppermute | solution.py:592
  20.0 5.2 %collective-permute-start.3 = (bf16[256,512]{1,0:T(8,128)(2,1)S(1)}, bf16[256,512]{1,0:T(8,128)(2,1)S(1)}, u32[]{:S(2)}, u32[]{:S(2)}) collective-permute-start(bf16[256,512]{1,0:T(8,128)(2,1)S(1)} %collective-permute-done.refs_0_), channel_id=1, source_target_pairs={{8,12},{9,13},{10,14},{11,15},{24,28},{25,29},{26,30},{27,31}} | collective-permute-start | bytes 786440 | tf_op jit(solution)/shard_map/ppermute | solution.py:593
  20.7 4.6 %copy-start.1 = (bf16[1,256,2048]{2,1,0:T(8,128)(2,1)S(1)}, bf16[1,256,2048]{2,1,0:T(8,128)(2,1)}, u32[]{:S(2)}) copy-start(bf16[1,256,2048]{2,1,0:T(8,128)(2,1)} %param.9) | copy-start | bytes 3145732
  20.7 4.5 %copy-start.8 = (s32[8]{0:T(128)S(1)}, s32[8]{0:T(128)}, u32[]{:S(2)}) copy-start(s32[8]{0:T(128)} %get-tuple-element.32.meta_ref) | copy-start | bytes 100
  26.3 7.6 %collective-permute-start.4 = (bf16[256,256]{1,0:T(8,128)(2,1)S(1)}, bf16[256,256]{1,0:T(8,128)(2,1)S(1)}, u32[]{:S(2)}, u32[]{:S(2)}) collective-permute-start(bf16[256,256]{1,0:T(8,128)(2,1)S(1)} %get-tuple-element.47), channel_id=1, source_target_pairs={{12,8},{8,4},{4,0},{13,9},{9,5},{5,1},{14,10},{10,6},{6,2},{15,11}... | collective-permute-start | bytes 393224 | tf_op jit(solution)/shard_map/ppermute | solution.py:604
  27.6 3.2 %copy-start.3 = (f32[256,128]{1,0:T(8,128)S(1)}, f32[256,128]{1,0:T(8,128)}, u32[]{:S(2)}) copy-start(f32[256,128]{1,0:T(8,128)} %get-tuple-element.33.cos_ref) | copy-start | bytes 393220
  27.6 3.2 %copy-start.5 = (f32[256,128]{1,0:T(8,128)S(1)}, f32[256,128]{1,0:T(8,128)}, u32[]{:S(2)}) copy-start(f32[256,128]{1,0:T(8,128)} %get-tuple-element.34.sin_ref) | copy-start | bytes 393220
  28.8 8.3 %collective-permute-start.5 = (bf16[256,256]{1,0:T(8,128)(2,1)S(1)}, bf16[256,256]{1,0:T(8,128)(2,1)S(1)}, u32[]{:S(2)}, u32[]{:S(2)}) collective-permute-start(bf16[256,256]{1,0:T(8,128)(2,1)S(1)} %get-tuple-element.55), channel_id=1, source_target_pairs={{12,8},{8,4},{4,0},{13,9},{9,5},{5,1},{14,10},{10,6},{6,2},{15,11}... | collective-permute-start | bytes 393224 | tf_op jit(solution)/shard_map/ppermute | solution.py:604
  30.1 11.0 %collective-permute-start.8 = (bf16[256,512]{1,0:T(8,128)(2,1)S(1)}, bf16[256,512]{1,0:T(8,128)(2,1)S(1)}, u32[]{:S(2)}, u32[]{:S(2)}) collective-permute-start(bf16[256,512]{1,0:T(8,128)(2,1)S(1)} %get-tuple-element.58), channel_id=1, source_target_pairs={{12,4},{13,5},{14,6},{15,7},{28,20},{29,21},{30,22},{31,23}} | collective-permute-start | bytes 786440 | tf_op jit(solution)/shard_map/ppermute | solution.py:608
  33.9 23.4 %collective-permute-start.6 = (bf16[256,256]{1,0:T(8,128)(2,1)S(1)}, bf16[256,256]{1,0:T(8,128)(2,1)S(1)}, u32[]{:S(2)}, u32[]{:S(2)}) collective-permute-start(bf16[256,256]{1,0:T(8,128)(2,1)S(1)} %add_terms.2.refs_0_), channel_id=1, source_target_pairs={{12,8},{8,0},{13,9},{9,1},{14,10},{10,2},{15,11},{11,3},{28,24},{2... | collective-permute-start | bytes 393224 | tf_op jit(solution)/shard_map/ppermute | solution.py:606
  37.1 20.2 %collective-permute-start.7 = (bf16[256,256]{1,0:T(8,128)(2,1)S(1)}, bf16[256,256]{1,0:T(8,128)(2,1)S(1)}, u32[]{:S(2)}, u32[]{:S(2)}) collective-permute-start(bf16[256,256]{1,0:T(8,128)(2,1)S(1)} %add_terms.3), channel_id=1, source_target_pairs={{12,8},{8,0},{13,9},{9,1},{14,10},{10,2},{15,11},{11,3},{28,24},{2... | collective-permute-start | bytes 393224 | tf_op jit(solution)/shard_map/ppermute | solution.py:606
where the time goes:
time: 58.9 us; the launch traced here: 58.7 us
  waiting for transfers between devices  20.8 us (35%)
  starting transfers between devices  17.3 us (29%)
  Pallas kernels  14.6 us (25%)
  local copies, waits for them, and re-layouts  5.23 us (9%)
  between operations  0.84 us (1%)
    ppermute x2, waiting for transfers between devices, relay(): thirds.append(lax.ppermute(third, 'ctx', [(3, 2), (2, 0)]))  16.2 us
    ppermute x1, starting transfers between devices, spread(): alpha = lax.ppermute(sent, 'ctx', [(0, 2), (2, 3)])  5.96 us
    pallas_call x2, Pallas kernels, local_terms(): pl.pallas_call(functools.partial(local_kernel, key_head), grid=(1,), out_...  5.46 us
    unnamed x20, local copies, waits for them, and re-layouts  5.23 us
    ppermute x1, starting transfers between devices, spread(): gamma = lax.ppermute(sent_again, 'ctx', [(0, 1), (1, 2)])  4.11 us
    ppermute x2, starting transfers between devices, relay(): firsts.append(lax.ppermute(first, 'ctx', [(3, 2), (2, 1), (1, 0)]))  2.58 us
    ppermute x2, starting transfers between devices, relay(): thirds.append(lax.ppermute(third, 'ctx', [(3, 2), (2, 0)]))  2.58 us
    ppermute x1, waiting for transfers between devices, spread(): gamma = lax.ppermute(sent_again, 'ctx', [(0, 1), (1, 2)])  2.34 us
  transfers between devices with their start and end apart: 9, of which 4 were waited for; matrix products, arithmetic and copies ran while one was open for 0% of the time, Pallas kernels for 17%

commit v1 on v0

--- a/solution.py
+++ b/solution.py
@@ -402,6 +402,10 @@
         term = acc_ref[pl.ds(start, slots), :].astype(term_ref.dtype)
         if term_ref.shape == term.shape:
             term_ref[...] = term
+        elif term_ref is terms[0]:
+            term_ref[:, : 2 * HEAD_DIM] = term
+            nearest = acc_ref[pl.ds(starts[1], slots), :].astype(term_ref.dtype)
+            term_ref[:, 2 * HEAD_DIM :] = nearest
         else:
             term_ref[:, : -2 * HEAD_DIM] = before[0][...]
             term_ref[:, -2 * HEAD_DIM :] = term
@@ -421,6 +425,8 @@
         step_units = 4
     terms = [jax.ShapeDtypeStruct((slots, 2 * HEAD_DIM), jnp.bfloat16)] * (ctx_size - 1)
     if relayed(ctx_size):
+        if key_head == 0:
+            terms[0] = jax.ShapeDtypeStruct((slots, 4 * HEAD_DIM), jnp.bfloat16)
         terms[1] = jax.ShapeDtypeStruct((slots, 2 * (key_head + 1) * HEAD_DIM), jnp.bfloat16)
         terms[2] = jax.ShapeDtypeStruct((slots, 2 * HEAD_DIM), jnp.float32)
     outs = pl.pallas_call(
@@ -499,7 +505,7 @@
     )
 
 
-def local_terms(key_head, meta, cos_full, sin_full, turned, out_grad, sent, own, joined, dq, after):
+def local_terms(meta, cos_full, sin_full, turned, out_grad, sent, own, key_head, joined, dq, after):
     slots = turned.shape[0]
     heads = joined[1].shape[0]
     weight, product, _ = own
@@ -534,13 +540,14 @@
 
 
 def add_kernel(own_ref, arrived_ref, *refs):
-    refs[-1][...] = (own_ref[...] + arrived_ref[...].astype(jnp.float32)).astype(jnp.bfloat16)
+    arrived = arrived_ref[:, : own_ref.shape[1]].astype(jnp.float32)
+    refs[-1][...] = (own_ref[...] + arrived).astype(jnp.bfloat16)
 
 
 def add_terms(own, arrived, after):
     return pl.pallas_call(
         add_kernel,
-        out_shape=jax.ShapeDtypeStruct(arrived.shape, jnp.bfloat16),
+        out_shape=jax.ShapeDtypeStruct(own.shape, jnp.bfloat16),
         in_specs=[VMEM] * (2 + len(after)),
         out_specs=VMEM,
         compiler_params=vmem(0, 16, 16),
@@ -555,13 +562,17 @@
     slots = cos_ref.shape[0]
     live = lax.broadcasted_iota(jnp.int32, (slots, HEAD_DIM), 0) < meta_ref[ctx_size]
     totals = [own[...] for own in owns]
-    for index in range(ctx_size - 1):
+    if relayed(ctx_size):
+        second = lax.axis_index("ctx") == 2
+        for head in range(key_heads):
+            first = terms.pop(0)[...].astype(jnp.float32)
+            beside = first[:, 2 * HEAD_DIM :] if first.shape[1] > 2 * HEAD_DIM else 0.0
+            totals[head] += jnp.where(second, beside, first[:, : 2 * HEAD_DIM])
+    while terms:
         parts = [terms.pop(0)]
         if parts[0].shape[1] == 2 * HEAD_DIM:
             parts += [terms.pop(0) for _ in range(key_heads - 1)]
         term = jnp.concatenate([part[...] for part in parts], axis=1).astype(jnp.float32)
-        if index == 0 and relayed(ctx_size):
-            term = jnp.where(lax.axis_index("ctx") == 2, 0.0, term)
         for head in range(key_heads):
             totals[head] += term[:, 2 * head * HEAD_DIM : 2 * (head + 1) * HEAD_DIM]
     for head, total in enumerate(totals):
@@ -596,16 +607,6 @@
         pairs = [(shard, shard + 1) for shard in range(hop - 1, ctx_size - 1)]
         blocks.append(lax.ppermute(blocks[-1], "ctx", pairs))
     return blocks[1:]
-
-
-def relay(terms):
-    firsts, thirds, after = [], [], []
-    for first, _, third in terms:
-        firsts.append(lax.ppermute(first, "ctx", [(3, 2), (2, 1), (1, 0)]))
-        third = add_terms(third, firsts[-1], after)
-        thirds.append(lax.ppermute(third, "ctx", [(3, 2), (2, 0)]))
-        after = [third]
-    return firsts + thirds + [lax.ppermute(terms[-1][1], "ctx", [(3, 1)])]
 
 
 def descend(terms, ctx_size):
@@ -644,17 +645,25 @@
         )
         terms.append(outs[0])
         joined.append(outs[1])
+    local = functools.partial(
+        local_terms, meta, cos_full, sin_full, turned, out_grad[0], sent, own
+    )
+    dq = None
     if relayed(ctx_size):
-        arrived = relay(terms)
+        down = [(3, 2), (2, 1), (1, 0)]
+        firsts = [lax.ppermute(first, "ctx", down) for first, _, _ in terms]
+        relays = []
+        for head in range(key_heads):
+            total = add_terms(terms[head][2], firsts[head], owns[-1:])
+            relays.append(lax.ppermute(total, "ctx", [(3, 2), (2, 0)] if relays else [(2, 0)]))
+            dq, own_terms = local(head, joined[head], dq, [total])
+            owns.append(own_terms)
+        arrived = firsts + relays + [lax.ppermute(terms[-1][1], "ctx", [(3, 1)])]
     else:
         arrived = [part for hop in zip(*[descend(term, ctx_size) for term in terms]) for part in hop]
-    dq = None
-    for head in range(key_heads):
-        after = [arrived[0]] if relayed(ctx_size) and head > 0 else []
-        dq, own_terms = local_terms(
-            head, meta, cos_full, sin_full, turned, out_grad[0], sent, own, joined[head], dq, after
-        )
-        owns.append(own_terms)
+        for head in range(key_heads):
+            dq, own_terms = local(head, joined[head], dq, [])
+            owns.append(own_terms)
     key_grad, value_grad = finish(meta, cos_full, sin_full, owns, arrived, ctx_size)
     return (dq[None], key_grad[None], value_grad[None])
 

time: 58.9 us -> 57.7 us (0.980)
  waiting for transfers between devices: 20.8 us -> 19.1 us
    ppermute x5, waiting for transfers between devices: 18.4 us -> 16.7 us  [the longest x2 8.42 us: body(): firsts = [lax.ppermute(first, 'ctx', down) for first, _, _ in terms]]
  transfers between devices with their start and end apart: 9 -> 9, of which waited for: 4 -> 3; matrix products, arithmetic and copies ran while one was open for 0% -> 0% of each run, Pallas kernels for 17% -> 17%
where the time goes in v1:
time: 57.7 us; the launch traced here: 57.1 us
  waiting for transfers between devices  19.1 us (33%)
  starting transfers between devices  17.3 us (30%)
  Pallas kernels  14.7 us (25%)
  local copies, waits for them, and re-layouts  5.23 us (9%)
  between operations  0.84 us (1%)
    ppermute x2, waiting for transfers between devices, body(): firsts = [lax.ppermute(first, 'ctx', down) for first, _, _ in terms]  8.42 us
    ppermute x2, waiting for transfers between devices, body(): lax.ppermute(total, 'ctx', [(3, 2), (2, 0)] if relays else [(2, 0)])  8.32 us
    ppermute x1, starting transfers between devices, spread(): alpha = lax.ppermute(sent, 'ctx', [(0, 2), (2, 3)])  5.96 us
    pallas_call x2, Pallas kernels, local_terms(): pl.pallas_call(functools.partial(local_kernel, key_head), grid=(1,), out_...  5.47 us
    unnamed x20, local copies, waits for them, and re-layouts  5.23 us
    ppermute x1, starting transfers between devices, spread(): gamma = lax.ppermute(sent_again, 'ctx', [(0, 1), (1, 2)])  4.11 us
    ppermute x2, starting transfers between devices, body(): firsts = [lax.ppermute(first, 'ctx', down) for first, _, _ in terms]  2.58 us
    ppermute x2, starting transfers between devices, body(): lax.ppermute(total, 'ctx', [(3, 2), (2, 0)] if relays else [(2, 0)])  2.58 us
  transfers between devices with their start and end apart: 9, of which 3 were waited for; matrix products, arithmetic and copies ran while one was open for 0% of the time, Pallas kernels for 17%

profile of v1, /device:TPU:0, one launch (start us, length us, event | category | flops | bytes accessed | tf_op | source)
XLA Modules:
  0.0 57.1 jit_solution(12479459450129817578)
XLA Ops:
  0.6 2.3 %prepare.1 = (s32[8]{0:T(128)}, f32[256,128]{1,0:T(8,128)}, f32[256,128]{1,0:T(8,128)}, bf16[256,512]{1,0:T(8,128)(2,1)}) custom-call(s32[1,512]{1,0:T(1,128)} %pos_hbm.1, bf16[256,256]{1,0:T(8,128)(2,1)} %bitcast.14, bf16[256,256]{1,0:T(8,128)(2,1)} %bitcast.15), custom_call_target="tpu_custom_call" | custom-call | tf_op jit(solution)/shard_map/prepare/pallas_call | solution.py:116
  2.9 6.0 %collective-permute-start = (bf16[256,512]{1,0:T(8,128)(2,1)}, bf16[256,512]{1,0:T(8,128)(2,1)S(1)}, u32[]{:S(2)}, u32[]{:S(2)}) collective-permute-start(bf16[256,512]{1,0:T(8,128)(2,1)} %get-tuple-element.35.sent_ref), channel_id=1, source_target_pairs={{0,8},{8,12},{1,9},{9,13},{2,10},{10,14},{3,11},{11,15},{16,24},{2... | collective-permute-start | bytes 786440 | tf_op jit(solution)/shard_map/ppermute | solution.py:601
  8.9 0.7 %collective-permute-start.1 = (bf16[256,512]{1,0:T(8,128)(2,1)}, bf16[256,512]{1,0:T(8,128)(2,1)S(1)}, u32[]{:S(2)}, u32[]{:S(2)}) collective-permute-start(bf16[256,512]{1,0:T(8,128)(2,1)} %get-tuple-element.35.sent_ref), channel_id=1, source_target_pairs={{4,12},{5,13},{6,14},{7,15},{20,28},{21,29},{22,30},{23,31}} | collective-permute-start | bytes 786440 | tf_op jit(solution)/shard_map/ppermute | solution.py:602
  9.5 0.0 copy-start
  9.6 1.2 %copy-done = bf16[1,256,2048]{2,1,0:T(8,128)(2,1)S(1)} copy-done((bf16[1,256,2048]{2,1,0:T(8,128)(2,1)S(1)}, bf16[1,256,2048]{2,1,0:T(8,128)(2,1)}, u32[]{:S(2)}) %copy-start) | copy-done | bytes 1048600
  10.8 0.9 %copy-done.2 = f32[256,128]{1,0:T(8,128)S(1)} copy-done((f32[256,128]{1,0:T(8,128)S(1)}, f32[256,128]{1,0:T(8,128)}, u32[]{:S(2)}) %copy-start.2) | copy-done | bytes 131096
  11.7 0.9 %copy-done.4 = f32[256,128]{1,0:T(8,128)S(1)} copy-done((f32[256,128]{1,0:T(8,128)S(1)}, f32[256,128]{1,0:T(8,128)}, u32[]{:S(2)}) %copy-start.4) | copy-done | bytes 131096
  12.6 0.9 %copy-done.6 = bf16[256,512]{1,0:T(8,128)(2,1)S(1)} copy-done((bf16[256,512]{1,0:T(8,128)(2,1)S(1)}, bf16[256,512]{1,0:T(8,128)(2,1)}, u32[]{:S(2)}) %copy-start.6) | copy-done | bytes 262168
  13.5 1.2 %copy-done.9 = bf16[1,256,2048]{2,1,0:T(8,128)(2,1)S(1)} copy-done((bf16[1,256,2048]{2,1,0:T(8,128)(2,1)S(1)}, bf16[1,256,2048]{2,1,0:T(8,128)(2,1)}, u32[]{:S(2)}) %copy-start.9) | copy-done | bytes 1048600
  14.8 1.1 %rotate_queries.1 = (bf16[256,2048]{1,0:T(8,128)(2,1)S(1)}, bf16[2048,256]{1,0:T(8,128)(2,1)S(1)}, bf16[2048,256]{1,0:T(8,128)(2,1)S(1)}, bf16[256,512]{1,0:T(8,128)(2,1)S(1)}) custom-call(f32[256,128]{1,0:T(8,128)S(1)} %copy-done.2, f32[256,128]{1,0:T(8,128)S(1)} %copy-done.4, bf16[256,2048]{1,0:T(8,128)(2,1)S(1)} %bitcast.12, ...), custom_call_target="tpu_custom_call" | custom-call | flops 3000000000 | bytes 4194304 | tf_op jit(solution)/shard_map/rotate_queries/pallas_call | solution.py:157
  15.9 4.1 %collective-permute-start.2 = (bf16[256,512]{1,0:T(8,128)(2,1)S(1)}, bf16[256,512]{1,0:T(8,128)(2,1)S(1)}, u32[]{:S(2)}, u32[]{:S(2)}) collective-permute-start(bf16[256,512]{1,0:T(8,128)(2,1)S(1)} %get-tuple-element.42), channel_id=1, source_target_pairs={{0,4},{4,8},{1,5},{5,9},{2,6},{6,10},{3,7},{7,11},{16,20},{20,24},... | collective-permute-start | bytes 786440 | tf_op jit(solution)/shard_map/ppermute | solution.py:603
  20.0 0.0 collective-permute-done.refs_0_
  20.0 0.7 %collective-permute-start.3 = (bf16[256,512]{1,0:T(8,128)(2,1)S(1)}, bf16[256,512]{1,0:T(8,128)(2,1)S(1)}, u32[]{:S(2)}, u32[]{:S(2)}) collective-permute-start(bf16[256,512]{1,0:T(8,128)(2,1)S(1)} %collective-permute-done.refs_0_), channel_id=1, source_target_pairs={{8,12},{9,13},{10,14},{11,15},{24,28},{25,29},{26,30},{27,31}} | collective-permute-start | bytes 786440 | tf_op jit(solution)/shard_map/ppermute | solution.py:604
  20.7 0.0 copy-start.1
  20.7 2.2 %own_scores.1 = (f32[16,256,256]{2,1,0:T(8,128)S(1)}, f32[16,256,256]{2,1,0:T(8,128)S(1)}, f32[16,8,256]{2,1,0:T(8,128)S(1)}) custom-call(bf16[256,512]{1,0:T(8,128)(2,1)S(1)} %copy-done.7, bf16[2048,256]{1,0:T(8,128)(2,1)S(1)} %get-tuple-element.37.turned_t_ref, bf16[2048,256]{1,0:T(8,128)(2,1)S(1)} %get-tuple-element.38.grad_t_ref), custom_call_target="tpu_custom_call" | custom-call | flops 5000000000 | bytes 10485760 | tf_op jit(solution)/shard_map/own_scores/pallas_call | solution.py:238
  22.9 2.3 %collective-permute-done.2.refs_2_ = bf16[256,512]{1,0:T(8,128)(2,1)S(1)} collective-permute-done((bf16[256,512]{1,0:T(8,128)(2,1)S(1)}, bf16[256,512]{1,0:T(8,128)(2,1)S(1)}, u32[]{:S(2)}, u32[]{:S(2)}) %collective-permute-start.2) | collective-permute-done | bytes 262176 | tf_op jit(solution)/shard_map/ppermute | solution.py:603
  25.3 1.0 %scores.2 = (bf16[256,512]{1,0:T(8,128)(2,1)S(1)}, bf16[256,256]{1,0:T(8,128)(2,1)S(1)}, f32[256,256]{1,0:T(8,128)S(1)}, bf16[576,2048]{1,0:T(8,128)(2,1)S(1)}, ...) custom-call(s32[8]{0:T(128)S(1)} %copy-done.8, bf16[256,2048]{1,0:T(8,128)(2,1)S(1)} %get-tuple-element.36.turned_ref, ...), custom_call_target="tpu_custom_call" | custom-call | flops 4000000000 | bytes 6291456 | tf_op jit(solution)/shard_map/scores/pallas_call | solution.py:432
  26.3 1.3 %collective-permute-start.5 = (bf16[256,512]{1,0:T(8,128)(2,1)S(1)}, bf16[256,512]{1,0:T(8,128)(2,1)S(1)}, u32[]{:S(2)}, u32[]{:S(2)}) collective-permute-start(bf16[256,512]{1,0:T(8,128)(2,1)S(1)} %get-tuple-element.53), channel_id=1, source_target_pairs={{12,8},{8,4},{4,0},{13,9},{9,5},{5,1},{14,10},{10,6},{6,2},{15,11}... | collective-permute-start | bytes 786440 | tf_op jit(solution)/shard_map/ppermute | solution.py:654
  27.6 0.0 copy-start.3
  27.6 0.0 copy-start.5
  27.6 1.2 %scores.3 = (bf16[256,256]{1,0:T(8,128)(2,1)S(1)}, bf16[256,512]{1,0:T(8,128)(2,1)S(1)}, f32[256,256]{1,0:T(8,128)S(1)}, bf16[576,2048]{1,0:T(8,128)(2,1)S(1)}, ...) custom-call(s32[8]{0:T(128)S(1)} %copy-done.8, bf16[256,2048]{1,0:T(8,128)(2,1)S(1)} %get-tuple-element.36.turned_ref, ...), custom_call_target="tpu_custom_call" | custom-call | flops 4000000000 | bytes 6291456 | tf_op jit(solution)/shard_map/scores/pallas_call | solution.py:432
  28.8 1.3 %collective-permute-start.4 = (bf16[256,256]{1,0:T(8,128)(2,1)S(1)}, bf16[256,256]{1,0:T(8,128)(2,1)S(1)}, u32[]{:S(2)}, u32[]{:S(2)}) collective-permute-start(bf16[256,256]{1,0:T(8,128)(2,1)S(1)} %get-tuple-element.48), channel_id=1, source_target_pairs={{12,8},{8,4},{4,0},{13,9},{9,5},{5,1},{14,10},{10,6},{6,2},{15,11}... | collective-permute-start | bytes 393224 | tf_op jit(solution)/shard_map/ppermute | solution.py:654
  30.1 0.7 %collective-permute-start.8 = (bf16[256,512]{1,0:T(8,128)(2,1)S(1)}, bf16[256,512]{1,0:T(8,128)(2,1)S(1)}, u32[]{:S(2)}, u32[]{:S(2)}) collective-permute-start(bf16[256,512]{1,0:T(8,128)(2,1)S(1)} %get-tuple-element.58), channel_id=1, source_target_pairs={{12,4},{13,5},{14,6},{15,7},{28,20},{29,21},{30,22},{31,23}} | collective-permute-start | bytes 786440 | tf_op jit(solution)/shard_map/ppermute | solution.py:661
  30.8 8.4 %collective-permute-done.5.arrived_ref.refs_2_ = bf16[256,512]{1,0:T(8,128)(2,1)S(1)} collective-permute-done((bf16[256,512]{1,0:T(8,128)(2,1)S(1)}, bf16[256,512]{1,0:T(8,128)(2,1)S(1)}, u32[]{:S(2)}, u32[]{:S(2)}) %collective-permute-start.5) | collective-permute-done | bytes 262176 | tf_op jit(solution)/shard_map/ppermute | solution.py:654
  39.2 1.3 %collective-permute-start.6 = (bf16[256,256]{1,0:T(8,128)(2,1)S(1)}, bf16[256,256]{1,0:T(8,128)(2,1)S(1)}, u32[]{:S(2)}, u32[]{:S(2)}) collective-permute-start(bf16[256,256]{1,0:T(8,128)(2,1)S(1)} %add_terms.2.refs_0_), channel_id=1, source_target_pairs={{8,0},{9,1},{10,2},{11,3},{24,16},{25,17},{26,18},{27,19}} | collective-permute-start | bytes 393224 | tf_op jit(solution)/shard_map/ppermute | solution.py:658
  40.5 2.7 %local_terms.2 = (bf16[256,2048]{1,0:T(8,128)(2,1)}, f32[256,256]{1,0:T(8,128)S(1)}) custom-call(s32[8]{0:T(128)S(1)} %copy-done.8, f32[256,128]{1,0:T(8,128)S(1)} %copy-done.3, f32[256,128]{1,0:T(8,128)S(1)} %copy-done.5, bf16[256,2048]{1,0:T(8,128)(2,1)S(1)} %get-tuple-element.36.turned_ref, bf16[256,2048]{1,0:T(8,128)(2,1)S(1)} %bitcast.10, ...), custom_call_target="tpu_custom_call" | custom-call | flops 4000000000 | bytes 10485760 | tf_op jit(solution)/shard_map/local_terms/pallas_call | solution.py:519
  43.2 0.0 collective-permute-done.4.arrived_ref.refs_3_
  43.3 1.3 %collective-permute-start.7 = (bf16[256,256]{1,0:T(8,128)(2,1)S(1)}, bf16[256,256]{1,0:T(8,128)(2,1)S(1)}, u32[]{:S(2)}, u32[]{:S(2)}) collective-permute-start(bf16[256,256]{1,0:T(8,128)(2,1)S(1)} %add_terms.3.refs_0_), channel_id=1, source_target_pairs={{12,8},{8,0},{13,9},{9,1},{14,10},{10,2},{15,11},{11,3},{28,24},{2... | collective-permute-start | bytes 393224 | tf_op jit(solution)/shard_map/ppermute | solution.py:658
  44.6 2.7 %local_terms.3 = (bf16[256,2048]{1,0:T(8,128)(2,1)}, f32[256,256]{1,0:T(8,128)S(1)}) custom-call(s32[8]{0:T(128)S(1)} %copy-done.8, f32[256,128]{1,0:T(8,128)S(1)} %copy-done.3, f32[256,128]{1,0:T(8,128)S(1)} %copy-done.5, bf16[256,2048]{1,0:T(8,128)(2,1)S(1)} %get-tuple-element.36.turned_ref, ...), custom_call_target="tpu_custom_call", output_to_operand_aliasing={{0}: (12, {})} | custom-call | flops 4000000000 | bytes 10485760 | tf_op jit(solution)/shard_map/local_terms/pallas_call | solution.py:519
  47.3 8.3 %collective-permute-done.7.refs_5_ = bf16[256,256]{1,0:T(8,128)(2,1)S(1)} collective-permute-done((bf16[256,256]{1,0:T(8,128)(2,1)S(1)}, bf16[256,256]{1,0:T(8,128)(2,1)S(1)}, u32[]{:S(2)}, u32[]{:S(2)}) %collective-permute-start.7) | collective-permute-done | bytes 131104 | tf_op jit(solution)/shard_map/ppermute | solution.py:658
  55.6 0.0 collective-permute-done.6.refs_4_
  55.6 1.5 %finish.1 = (bf16[256,256]{1,0:T(8,128)(2,1)}, bf16[256,256]{1,0:T(8,128)(2,1)}) custom-call(s32[8]{0:T(128)S(1)} %copy-done.8, f32[256,128]{1,0:T(8,128)S(1)} %copy-done.3, f32[256,128]{1,0:T(8,128)S(1)} %copy-done.5, f32[256,256]{1,0:T(8,128)S(1)} %get-tuple-element.54.refs_0_, f32[256,256]{1,0:T(8,128)S(1)} %get-tuple-element.57.refs_1_, ...), custom_call_target="tpu_custom_call" | custom-call | tf_op jit(solution)/shard_map/finish/pallas_call | solution.py:589
  (16 shorter events, 0.1 us)
Async XLA Ops:
  2.9 17.1 %collective-permute-start = (bf16[256,512]{1,0:T(8,128)(2,1)}, bf16[256,512]{1,0:T(8,128)(2,1)S(1)}, u32[]{:S(2)}, u32[]{:S(2)}) collective-permute-start(bf16[256,512]{1,0:T(8,128)(2,1)} %get-tuple-element.35.sent_ref), channel_id=1, source_target_pairs={{0,8},{8,12},{1,9},{9,13},{2,10},{10,14},{3,11},{11,15},{16,24},{2... | collective-permute-start | bytes 786440 | tf_op jit(solution)/shard_map/ppermute | solution.py:601
  8.9 16.4 %collective-permute-start.1 = (bf16[256,512]{1,0:T(8,128)(2,1)}, bf16[256,512]{1,0:T(8,128)(2,1)S(1)}, u32[]{:S(2)}, u32[]{:S(2)}) collective-permute-start(bf16[256,512]{1,0:T(8,128)(2,1)} %get-tuple-element.35.sent_ref), channel_id=1, source_target_pairs={{4,12},{5,13},{6,14},{7,15},{20,28},{21,29},{22,30},{23,31}} | collective-permute-start | bytes 786440 | tf_op jit(solution)/shard_map/ppermute | solution.py:602
  9.5 1.2 %copy-start = (bf16[1,256,2048]{2,1,0:T(8,128)(2,1)S(1)}, bf16[1,256,2048]{2,1,0:T(8,128)(2,1)}, u32[]{:S(2)}) copy-start(bf16[1,256,2048]{2,1,0:T(8,128)(2,1)} %param.9) | copy-start | bytes 3145732
  10.8 0.9 %copy-start.2 = (f32[256,128]{1,0:T(8,128)S(1)}, f32[256,128]{1,0:T(8,128)}, u32[]{:S(2)}) copy-start(f32[256,128]{1,0:T(8,128)} %get-tuple-element.33.cos_ref) | copy-start | bytes 393220
  11.7 0.9 %copy-start.4 = (f32[256,128]{1,0:T(8,128)S(1)}, f32[256,128]{1,0:T(8,128)}, u32[]{:S(2)}) copy-start(f32[256,128]{1,0:T(8,128)} %get-tuple-element.34.sin_ref) | copy-start | bytes 393220
  12.6 0.9 %copy-start.6 = (bf16[256,512]{1,0:T(8,128)(2,1)S(1)}, bf16[256,512]{1,0:T(8,128)(2,1)}, u32[]{:S(2)}) copy-start(bf16[256,512]{1,0:T(8,128)(2,1)} %get-tuple-element.35.sent_ref) | copy-start | bytes 786436
  13.5 1.2 %copy-start.9 = (bf16[1,256,2048]{2,1,0:T(8,128)(2,1)S(1)}, bf16[1,256,2048]{2,1,0:T(8,128)(2,1)}, u32[]{:S(2)}) copy-start(bf16[1,256,2048]{2,1,0:T(8,128)(2,1)} %param.6) | copy-start | bytes 3145732
  14.8 6.0 %copy-start.7 = (bf16[256,512]{1,0:T(8,128)(2,1)S(1)}, bf16[256,512]{1,0:T(8,128)(2,1)}, u32[]{:S(2)}) copy-start(bf16[256,512]{1,0:T(8,128)(2,1)} %get-tuple-element.35.sent_ref) | copy-start | bytes 786436
  15.9 9.4 %collective-permute-start.2 = (bf16[256,512]{1,0:T(8,128)(2,1)S(1)}, bf16[256,512]{1,0:T(8,128)(2,1)S(1)}, u32[]{:S(2)}, u32[]{:S(2)}) collective-permute-start(bf16[256,512]{1,0:T(8,128)(2,1)S(1)} %get-tuple-element.42), channel_id=1, source_target_pairs={{0,4},{4,8},{1,5},{5,9},{2,6},{6,10},{3,7},{7,11},{16,20},{20,24},... | collective-permute-start | bytes 786440 | tf_op jit(solution)/shard_map/ppermute | solution.py:603
  20.0 5.2 %collective-permute-start.3 = (bf16[256,512]{1,0:T(8,128)(2,1)S(1)}, bf16[256,512]{1,0:T(8,128)(2,1)S(1)}, u32[]{:S(2)}, u32[]{:S(2)}) collective-permute-start(bf16[256,512]{1,0:T(8,128)(2,1)S(1)} %collective-permute-done.refs_0_), channel_id=1, source_target_pairs={{8,12},{9,13},{10,14},{11,15},{24,28},{25,29},{26,30},{27,31}} | collective-permute-start | bytes 786440 | tf_op jit(solution)/shard_map/ppermute | solution.py:604
  20.7 4.6 %copy-start.1 = (bf16[1,256,2048]{2,1,0:T(8,128)(2,1)S(1)}, bf16[1,256,2048]{2,1,0:T(8,128)(2,1)}, u32[]{:S(2)}) copy-start(bf16[1,256,2048]{2,1,0:T(8,128)(2,1)} %param.9) | copy-start | bytes 3145732
  20.7 4.5 %copy-start.8 = (s32[8]{0:T(128)S(1)}, s32[8]{0:T(128)}, u32[]{:S(2)}) copy-start(s32[8]{0:T(128)} %get-tuple-element.32.meta_ref) | copy-start | bytes 100
  26.3 12.9 %collective-permute-start.5 = (bf16[256,512]{1,0:T(8,128)(2,1)S(1)}, bf16[256,512]{1,0:T(8,128)(2,1)S(1)}, u32[]{:S(2)}, u32[]{:S(2)}) collective-permute-start(bf16[256,512]{1,0:T(8,128)(2,1)S(1)} %get-tuple-element.53), channel_id=1, source_target_pairs={{12,8},{8,4},{4,0},{13,9},{9,5},{5,1},{14,10},{10,6},{6,2},{15,11}... | collective-permute-start | bytes 786440 | tf_op jit(solution)/shard_map/ppermute | solution.py:654
  27.6 12.9 %copy-start.3 = (f32[256,128]{1,0:T(8,128)S(1)}, f32[256,128]{1,0:T(8,128)}, u32[]{:S(2)}) copy-start(f32[256,128]{1,0:T(8,128)} %get-tuple-element.33.cos_ref) | copy-start | bytes 393220
  27.6 12.9 %copy-start.5 = (f32[256,128]{1,0:T(8,128)S(1)}, f32[256,128]{1,0:T(8,128)}, u32[]{:S(2)}) copy-start(f32[256,128]{1,0:T(8,128)} %get-tuple-element.34.sin_ref) | copy-start | bytes 393220
  28.8 14.5 %collective-permute-start.4 = (bf16[256,256]{1,0:T(8,128)(2,1)S(1)}, bf16[256,256]{1,0:T(8,128)(2,1)S(1)}, u32[]{:S(2)}, u32[]{:S(2)}) collective-permute-start(bf16[256,256]{1,0:T(8,128)(2,1)S(1)} %get-tuple-element.48), channel_id=1, source_target_pairs={{12,8},{8,4},{4,0},{13,9},{9,5},{5,1},{14,10},{10,6},{6,2},{15,11}... | collective-permute-start | bytes 393224 | tf_op jit(solution)/shard_map/ppermute | solution.py:654
  30.1 17.3 %collective-permute-start.8 = (bf16[256,512]{1,0:T(8,128)(2,1)S(1)}, bf16[256,512]{1,0:T(8,128)(2,1)S(1)}, u32[]{:S(2)}, u32[]{:S(2)}) collective-permute-start(bf16[256,512]{1,0:T(8,128)(2,1)S(1)} %get-tuple-element.58), channel_id=1, source_target_pairs={{12,4},{13,5},{14,6},{15,7},{28,20},{29,21},{30,22},{31,23}} | collective-permute-start | bytes 786440 | tf_op jit(solution)/shard_map/ppermute | solution.py:661
  39.2 16.4 %collective-permute-start.6 = (bf16[256,256]{1,0:T(8,128)(2,1)S(1)}, bf16[256,256]{1,0:T(8,128)(2,1)S(1)}, u32[]{:S(2)}, u32[]{:S(2)}) collective-permute-start(bf16[256,256]{1,0:T(8,128)(2,1)S(1)} %add_terms.2.refs_0_), channel_id=1, source_target_pairs={{8,0},{9,1},{10,2},{11,3},{24,16},{25,17},{26,18},{27,19}} | collective-permute-start | bytes 393224 | tf_op jit(solution)/shard_map/ppermute | solution.py:658
  43.3 12.4 %collective-permute-start.7 = (bf16[256,256]{1,0:T(8,128)(2,1)S(1)}, bf16[256,256]{1,0:T(8,128)(2,1)S(1)}, u32[]{:S(2)}, u32[]{:S(2)}) collective-permute-start(bf16[256,256]{1,0:T(8,128)(2,1)S(1)} %add_terms.3.refs_0_), channel_id=1, source_target_pairs={{12,8},{8,0},{13,9},{9,1},{14,10},{10,2},{15,11},{11,3},{28,24},{2... | collective-permute-start | bytes 393224 | tf_op jit(solution)/shard_map/ppermute | solution.py:658

commit v2 on v1

--- a/solution.py
+++ b/solution.py
@@ -76,7 +76,7 @@
 def prepare_kernel(
     ctx_size, pos_hbm, keys_hbm, values_hbm, meta_ref, cos_ref, sin_ref, sent_ref, *refs
 ):
-    pos_ref, keys_ref, values_ref, sems = refs
+    sent_heads, (pos_ref, keys_ref, values_ref, sems) = refs[:-4], refs[-4:]
     sources = (pos_hbm, keys_hbm, values_hbm)
     targets = (pos_ref, keys_ref, values_ref)
     copies = [
@@ -103,9 +103,9 @@
     for lane in range(0, keys_ref.shape[1], HEAD_DIM):
         lanes = slice(lane, lane + HEAD_DIM)
         key = turn(keys_ref[:, lanes].astype(jnp.float32), cos_full, sin_full)
-        middle = 2 * lane + HEAD_DIM
-        sent_ref[:, 2 * lane : middle] = key.astype(jnp.bfloat16)
-        sent_ref[:, middle : middle + HEAD_DIM] = values_ref[:, lanes]
+        both = jnp.concatenate([key.astype(jnp.bfloat16), values_ref[:, lanes]], axis=1)
+        sent_ref[:, 2 * lane : 2 * (lane + HEAD_DIM)] = both
+        sent_heads[lane // HEAD_DIM][...] = both
 
 
 def prepare(positions, keys, values, ctx_size):
@@ -120,9 +120,10 @@
             table,
             table,
             sent,
+            *[jax.ShapeDtypeStruct((slots, 2 * HEAD_DIM), jnp.bfloat16)] * (width // HEAD_DIM),
         ),
         in_specs=[HBM] * 3,
-        out_specs=(SMEM, VMEM, VMEM, VMEM),
+        out_specs=(SMEM,) + (VMEM,) * (3 + width // HEAD_DIM),
         scratch_shapes=[pltpu.VMEM(operand.shape, operand.dtype) for operand in operands]
         + [pltpu.SemaphoreType.DMA((3,))],
         compiler_params=vmem(positions.shape[1], 60, 60),
@@ -203,7 +204,11 @@
     return slice((2 * key_head + 1) * HEAD_DIM, 2 * (key_head + 1) * HEAD_DIM)
 
 
-def own_kernel(step_heads, sent_ref, turned_t_ref, grad_t_ref, weight_ref, product_ref, sums_ref, bias_ref):
+def own_kernel(step_heads, count, sent_ref, turned_t_ref, grad_t_ref, *refs):
+    weight_ref, product_ref, sums_ref = refs[count : count + 3]
+    bias_ref = refs[-1]
+    for source, target in zip(refs[:count], refs[count + 3 : -1]):
+        target[...] = source[...]
     slots = sent_ref.shape[0]
     key_heads = sent_ref.shape[1] // HEAD_DIM // 2
     heads = turned_t_ref.shape[0] // HEAD_DIM // key_heads
@@ -231,22 +236,28 @@
         lax.fori_loop(0, heads // step_heads, step, 0)
 
 
-def own_scores(sent, turned_t, grad_t):
+def own_scores(sent, turned_t, grad_t, handed):
     slots = sent.shape[0]
     heads = turned_t.shape[0] // HEAD_DIM
     square = jax.ShapeDtypeStruct((heads, slots, slots), jnp.float32)
-    return pl.pallas_call(
-        functools.partial(own_kernel, 4),
-        out_shape=(square, square, jax.ShapeDtypeStruct((heads, 8, slots), jnp.float32)),
-        in_specs=[VMEM] * 3,
-        out_specs=(VMEM,) * 3,
+    outs = pl.pallas_call(
+        functools.partial(own_kernel, 4, len(handed)),
+        out_shape=(
+            square,
+            square,
+            jax.ShapeDtypeStruct((heads, 8, slots), jnp.float32),
+            *[jax.ShapeDtypeStruct(array.shape, array.dtype) for array in handed],
+        ),
+        in_specs=[VMEM] * (3 + len(handed)),
+        out_specs=(VMEM,) * (3 + len(handed)),
         scratch_shapes=[pltpu.VMEM((slots, slots), jnp.float32)],
         compiler_params=vmem(0, 16, 16),
         cost_estimate=pl.CostEstimate(
             flops=5 * 10**9, bytes_accessed=10 * 1024 * 1024, transcendentals=0
         ),
         name="own_scores",
-    )(sent, turned_t, grad_t)
+    )(sent, turned_t, grad_t, *handed)
+    return outs[:3], outs[3:]
 
 
 def scores_kernel(
@@ -277,16 +288,17 @@
         last = lax.axis_index("ctx") == ctx_size - 1
         sent_hops = [jnp.where(last, 3, 1), 2, jnp.where(last, 1, 2)]
 
-    def blocks_of(lanes):
-        blocks = [block[:, lanes] for block in inputs]
+    def blocks_of(lanes, lanes_alone):
+        alone = [block.shape[1] == 2 * HEAD_DIM for block in inputs]
+        blocks = [block[:, lanes_alone if one else lanes] for block, one in zip(inputs, alone)]
         if relayed(ctx_size):
             alpha, beta, gamma, delta = blocks
             blocks = [jnp.where(last, alpha, gamma), jnp.where(last, beta, alpha), delta]
         return blocks
 
-    for ref, lanes in ((key_ref, key_lanes(key_head)), (value_ref, value_lanes(key_head))):
+    for ref, lanes in ((key_ref, key_lanes), (value_ref, value_lanes)):
         ref[slots:span, :] = jnp.zeros((span - slots, HEAD_DIM), jnp.bfloat16)
-        blocks = blocks_of(lanes)
+        blocks = blocks_of(lanes(key_head), lanes(0))
         for hop in range(ctx_size - 1, 0, -1):
             ref[pl.ds(starts[hop], slots), :] = blocks[hop - 1]
     place = lax.broadcasted_iota(jnp.int32, bias_ref.shape, 0)
@@ -415,9 +427,8 @@
     return ctx_size == 4
 
 
-def scores(key_head, meta, turned, out_grad, turned_t, grad_t, sums, blocks, after, routed, ctx_size):
-    slots, width = blocks[0].shape
-    heads = turned.shape[1] // (width // 2)
+def scores(key_head, heads, meta, turned, out_grad, turned_t, grad_t, sums, blocks, after, routed, ctx_size):
+    slots = turned.shape[0]
     span = -(-(routed + ctx_size * ALIGN) // CHUNK) * CHUNK
     sizes, step_units = [(span, slots)], 1
     if span == 2 * CHUNK and routed - slots // 2 + ctx_size * ALIGN <= 3 * CHUNK // 2 + ALIGN:
@@ -596,12 +607,7 @@
     )(meta, cos_full, sin_full, *owns, *terms)
 
 
-def spread(sent, sent_again, ctx_size):
-    if relayed(ctx_size):
-        alpha = lax.ppermute(sent, "ctx", [(0, 2), (2, 3)])
-        beta = lax.ppermute(sent, "ctx", [(1, 3)])
-        gamma = lax.ppermute(sent_again, "ctx", [(0, 1), (1, 2)])
-        return [alpha, beta, gamma, lax.ppermute(alpha, "ctx", [(2, 3)])]
+def climb(sent, ctx_size):
     blocks = [sent]
     for hop in range(1, ctx_size):
         pairs = [(shard, shard + 1) for shard in range(hop - 1, ctx_size - 1)]
@@ -621,24 +627,37 @@
     ctx_size = lax.axis_size("ctx")
     routed = positions.shape[1]
     key_heads = keys.shape[2] // HEAD_DIM
-    meta, cos_full, sin_full, sent = prepare(positions, keys[0], values[0], ctx_size)
+    meta, cos_full, sin_full, sent, *sent_heads = prepare(positions, keys[0], values[0], ctx_size)
     turned, turned_t, grad_t, sent_again = rotate_queries(
-        cos_full, sin_full, queries[0], out_grad[0], sent
+        cos_full, sin_full, queries[0], out_grad[0], sent_heads[0]
     )
-    blocks = spread(sent, sent_again, ctx_size)
-    own = own_scores(sent, turned_t, grad_t)
+    if relayed(ctx_size):
+        alphas = [lax.ppermute(part, "ctx", [(0, 2), (2, 3)]) for part in sent_heads]
+        beta = lax.ppermute(sent, "ctx", [(1, 3)])
+        own, handed = own_scores(sent, turned_t, grad_t, sent_heads[1:] + alphas[1:])
+        blocks = []
+        for head, alpha in enumerate(alphas):
+            near, far = sent_again, alpha
+            if head > 0:
+                near, far = handed[head - 1], handed[head + key_heads - 2]
+            gamma = lax.ppermute(near, "ctx", [(0, 1), (1, 2)])
+            blocks.append([alpha, beta, gamma, lax.ppermute(far, "ctx", [(2, 3)])])
+    else:
+        blocks = [climb(sent, ctx_size)] * key_heads
+        own, _ = own_scores(sent, turned_t, grad_t, [])
     terms, joined, owns = [], [], []
     for head in range(key_heads):
         after = [terms[-1][1]] if terms else []
         outs = scores(
             head,
+            queries.shape[2] // HEAD_DIM // key_heads,
             meta,
             turned,
             out_grad[0],
             turned_t,
             grad_t,
             own[2],
-            blocks,
+            blocks[head],
             after,
             routed,
             ctx_size,

time: 57.7 us -> 55.1 us (0.955)
  waiting for transfers between devices: 19.1 us -> 11.7 us
  starting transfers between devices: 17.3 us -> 21.7 us
    ppermute x4 -> x7, starting transfers between devices: 11.4 us -> 15.8 us  [the longest x2 9.43 us: body(): lax.ppermute(part, 'ctx', [(0, 2), (2, 3)])]
    ppermute x2, waiting for transfers between devices: 8.42 us -> 5.57 us  [body(): firsts = [lax.ppermute(first, 'ctx', down) for first, _, _ in terms]]
    ppermute x4 -> x7, waiting for transfers between devices: 2.34 us -> 0.02 us  [the longest x2 0.01 us: body(): blocks.append([alpha, beta, gamma, lax.ppermute(far, 'ctx', [(2, 3)])])]
    ppermute x2, waiting for transfers between devices: 8.32 us -> 6.12 us  [body(): lax.ppermute(total, 'ctx', [(3, 2), (2, 0)] if relays else [(2, 0)])]
    unnamed x20 -> x22, local copies, waits for them, and re-layouts: 5.23 us -> 5.19 us
  transfers between devices with their start and end apart: 9 -> 12, of which waited for: 3 -> 3; matrix products, arithmetic and copies ran while one was open for 0% -> 0% of each run, Pallas kernels for 17% -> 20%
where the time goes in v2:
time: 55.1 us; the launch traced here: 54.3 us
  starting transfers between devices  21.7 us (39%)
  Pallas kernels  14.8 us (27%)
  waiting for transfers between devices  11.7 us (21%)
  local copies, waits for them, and re-layouts  5.19 us (9%)
  between operations  0.92 us (2%)
    ppermute x2, starting transfers between devices, body(): lax.ppermute(part, 'ctx', [(0, 2), (2, 3)])  9.43 us
    ppermute x2, waiting for transfers between devices, body(): lax.ppermute(total, 'ctx', [(3, 2), (2, 0)] if relays else [(2, 0)])  6.12 us
    ppermute x2, waiting for transfers between devices, body(): firsts = [lax.ppermute(first, 'ctx', down) for first, _, _ in terms]  5.57 us
    pallas_call x2, Pallas kernels, local_terms(): pl.pallas_call(functools.partial(local_kernel, key_head), grid=(1,), out_...  5.46 us
    unnamed x22, local copies, waits for them, and re-layouts  5.19 us
    ppermute x2, starting transfers between devices, body(): gamma = lax.ppermute(near, 'ctx', [(0, 1), (1, 2)])  4.39 us
    ppermute x2, starting transfers between devices, body(): firsts = [lax.ppermute(first, 'ctx', down) for first, _, _ in terms]  2.58 us
    ppermute x2, starting transfers between devices, body(): lax.ppermute(total, 'ctx', [(3, 2), (2, 0)] if relays else [(2, 0)])  2.58 us
  transfers between devices with their start and end apart: 12, of which 3 were waited for; matrix products, arithmetic and copies ran while one was open for 0% of the time, Pallas kernels for 20%

profile of v2, /device:TPU:0, one launch (start us, length us, event | category | flops | bytes accessed | tf_op | source)
XLA Modules:
  0.0 54.3 jit_solution(7364829962295722172)
XLA Ops:
  0.6 2.3 %prepare.1 = (s32[8]{0:T(128)}, f32[256,128]{1,0:T(8,128)}, f32[256,128]{1,0:T(8,128)}, bf16[256,512]{1,0:T(8,128)(2,1)}, bf16[256,256]{1,0:T(8,128)(2,1)}, /*index=5*/bf16[256,256]{1,0:T(8,128)(2,1)}) custom-call(s32[1,512]{1,0:T(1,128)} %pos_hbm.1, bf16[256,256]{1,0:T(8,128)(2,1)} %bitcast.14, bf16[256,256]{1,0:T(8,128)(2,1)} %bitcast.15), custom_call_target="tpu_custom_call" | custom-call | tf_op jit(solution)/shard_map/prepare/pallas_call | solution.py:116
  3.0 5.9 %collective-permute-start.4 = (bf16[256,256]{1,0:T(8,128)(2,1)}, bf16[256,256]{1,0:T(8,128)(2,1)S(1)}, u32[]{:S(2)}, u32[]{:S(2)}) collective-permute-start(bf16[256,256]{1,0:T(8,128)(2,1)} %get-tuple-element.39.sent_ref), channel_id=1, source_target_pairs={{0,8},{8,12},{1,9},{9,13},{2,10},{10,14},{3,11},{11,15},{16,24},{2... | collective-permute-start | bytes 393224 | tf_op jit(solution)/shard_map/ppermute | solution.py:635
  8.9 3.5 %collective-permute-start = (bf16[256,256]{1,0:T(8,128)(2,1)}, bf16[256,256]{1,0:T(8,128)(2,1)S(1)}, u32[]{:S(2)}, u32[]{:S(2)}) collective-permute-start(bf16[256,256]{1,0:T(8,128)(2,1)} %get-tuple-element.44.refs_0_), channel_id=1, source_target_pairs={{0,8},{8,12},{1,9},{9,13},{2,10},{10,14},{3,11},{11,15},{16,24},{2... | collective-permute-start | bytes 393224 | tf_op jit(solution)/shard_map/ppermute | solution.py:635
  12.4 0.7 %collective-permute-start.1 = (bf16[256,512]{1,0:T(8,128)(2,1)}, bf16[256,512]{1,0:T(8,128)(2,1)S(1)}, u32[]{:S(2)}, u32[]{:S(2)}) collective-permute-start(bf16[256,512]{1,0:T(8,128)(2,1)} %get-tuple-element.41.sent_ref), channel_id=1, source_target_pairs={{4,12},{5,13},{6,14},{7,15},{20,28},{21,29},{22,30},{23,31}} | collective-permute-start | bytes 786440 | tf_op jit(solution)/shard_map/ppermute | solution.py:636
  13.1 0.0 copy-start
  13.1 1.2 %copy-done = bf16[1,256,2048]{2,1,0:T(8,128)(2,1)S(1)} copy-done((bf16[1,256,2048]{2,1,0:T(8,128)(2,1)S(1)}, bf16[1,256,2048]{2,1,0:T(8,128)(2,1)}, u32[]{:S(2)}) %copy-start) | copy-done | bytes 1048600
  14.3 0.9 %copy-done.2 = f32[256,128]{1,0:T(8,128)S(1)} copy-done((f32[256,128]{1,0:T(8,128)S(1)}, f32[256,128]{1,0:T(8,128)}, u32[]{:S(2)}) %copy-start.2) | copy-done | bytes 131096
  15.2 0.9 %copy-done.4 = f32[256,128]{1,0:T(8,128)S(1)} copy-done((f32[256,128]{1,0:T(8,128)S(1)}, f32[256,128]{1,0:T(8,128)}, u32[]{:S(2)}) %copy-start.4) | copy-done | bytes 131096
  16.1 1.2 %copy-done.8 = bf16[1,256,2048]{2,1,0:T(8,128)(2,1)S(1)} copy-done((bf16[1,256,2048]{2,1,0:T(8,128)(2,1)S(1)}, bf16[1,256,2048]{2,1,0:T(8,128)(2,1)}, u32[]{:S(2)}) %copy-start.8) | copy-done | bytes 1048600
  17.3 0.9 %copy-done.10 = bf16[256,256]{1,0:T(8,128)(2,1)S(1)} copy-done((bf16[256,256]{1,0:T(8,128)(2,1)S(1)}, bf16[256,256]{1,0:T(8,128)(2,1)}, u32[]{:S(2)}) %copy-start.10) | copy-done | bytes 131096
  18.3 1.1 %rotate_queries.1 = (bf16[256,2048]{1,0:T(8,128)(2,1)S(1)}, bf16[2048,256]{1,0:T(8,128)(2,1)S(1)}, bf16[2048,256]{1,0:T(8,128)(2,1)S(1)}, bf16[256,256]{1,0:T(8,128)(2,1)S(1)}) custom-call(f32[256,128]{1,0:T(8,128)S(1)} %copy-done.2, f32[256,128]{1,0:T(8,128)S(1)} %copy-done.4, bf16[256,2048]{1,0:T(8,128)(2,1)S(1)} %bitcast.12, ...), custom_call_target="tpu_custom_call" | custom-call | flops 3000000000 | bytes 4194304 | tf_op jit(solution)/shard_map/rotate_queries/pallas_call | solution.py:158
  19.4 1.9 %collective-permute-start.5 = (bf16[256,256]{1,0:T(8,128)(2,1)S(1)}, bf16[256,256]{1,0:T(8,128)(2,1)S(1)}, u32[]{:S(2)}, u32[]{:S(2)}) collective-permute-start(bf16[256,256]{1,0:T(8,128)(2,1)S(1)} %get-tuple-element.50), channel_id=1, source_target_pairs={{0,4},{4,8},{1,5},{5,9},{2,6},{6,10},{3,7},{7,11},{16,20},{20,24},... | collective-permute-start | bytes 393224 | tf_op jit(solution)/shard_map/ppermute | solution.py:643
  21.3 0.7 %collective-permute-start.6 = (bf16[256,256]{1,0:T(8,128)(2,1)S(1)}, bf16[256,256]{1,0:T(8,128)(2,1)S(1)}, u32[]{:S(2)}, u32[]{:S(2)}) collective-permute-start(bf16[256,256]{1,0:T(8,128)(2,1)S(1)} %collective-permute-done.4.refs_0_), channel_id=1, source_target_pairs={{8,12},{9,13},{10,14},{11,15},{24,28},{25,29},{26,30},{27,31}} | collective-permute-start | bytes 393224 | tf_op jit(solution)/shard_map/ppermute | solution.py:644
  22.0 0.0 copy-start.1
  22.1 2.2 %own_scores.1 = (f32[16,256,256]{2,1,0:T(8,128)S(1)}, f32[16,256,256]{2,1,0:T(8,128)S(1)}, f32[16,8,256]{2,1,0:T(8,128)S(1)}, bf16[256,256]{1,0:T(8,128)(2,1)S(1)}, bf16[256,256]{1,0:T(8,128)(2,1)S(1)}) custom-call(bf16[256,512]{1,0:T(8,128)(2,1)S(1)} %copy-done.6, bf16[2048,256]{1,0:T(8,128)(2,1)S(1)} %get-tuple-element.42.turned_t_ref, ...), custom_call_target="tpu_custom_call" | custom-call | flops 5000000000 | bytes 10485760 | tf_op jit(solution)/shard_map/own_scores/pallas_call | solution.py:243
  24.3 2.5 %collective-permute-start.2 = (bf16[256,256]{1,0:T(8,128)(2,1)S(1)}, bf16[256,256]{1,0:T(8,128)(2,1)S(1)}, u32[]{:S(2)}, u32[]{:S(2)}) collective-permute-start(bf16[256,256]{1,0:T(8,128)(2,1)S(1)} %get-tuple-element.48), channel_id=1, source_target_pairs={{0,4},{4,8},{1,5},{5,9},{2,6},{6,10},{3,7},{7,11},{16,20},{20,24},... | collective-permute-start | bytes 393224 | tf_op jit(solution)/shard_map/ppermute | solution.py:643
  26.8 0.7 %collective-permute-start.3 = (bf16[256,256]{1,0:T(8,128)(2,1)S(1)}, bf16[256,256]{1,0:T(8,128)(2,1)S(1)}, u32[]{:S(2)}, u32[]{:S(2)}) collective-permute-start(bf16[256,256]{1,0:T(8,128)(2,1)S(1)} %get-tuple-element.49), channel_id=1, source_target_pairs={{8,12},{9,13},{10,14},{11,15},{24,28},{25,29},{26,30},{27,31}} | collective-permute-start | bytes 393224 | tf_op jit(solution)/shard_map/ppermute | solution.py:644
  27.5 1.0 %scores.2 = (bf16[256,512]{1,0:T(8,128)(2,1)S(1)}, bf16[256,256]{1,0:T(8,128)(2,1)S(1)}, f32[256,256]{1,0:T(8,128)S(1)}, bf16[576,2048]{1,0:T(8,128)(2,1)S(1)}, ...) custom-call(s32[8]{0:T(128)S(1)} %copy-done.7, bf16[256,2048]{1,0:T(8,128)(2,1)S(1)} %get-tuple-element.40.turned_ref, ...), custom_call_target="tpu_custom_call" | custom-call | flops 4000000000 | bytes 6291456 | tf_op jit(solution)/shard_map/scores/pallas_call | solution.py:443
  28.5 1.3 %collective-permute-start.8 = (bf16[256,512]{1,0:T(8,128)(2,1)S(1)}, bf16[256,512]{1,0:T(8,128)(2,1)S(1)}, u32[]{:S(2)}, u32[]{:S(2)}) collective-permute-start(bf16[256,512]{1,0:T(8,128)(2,1)S(1)} %get-tuple-element.61), channel_id=1, source_target_pairs={{12,8},{8,4},{4,0},{13,9},{9,5},{5,1},{14,10},{10,6},{6,2},{15,11}... | collective-permute-start | bytes 786440 | tf_op jit(solution)/shard_map/ppermute | solution.py:673
  29.8 0.0 copy-start.3
  29.8 0.0 copy-start.5
  29.8 1.2 %scores.3 = (bf16[256,256]{1,0:T(8,128)(2,1)S(1)}, bf16[256,512]{1,0:T(8,128)(2,1)S(1)}, f32[256,256]{1,0:T(8,128)S(1)}, bf16[576,2048]{1,0:T(8,128)(2,1)S(1)}, ...) custom-call(s32[8]{0:T(128)S(1)} %copy-done.7, bf16[256,2048]{1,0:T(8,128)(2,1)S(1)} %get-tuple-element.40.turned_ref, ...), custom_call_target="tpu_custom_call" | custom-call | flops 4000000000 | bytes 6291456 | tf_op jit(solution)/shard_map/scores/pallas_call | solution.py:443
  31.0 1.3 %collective-permute-start.7 = (bf16[256,256]{1,0:T(8,128)(2,1)S(1)}, bf16[256,256]{1,0:T(8,128)(2,1)S(1)}, u32[]{:S(2)}, u32[]{:S(2)}) collective-permute-start(bf16[256,256]{1,0:T(8,128)(2,1)S(1)} %get-tuple-element.56), channel_id=1, source_target_pairs={{12,8},{8,4},{4,0},{13,9},{9,5},{5,1},{14,10},{10,6},{6,2},{15,11}... | collective-permute-start | bytes 393224 | tf_op jit(solution)/shard_map/ppermute | solution.py:673
  32.3 0.7 %collective-permute-start.11 = (bf16[256,512]{1,0:T(8,128)(2,1)S(1)}, bf16[256,512]{1,0:T(8,128)(2,1)S(1)}, u32[]{:S(2)}, u32[]{:S(2)}) collective-permute-start(bf16[256,512]{1,0:T(8,128)(2,1)S(1)} %get-tuple-element.66), channel_id=1, source_target_pairs={{12,4},{13,5},{14,6},{15,7},{28,20},{29,21},{30,22},{31,23}} | collective-permute-start | bytes 786440 | tf_op jit(solution)/shard_map/ppermute | solution.py:680
  33.0 5.6 %collective-permute-done.8.arrived_ref.refs_2_ = bf16[256,512]{1,0:T(8,128)(2,1)S(1)} collective-permute-done((bf16[256,512]{1,0:T(8,128)(2,1)S(1)}, bf16[256,512]{1,0:T(8,128)(2,1)S(1)}, u32[]{:S(2)}, u32[]{:S(2)}) %collective-permute-start.8) | collective-permute-done | bytes 262176 | tf_op jit(solution)/shard_map/ppermute | solution.py:673
  38.6 1.3 %collective-permute-start.9 = (bf16[256,256]{1,0:T(8,128)(2,1)S(1)}, bf16[256,256]{1,0:T(8,128)(2,1)S(1)}, u32[]{:S(2)}, u32[]{:S(2)}) collective-permute-start(bf16[256,256]{1,0:T(8,128)(2,1)S(1)} %add_terms.2.refs_0_), channel_id=1, source_target_pairs={{8,0},{9,1},{10,2},{11,3},{24,16},{25,17},{26,18},{27,19}} | collective-permute-start | bytes 393224 | tf_op jit(solution)/shard_map/ppermute | solution.py:677
  39.9 2.7 %local_terms.2 = (bf16[256,2048]{1,0:T(8,128)(2,1)}, f32[256,256]{1,0:T(8,128)S(1)}) custom-call(s32[8]{0:T(128)S(1)} %copy-done.7, f32[256,128]{1,0:T(8,128)S(1)} %copy-done.3, f32[256,128]{1,0:T(8,128)S(1)} %copy-done.5, bf16[256,2048]{1,0:T(8,128)(2,1)S(1)} %get-tuple-element.40.turned_ref, bf16[256,2048]{1,0:T(8,128)(2,1)S(1)} %bitcast.10, ...), custom_call_target="tpu_custom_call" | custom-call | flops 4000000000 | bytes 10485760 | tf_op jit(solution)/shard_map/local_terms/pallas_call | solution.py:530
  42.7 1.3 %collective-permute-start.10 = (bf16[256,256]{1,0:T(8,128)(2,1)S(1)}, bf16[256,256]{1,0:T(8,128)(2,1)S(1)}, u32[]{:S(2)}, u32[]{:S(2)}) collective-permute-start(bf16[256,256]{1,0:T(8,128)(2,1)S(1)} %add_terms.3.refs_0_), channel_id=1, source_target_pairs={{12,8},{8,0},{13,9},{9,1},{14,10},{10,2},{15,11},{11,3},{28,24},{2... | collective-permute-start | bytes 393224 | tf_op jit(solution)/shard_map/ppermute | solution.py:677
  44.0 2.7 %local_terms.3 = (bf16[256,2048]{1,0:T(8,128)(2,1)}, f32[256,256]{1,0:T(8,128)S(1)}) custom-call(s32[8]{0:T(128)S(1)} %copy-done.7, f32[256,128]{1,0:T(8,128)S(1)} %copy-done.3, f32[256,128]{1,0:T(8,128)S(1)} %copy-done.5, bf16[256,2048]{1,0:T(8,128)(2,1)S(1)} %get-tuple-element.40.turned_ref, ...), custom_call_target="tpu_custom_call", output_to_operand_aliasing={{0}: (12, {})} | custom-call | flops 4000000000 | bytes 10485760 | tf_op jit(solution)/shard_map/local_terms/pallas_call | solution.py:530
  46.7 4.2 %collective-permute-done.9.refs_4_ = bf16[256,256]{1,0:T(8,128)(2,1)S(1)} collective-permute-done((bf16[256,256]{1,0:T(8,128)(2,1)S(1)}, bf16[256,256]{1,0:T(8,128)(2,1)S(1)}, u32[]{:S(2)}, u32[]{:S(2)}) %collective-permute-start.9) | collective-permute-done | bytes 131104 | tf_op jit(solution)/shard_map/ppermute | solution.py:677
  50.9 2.0 %collective-permute-done.10.refs_5_ = bf16[256,256]{1,0:T(8,128)(2,1)S(1)} collective-permute-done((bf16[256,256]{1,0:T(8,128)(2,1)S(1)}, bf16[256,256]{1,0:T(8,128)(2,1)S(1)}, u32[]{:S(2)}, u32[]{:S(2)}) %collective-permute-start.10) | collective-permute-done | bytes 131104 | tf_op jit(solution)/shard_map/ppermute | solution.py:677
  52.8 1.4 %finish.1 = (bf16[256,256]{1,0:T(8,128)(2,1)}, bf16[256,256]{1,0:T(8,128)(2,1)}) custom-call(s32[8]{0:T(128)S(1)} %copy-done.7, f32[256,128]{1,0:T(8,128)S(1)} %copy-done.3, f32[256,128]{1,0:T(8,128)S(1)} %copy-done.5, f32[256,256]{1,0:T(8,128)S(1)} %get-tuple-element.62.refs_0_, f32[256,256]{1,0:T(8,128)S(1)} %get-tuple-element.65.refs_1_, ...), custom_call_target="tpu_custom_call" | custom-call | tf_op jit(solution)/shard_map/finish/pallas_call | solution.py:600
  (24 shorter events, 0.1 us)
Async XLA Ops:
  3.0 18.4 %collective-permute-start.4 = (bf16[256,256]{1,0:T(8,128)(2,1)}, bf16[256,256]{1,0:T(8,128)(2,1)S(1)}, u32[]{:S(2)}, u32[]{:S(2)}) collective-permute-start(bf16[256,256]{1,0:T(8,128)(2,1)} %get-tuple-element.39.sent_ref), channel_id=1, source_target_pairs={{0,8},{8,12},{1,9},{9,13},{2,10},{10,14},{3,11},{11,15},{16,24},{2... | collective-permute-start | bytes 393224 | tf_op jit(solution)/shard_map/ppermute | solution.py:635
  8.9 13.1 %collective-permute-start = (bf16[256,256]{1,0:T(8,128)(2,1)}, bf16[256,256]{1,0:T(8,128)(2,1)S(1)}, u32[]{:S(2)}, u32[]{:S(2)}) collective-permute-start(bf16[256,256]{1,0:T(8,128)(2,1)} %get-tuple-element.44.refs_0_), channel_id=1, source_target_pairs={{0,8},{8,12},{1,9},{9,13},{2,10},{10,14},{3,11},{11,15},{16,24},{2... | collective-permute-start | bytes 393224 | tf_op jit(solution)/shard_map/ppermute | solution.py:635
  12.4 15.1 %collective-permute-start.1 = (bf16[256,512]{1,0:T(8,128)(2,1)}, bf16[256,512]{1,0:T(8,128)(2,1)S(1)}, u32[]{:S(2)}, u32[]{:S(2)}) collective-permute-start(bf16[256,512]{1,0:T(8,128)(2,1)} %get-tuple-element.41.sent_ref), channel_id=1, source_target_pairs={{4,12},{5,13},{6,14},{7,15},{20,28},{21,29},{22,30},{23,31}} | collective-permute-start | bytes 786440 | tf_op jit(solution)/shard_map/ppermute | solution.py:636
  13.1 1.2 %copy-start = (bf16[1,256,2048]{2,1,0:T(8,128)(2,1)S(1)}, bf16[1,256,2048]{2,1,0:T(8,128)(2,1)}, u32[]{:S(2)}) copy-start(bf16[1,256,2048]{2,1,0:T(8,128)(2,1)} %param.9) | copy-start | bytes 3145732
  14.3 0.9 %copy-start.2 = (f32[256,128]{1,0:T(8,128)S(1)}, f32[256,128]{1,0:T(8,128)}, u32[]{:S(2)}) copy-start(f32[256,128]{1,0:T(8,128)} %get-tuple-element.37.cos_ref) | copy-start | bytes 393220
  15.2 0.9 %copy-start.4 = (f32[256,128]{1,0:T(8,128)S(1)}, f32[256,128]{1,0:T(8,128)}, u32[]{:S(2)}) copy-start(f32[256,128]{1,0:T(8,128)} %get-tuple-element.38.sin_ref) | copy-start | bytes 393220
  16.1 1.2 %copy-start.8 = (bf16[1,256,2048]{2,1,0:T(8,128)(2,1)S(1)}, bf16[1,256,2048]{2,1,0:T(8,128)(2,1)}, u32[]{:S(2)}) copy-start(bf16[1,256,2048]{2,1,0:T(8,128)(2,1)} %param.6) | copy-start | bytes 3145732
  17.3 0.9 %copy-start.10 = (bf16[256,256]{1,0:T(8,128)(2,1)S(1)}, bf16[256,256]{1,0:T(8,128)(2,1)}, u32[]{:S(2)}) copy-start(bf16[256,256]{1,0:T(8,128)(2,1)} %get-tuple-element.39.sent_ref) | copy-start | bytes 393220
  18.3 3.8 %copy-start.6 = (bf16[256,512]{1,0:T(8,128)(2,1)S(1)}, bf16[256,512]{1,0:T(8,128)(2,1)}, u32[]{:S(2)}) copy-start(bf16[256,512]{1,0:T(8,128)(2,1)} %get-tuple-element.41.sent_ref) | copy-start | bytes 786436
  18.3 3.8 %copy-start.9 = (bf16[256,256]{1,0:T(8,128)(2,1)S(1)}, bf16[256,256]{1,0:T(8,128)(2,1)}, u32[]{:S(2)}) copy-start(bf16[256,256]{1,0:T(8,128)(2,1)} %get-tuple-element.44.refs_0_) | copy-start | bytes 393220
  19.4 8.1 %collective-permute-start.5 = (bf16[256,256]{1,0:T(8,128)(2,1)S(1)}, bf16[256,256]{1,0:T(8,128)(2,1)S(1)}, u32[]{:S(2)}, u32[]{:S(2)}) collective-permute-start(bf16[256,256]{1,0:T(8,128)(2,1)S(1)} %get-tuple-element.50), channel_id=1, source_target_pairs={{0,4},{4,8},{1,5},{5,9},{2,6},{6,10},{3,7},{7,11},{16,20},{20,24},... | collective-permute-start | bytes 393224 | tf_op jit(solution)/shard_map/ppermute | solution.py:643
  21.3 6.1 %collective-permute-start.6 = (bf16[256,256]{1,0:T(8,128)(2,1)S(1)}, bf16[256,256]{1,0:T(8,128)(2,1)S(1)}, u32[]{:S(2)}, u32[]{:S(2)}) collective-permute-start(bf16[256,256]{1,0:T(8,128)(2,1)S(1)} %collective-permute-done.4.refs_0_), channel_id=1, source_target_pairs={{8,12},{9,13},{10,14},{11,15},{24,28},{25,29},{26,30},{27,31}} | collective-permute-start | bytes 393224 | tf_op jit(solution)/shard_map/ppermute | solution.py:644
  22.0 5.5 %copy-start.1 = (bf16[1,256,2048]{2,1,0:T(8,128)(2,1)S(1)}, bf16[1,256,2048]{2,1,0:T(8,128)(2,1)}, u32[]{:S(2)}) copy-start(bf16[1,256,2048]{2,1,0:T(8,128)(2,1)} %param.9) | copy-start | bytes 3145732
  22.1 5.4 %copy-start.7 = (s32[8]{0:T(128)S(1)}, s32[8]{0:T(128)}, u32[]{:S(2)}) copy-start(s32[8]{0:T(128)} %get-tuple-element.36.meta_ref) | copy-start | bytes 100
  24.3 5.5 %collective-permute-start.2 = (bf16[256,256]{1,0:T(8,128)(2,1)S(1)}, bf16[256,256]{1,0:T(8,128)(2,1)S(1)}, u32[]{:S(2)}, u32[]{:S(2)}) collective-permute-start(bf16[256,256]{1,0:T(8,128)(2,1)S(1)} %get-tuple-element.48), channel_id=1, source_target_pairs={{0,4},{4,8},{1,5},{5,9},{2,6},{6,10},{3,7},{7,11},{16,20},{20,24},... | collective-permute-start | bytes 393224 | tf_op jit(solution)/shard_map/ppermute | solution.py:643
  26.8 3.0 %collective-permute-start.3 = (bf16[256,256]{1,0:T(8,128)(2,1)S(1)}, bf16[256,256]{1,0:T(8,128)(2,1)S(1)}, u32[]{:S(2)}, u32[]{:S(2)}) collective-permute-start(bf16[256,256]{1,0:T(8,128)(2,1)S(1)} %get-tuple-element.49), channel_id=1, source_target_pairs={{8,12},{9,13},{10,14},{11,15},{24,28},{25,29},{26,30},{27,31}} | collective-permute-start | bytes 393224 | tf_op jit(solution)/shard_map/ppermute | solution.py:644
  28.5 10.1 %collective-permute-start.8 = (bf16[256,512]{1,0:T(8,128)(2,1)S(1)}, bf16[256,512]{1,0:T(8,128)(2,1)S(1)}, u32[]{:S(2)}, u32[]{:S(2)}) collective-permute-start(bf16[256,512]{1,0:T(8,128)(2,1)S(1)} %get-tuple-element.61), channel_id=1, source_target_pairs={{12,8},{8,4},{4,0},{13,9},{9,5},{5,1},{14,10},{10,6},{6,2},{15,11}... | collective-permute-start | bytes 786440 | tf_op jit(solution)/shard_map/ppermute | solution.py:673
  29.8 10.1 %copy-start.3 = (f32[256,128]{1,0:T(8,128)S(1)}, f32[256,128]{1,0:T(8,128)}, u32[]{:S(2)}) copy-start(f32[256,128]{1,0:T(8,128)} %get-tuple-element.37.cos_ref) | copy-start | bytes 393220
  29.8 10.1 %copy-start.5 = (f32[256,128]{1,0:T(8,128)S(1)}, f32[256,128]{1,0:T(8,128)}, u32[]{:S(2)}) copy-start(f32[256,128]{1,0:T(8,128)} %get-tuple-element.38.sin_ref) | copy-start | bytes 393220
  31.0 11.6 %collective-permute-start.7 = (bf16[256,256]{1,0:T(8,128)(2,1)S(1)}, bf16[256,256]{1,0:T(8,128)(2,1)S(1)}, u32[]{:S(2)}, u32[]{:S(2)}) collective-permute-start(bf16[256,256]{1,0:T(8,128)(2,1)S(1)} %get-tuple-element.56), channel_id=1, source_target_pairs={{12,8},{8,4},{4,0},{13,9},{9,5},{5,1},{14,10},{10,6},{6,2},{15,11}... | collective-permute-start | bytes 393224 | tf_op jit(solution)/shard_map/ppermute | solution.py:673
  32.3 14.4 %collective-permute-start.11 = (bf16[256,512]{1,0:T(8,128)(2,1)S(1)}, bf16[256,512]{1,0:T(8,128)(2,1)S(1)}, u32[]{:S(2)}, u32[]{:S(2)}) collective-permute-start(bf16[256,512]{1,0:T(8,128)(2,1)S(1)} %get-tuple-element.66), channel_id=1, source_target_pairs={{12,4},{13,5},{14,6},{15,7},{28,20},{29,21},{30,22},{31,23}} | collective-permute-start | bytes 786440 | tf_op jit(solution)/shard_map/ppermute | solution.py:680
  38.6 12.3 %collective-permute-start.9 = (bf16[256,256]{1,0:T(8,128)(2,1)S(1)}, bf16[256,256]{1,0:T(8,128)(2,1)S(1)}, u32[]{:S(2)}, u32[]{:S(2)}) collective-permute-start(bf16[256,256]{1,0:T(8,128)(2,1)S(1)} %add_terms.2.refs_0_), channel_id=1, source_target_pairs={{8,0},{9,1},{10,2},{11,3},{24,16},{25,17},{26,18},{27,19}} | collective-permute-start | bytes 393224 | tf_op jit(solution)/shard_map/ppermute | solution.py:677
  42.7 10.2 %collective-permute-start.10 = (bf16[256,256]{1,0:T(8,128)(2,1)S(1)}, bf16[256,256]{1,0:T(8,128)(2,1)S(1)}, u32[]{:S(2)}, u32[]{:S(2)}) collective-permute-start(bf16[256,256]{1,0:T(8,128)(2,1)S(1)} %add_terms.3.refs_0_), channel_id=1, source_target_pairs={{12,8},{8,0},{13,9},{9,1},{14,10},{10,2},{15,11},{11,3},{28,24},{2... | collective-permute-start | bytes 393224 | tf_op jit(solution)/shard_map/ppermute | solution.py:677

commit v3 on v2

--- a/solution.py
+++ b/solution.py
@@ -126,7 +126,7 @@
         out_specs=(SMEM,) + (VMEM,) * (3 + width // HEAD_DIM),
         scratch_shapes=[pltpu.VMEM(operand.shape, operand.dtype) for operand in operands]
         + [pltpu.SemaphoreType.DMA((3,))],
-        compiler_params=vmem(positions.shape[1], 60, 60),
+        compiler_params=vmem(positions.shape[1], 54, 60),
         name="prepare",
     )(*operands)
 
@@ -286,7 +286,7 @@
     sent_hops = list(range(1, ctx_size))
     if relayed(ctx_size):
         last = lax.axis_index("ctx") == ctx_size - 1
-        sent_hops = [jnp.where(last, 3, 1), 2, jnp.where(last, 1, 2)]
+        sent_hops = [jnp.where(last, 3, 1), jnp.where(last, 2, 1), jnp.where(last, 1, 2)]
 
     def blocks_of(lanes, lanes_alone):
         alone = [block.shape[1] == 2 * HEAD_DIM for block in inputs]
@@ -669,15 +669,14 @@
     )
     dq = None
     if relayed(ctx_size):
-        down = [(3, 2), (2, 1), (1, 0)]
-        firsts = [lax.ppermute(first, "ctx", down) for first, _, _ in terms]
+        firsts = [lax.ppermute(first, "ctx", [(3, 2), (2, 1)]) for first, _, _ in terms]
         relays = []
         for head in range(key_heads):
             total = add_terms(terms[head][2], firsts[head], owns[-1:])
             relays.append(lax.ppermute(total, "ctx", [(3, 2), (2, 0)] if relays else [(2, 0)]))
             dq, own_terms = local(head, joined[head], dq, [total])
             owns.append(own_terms)
-        arrived = firsts + relays + [lax.ppermute(terms[-1][1], "ctx", [(3, 1)])]
+        arrived = firsts + relays + [lax.ppermute(terms[-1][1], "ctx", [(3, 1), (1, 0)])]
     else:
         arrived = [part for hop in zip(*[descend(term, ctx_size) for term in terms]) for part in hop]
         for head in range(key_heads):

time: 55.1 us -> 55.2 us (level); the launches traced: 54.3 us -> 56.2 us
  waiting for transfers between devices: 11.7 us -> 14.3 us
  starting transfers between devices: 21.7 us -> 21.1 us
    ppermute x2, waiting for transfers between devices: 6.12 us -> 8.51 us  [body(): lax.ppermute(total, 'ctx', [(3, 2), (2, 0)] if relays else [(2, 0)])]
    ppermute x3, starting transfers between devices: 3.26 us -> 2.64 us  [the longest x2 1.35 us: body(): lax.ppermute(first, 'ctx', [(3, 2), (2, 1)])]
  transfers between devices with their start and end apart: 12 -> 12, of which waited for: 3 -> 4; matrix products, arithmetic and copies ran while one was open for 0% -> 0% of each run, Pallas kernels for 20% -> 20%
where the time goes in v3:
time: 55.2 us; the launch traced here: 56.2 us
  starting transfers between devices  21.1 us (38%)
  Pallas kernels  14.8 us (27%)
  waiting for transfers between devices  14.3 us (26%)
  local copies, waits for them, and re-layouts  5.18 us (9%)
  between operations  0.9 us (2%)
    ppermute x2, starting transfers between devices, body(): lax.ppermute(part, 'ctx', [(0, 2), (2, 3)])  9.43 us
    ppermute x2, waiting for transfers between devices, body(): lax.ppermute(total, 'ctx', [(3, 2), (2, 0)] if relays else [(2, 0)])  8.51 us
    ppermute x1, waiting for transfers between devices, body(): lax.ppermute(terms[-1][1], 'ctx', [(3, 1), (1, 0)])  5.67 us
    pallas_call x2, Pallas kernels, local_terms(): pl.pallas_call(functools.partial(local_kernel, key_head), grid=(1,), out_...  5.46 us
    unnamed x22, local copies, waits for them, and re-layouts  5.18 us
    ppermute x2, starting transfers between devices, body(): gamma = lax.ppermute(near, 'ctx', [(0, 1), (1, 2)])  4.39 us
    ppermute x2, starting transfers between devices, body(): lax.ppermute(total, 'ctx', [(3, 2), (2, 0)] if relays else [(2, 0)])  2.58 us
    pallas_call x1, Pallas kernels, prepare(): pl.pallas_call(functools.partial(prepare_kernel, ctx_size), out_shape=(ja...  2.31 us
  transfers between devices with their start and end apart: 12, of which 4 were waited for; matrix products, arithmetic and copies ran while one was open for 0% of the time, Pallas kernels for 20%

profile of v3, /device:TPU:0, one launch (start us, length us, event | category | flops | bytes accessed | tf_op | source)
XLA Modules:
  0.0 56.2 jit_solution(15657926206992135808)
XLA Ops:
  0.6 2.3 %prepare.1 = (s32[8]{0:T(128)}, f32[256,128]{1,0:T(8,128)}, f32[256,128]{1,0:T(8,128)}, bf16[256,512]{1,0:T(8,128)(2,1)}, bf16[256,256]{1,0:T(8,128)(2,1)}, /*index=5*/bf16[256,256]{1,0:T(8,128)(2,1)}) custom-call(s32[1,512]{1,0:T(1,128)} %pos_hbm.1, bf16[256,256]{1,0:T(8,128)(2,1)} %bitcast.14, bf16[256,256]{1,0:T(8,128)(2,1)} %bitcast.15), custom_call_target="tpu_custom_call" | custom-call | tf_op jit(solution)/shard_map/prepare/pallas_call | solution.py:116
  3.0 5.9 %collective-permute-start.4 = (bf16[256,256]{1,0:T(8,128)(2,1)}, bf16[256,256]{1,0:T(8,128)(2,1)S(1)}, u32[]{:S(2)}, u32[]{:S(2)}) collective-permute-start(bf16[256,256]{1,0:T(8,128)(2,1)} %get-tuple-element.39.sent_ref), channel_id=1, source_target_pairs={{0,8},{8,12},{1,9},{9,13},{2,10},{10,14},{3,11},{11,15},{16,24},{2... | collective-permute-start | bytes 393224 | tf_op jit(solution)/shard_map/ppermute | solution.py:635
  8.9 3.5 %collective-permute-start = (bf16[256,256]{1,0:T(8,128)(2,1)}, bf16[256,256]{1,0:T(8,128)(2,1)S(1)}, u32[]{:S(2)}, u32[]{:S(2)}) collective-permute-start(bf16[256,256]{1,0:T(8,128)(2,1)} %get-tuple-element.44.refs_0_), channel_id=1, source_target_pairs={{0,8},{8,12},{1,9},{9,13},{2,10},{10,14},{3,11},{11,15},{16,24},{2... | collective-permute-start | bytes 393224 | tf_op jit(solution)/shard_map/ppermute | solution.py:635
  12.4 0.7 %collective-permute-start.1 = (bf16[256,512]{1,0:T(8,128)(2,1)}, bf16[256,512]{1,0:T(8,128)(2,1)S(1)}, u32[]{:S(2)}, u32[]{:S(2)}) collective-permute-start(bf16[256,512]{1,0:T(8,128)(2,1)} %get-tuple-element.41.sent_ref), channel_id=1, source_target_pairs={{4,12},{5,13},{6,14},{7,15},{20,28},{21,29},{22,30},{23,31}} | collective-permute-start | bytes 786440 | tf_op jit(solution)/shard_map/ppermute | solution.py:636
  13.1 0.0 copy-start
  13.1 1.2 %copy-done = bf16[1,256,2048]{2,1,0:T(8,128)(2,1)S(1)} copy-done((bf16[1,256,2048]{2,1,0:T(8,128)(2,1)S(1)}, bf16[1,256,2048]{2,1,0:T(8,128)(2,1)}, u32[]{:S(2)}) %copy-start) | copy-done | bytes 1048600
  14.3 0.9 %copy-done.2 = f32[256,128]{1,0:T(8,128)S(1)} copy-done((f32[256,128]{1,0:T(8,128)S(1)}, f32[256,128]{1,0:T(8,128)}, u32[]{:S(2)}) %copy-start.2) | copy-done | bytes 131096
  15.2 0.9 %copy-done.4 = f32[256,128]{1,0:T(8,128)S(1)} copy-done((f32[256,128]{1,0:T(8,128)S(1)}, f32[256,128]{1,0:T(8,128)}, u32[]{:S(2)}) %copy-start.4) | copy-done | bytes 131096
  16.1 1.2 %copy-done.8 = bf16[1,256,2048]{2,1,0:T(8,128)(2,1)S(1)} copy-done((bf16[1,256,2048]{2,1,0:T(8,128)(2,1)S(1)}, bf16[1,256,2048]{2,1,0:T(8,128)(2,1)}, u32[]{:S(2)}) %copy-start.8) | copy-done | bytes 1048600
  17.3 0.9 %copy-done.10 = bf16[256,256]{1,0:T(8,128)(2,1)S(1)} copy-done((bf16[256,256]{1,0:T(8,128)(2,1)S(1)}, bf16[256,256]{1,0:T(8,128)(2,1)}, u32[]{:S(2)}) %copy-start.10) | copy-done | bytes 131096
  18.3 1.1 %rotate_queries.1 = (bf16[256,2048]{1,0:T(8,128)(2,1)S(1)}, bf16[2048,256]{1,0:T(8,128)(2,1)S(1)}, bf16[2048,256]{1,0:T(8,128)(2,1)S(1)}, bf16[256,256]{1,0:T(8,128)(2,1)S(1)}) custom-call(f32[256,128]{1,0:T(8,128)S(1)} %copy-done.2, f32[256,128]{1,0:T(8,128)S(1)} %copy-done.4, bf16[256,2048]{1,0:T(8,128)(2,1)S(1)} %bitcast.12, ...), custom_call_target="tpu_custom_call" | custom-call | flops 3000000000 | bytes 4194304 | tf_op jit(solution)/shard_map/rotate_queries/pallas_call | solution.py:158
  19.4 1.9 %collective-permute-start.5 = (bf16[256,256]{1,0:T(8,128)(2,1)S(1)}, bf16[256,256]{1,0:T(8,128)(2,1)S(1)}, u32[]{:S(2)}, u32[]{:S(2)}) collective-permute-start(bf16[256,256]{1,0:T(8,128)(2,1)S(1)} %get-tuple-element.50), channel_id=1, source_target_pairs={{0,4},{4,8},{1,5},{5,9},{2,6},{6,10},{3,7},{7,11},{16,20},{20,24},... | collective-permute-start | bytes 393224 | tf_op jit(solution)/shard_map/ppermute | solution.py:643
  21.3 0.0 collective-permute-done.4.refs_0_
  21.3 0.7 %collective-permute-start.6 = (bf16[256,256]{1,0:T(8,128)(2,1)S(1)}, bf16[256,256]{1,0:T(8,128)(2,1)S(1)}, u32[]{:S(2)}, u32[]{:S(2)}) collective-permute-start(bf16[256,256]{1,0:T(8,128)(2,1)S(1)} %collective-permute-done.4.refs_0_), channel_id=1, source_target_pairs={{8,12},{9,13},{10,14},{11,15},{24,28},{25,29},{26,30},{27,31}} | collective-permute-start | bytes 393224 | tf_op jit(solution)/shard_map/ppermute | solution.py:644
  22.0 0.0 copy-start.1
  22.1 2.2 %own_scores.1 = (f32[16,256,256]{2,1,0:T(8,128)S(1)}, f32[16,256,256]{2,1,0:T(8,128)S(1)}, f32[16,8,256]{2,1,0:T(8,128)S(1)}, bf16[256,256]{1,0:T(8,128)(2,1)S(1)}, bf16[256,256]{1,0:T(8,128)(2,1)S(1)}) custom-call(bf16[256,512]{1,0:T(8,128)(2,1)S(1)} %copy-done.6, bf16[2048,256]{1,0:T(8,128)(2,1)S(1)} %get-tuple-element.42.turned_t_ref, ...), custom_call_target="tpu_custom_call" | custom-call | flops 5000000000 | bytes 10485760 | tf_op jit(solution)/shard_map/own_scores/pallas_call | solution.py:243
  24.3 2.5 %collective-permute-start.2 = (bf16[256,256]{1,0:T(8,128)(2,1)S(1)}, bf16[256,256]{1,0:T(8,128)(2,1)S(1)}, u32[]{:S(2)}, u32[]{:S(2)}) collective-permute-start(bf16[256,256]{1,0:T(8,128)(2,1)S(1)} %get-tuple-element.48), channel_id=1, source_target_pairs={{0,4},{4,8},{1,5},{5,9},{2,6},{6,10},{3,7},{7,11},{16,20},{20,24},... | collective-permute-start | bytes 393224 | tf_op jit(solution)/shard_map/ppermute | solution.py:643
  26.8 0.7 %collective-permute-start.3 = (bf16[256,256]{1,0:T(8,128)(2,1)S(1)}, bf16[256,256]{1,0:T(8,128)(2,1)S(1)}, u32[]{:S(2)}, u32[]{:S(2)}) collective-permute-start(bf16[256,256]{1,0:T(8,128)(2,1)S(1)} %get-tuple-element.49), channel_id=1, source_target_pairs={{8,12},{9,13},{10,14},{11,15},{24,28},{25,29},{26,30},{27,31}} | collective-permute-start | bytes 393224 | tf_op jit(solution)/shard_map/ppermute | solution.py:644
  27.5 1.0 %scores.2 = (bf16[256,512]{1,0:T(8,128)(2,1)S(1)}, bf16[256,256]{1,0:T(8,128)(2,1)S(1)}, f32[256,256]{1,0:T(8,128)S(1)}, bf16[576,2048]{1,0:T(8,128)(2,1)S(1)}, ...) custom-call(s32[8]{0:T(128)S(1)} %copy-done.7, bf16[256,2048]{1,0:T(8,128)(2,1)S(1)} %get-tuple-element.40.turned_ref, ...), custom_call_target="tpu_custom_call" | custom-call | flops 4000000000 | bytes 6291456 | tf_op jit(solution)/shard_map/scores/pallas_call | solution.py:443
  28.5 0.7 %collective-permute-start.8 = (bf16[256,512]{1,0:T(8,128)(2,1)S(1)}, bf16[256,512]{1,0:T(8,128)(2,1)S(1)}, u32[]{:S(2)}, u32[]{:S(2)}) collective-permute-start(bf16[256,512]{1,0:T(8,128)(2,1)S(1)} %get-tuple-element.61), channel_id=1, source_target_pairs={{12,8},{8,4},{13,9},{9,5},{14,10},{10,6},{15,11},{11,7},{28,24},{2... | collective-permute-start | bytes 786440 | tf_op jit(solution)/shard_map/ppermute | solution.py:672
  29.2 0.1 collective-permute-done.2.refs_2_
  29.3 1.1 %scores.3 = (bf16[256,256]{1,0:T(8,128)(2,1)S(1)}, bf16[256,512]{1,0:T(8,128)(2,1)S(1)}, f32[256,256]{1,0:T(8,128)S(1)}, bf16[576,2048]{1,0:T(8,128)(2,1)S(1)}, ...) custom-call(s32[8]{0:T(128)S(1)} %copy-done.7, bf16[256,2048]{1,0:T(8,128)(2,1)S(1)} %get-tuple-element.40.turned_ref, ...), custom_call_target="tpu_custom_call" | custom-call | flops 4000000000 | bytes 6291456 | tf_op jit(solution)/shard_map/scores/pallas_call | solution.py:443
  30.4 0.7 %collective-permute-start.7 = (bf16[256,256]{1,0:T(8,128)(2,1)S(1)}, bf16[256,256]{1,0:T(8,128)(2,1)S(1)}, u32[]{:S(2)}, u32[]{:S(2)}) collective-permute-start(bf16[256,256]{1,0:T(8,128)(2,1)S(1)} %get-tuple-element.56), channel_id=1, source_target_pairs={{12,8},{8,4},{13,9},{9,5},{14,10},{10,6},{15,11},{11,7},{28,24},{2... | collective-permute-start | bytes 393224 | tf_op jit(solution)/shard_map/ppermute | solution.py:672
  31.1 1.3 %collective-permute-start.11 = (bf16[256,512]{1,0:T(8,128)(2,1)S(1)}, bf16[256,512]{1,0:T(8,128)(2,1)S(1)}, u32[]{:S(2)}, u32[]{:S(2)}) collective-permute-start(bf16[256,512]{1,0:T(8,128)(2,1)S(1)} %get-tuple-element.66), channel_id=1, source_target_pairs={{12,4},{4,0},{13,5},{5,1},{14,6},{6,2},{15,7},{7,3},{28,20},{20,16... | collective-permute-start | bytes 786440 | tf_op jit(solution)/shard_map/ppermute | solution.py:679
  32.5 1.3 %collective-permute-start.9 = (bf16[256,256]{1,0:T(8,128)(2,1)S(1)}, bf16[256,256]{1,0:T(8,128)(2,1)S(1)}, u32[]{:S(2)}, u32[]{:S(2)}) collective-permute-start(bf16[256,256]{1,0:T(8,128)(2,1)S(1)} %add_terms.2.refs_0_), channel_id=1, source_target_pairs={{8,0},{9,1},{10,2},{11,3},{24,16},{25,17},{26,18},{27,19}} | collective-permute-start | bytes 393224 | tf_op jit(solution)/shard_map/ppermute | solution.py:676
  33.8 2.7 %local_terms.2 = (bf16[256,2048]{1,0:T(8,128)(2,1)}, f32[256,256]{1,0:T(8,128)S(1)}) custom-call(s32[8]{0:T(128)S(1)} %copy-done.7, f32[256,128]{1,0:T(8,128)S(1)} %copy-done.3, f32[256,128]{1,0:T(8,128)S(1)} %copy-done.5, bf16[256,2048]{1,0:T(8,128)(2,1)S(1)} %get-tuple-element.40.turned_ref, bf16[256,2048]{1,0:T(8,128)(2,1)S(1)} %bitcast.10, ...), custom_call_target="tpu_custom_call" | custom-call | flops 4000000000 | bytes 10485760 | tf_op jit(solution)/shard_map/local_terms/pallas_call | solution.py:530
  36.6 1.3 %collective-permute-start.10 = (bf16[256,256]{1,0:T(8,128)(2,1)S(1)}, bf16[256,256]{1,0:T(8,128)(2,1)S(1)}, u32[]{:S(2)}, u32[]{:S(2)}) collective-permute-start(bf16[256,256]{1,0:T(8,128)(2,1)S(1)} %add_terms.3.refs_0_), channel_id=1, source_target_pairs={{12,8},{8,0},{13,9},{9,1},{14,10},{10,2},{15,11},{11,3},{28,24},{2... | collective-permute-start | bytes 393224 | tf_op jit(solution)/shard_map/ppermute | solution.py:676
  37.9 2.7 %local_terms.3 = (bf16[256,2048]{1,0:T(8,128)(2,1)}, f32[256,256]{1,0:T(8,128)S(1)}) custom-call(s32[8]{0:T(128)S(1)} %copy-done.7, f32[256,128]{1,0:T(8,128)S(1)} %copy-done.3, f32[256,128]{1,0:T(8,128)S(1)} %copy-done.5, bf16[256,2048]{1,0:T(8,128)(2,1)S(1)} %get-tuple-element.40.turned_ref, ...), custom_call_target="tpu_custom_call", output_to_operand_aliasing={{0}: (12, {})} | custom-call | flops 4000000000 | bytes 10485760 | tf_op jit(solution)/shard_map/local_terms/pallas_call | solution.py:530
  40.6 5.7 %collective-permute-done.11.refs_6_ = bf16[256,512]{1,0:T(8,128)(2,1)S(1)} collective-permute-done((bf16[256,512]{1,0:T(8,128)(2,1)S(1)}, bf16[256,512]{1,0:T(8,128)(2,1)S(1)}, u32[]{:S(2)}, u32[]{:S(2)}) %collective-permute-start.11) | collective-permute-done | bytes 262176 | tf_op jit(solution)/shard_map/ppermute | solution.py:679
  46.3 6.8 %collective-permute-done.9.refs_4_ = bf16[256,256]{1,0:T(8,128)(2,1)S(1)} collective-permute-done((bf16[256,256]{1,0:T(8,128)(2,1)S(1)}, bf16[256,256]{1,0:T(8,128)(2,1)S(1)}, u32[]{:S(2)}, u32[]{:S(2)}) %collective-permute-start.9) | collective-permute-done | bytes 131104 | tf_op jit(solution)/shard_map/ppermute | solution.py:676
  53.0 1.7 %collective-permute-done.10.refs_5_ = bf16[256,256]{1,0:T(8,128)(2,1)S(1)} collective-permute-done((bf16[256,256]{1,0:T(8,128)(2,1)S(1)}, bf16[256,256]{1,0:T(8,128)(2,1)S(1)}, u32[]{:S(2)}, u32[]{:S(2)}) %collective-permute-start.10) | collective-permute-done | bytes 131104 | tf_op jit(solution)/shard_map/ppermute | solution.py:676
  54.8 1.4 %finish.1 = (bf16[256,256]{1,0:T(8,128)(2,1)}, bf16[256,256]{1,0:T(8,128)(2,1)}) custom-call(s32[8]{0:T(128)S(1)} %copy-done.7, f32[256,128]{1,0:T(8,128)S(1)} %copy-done.3, f32[256,128]{1,0:T(8,128)S(1)} %copy-done.5, f32[256,256]{1,0:T(8,128)S(1)} %get-tuple-element.62.refs_0_, f32[256,256]{1,0:T(8,128)S(1)} %get-tuple-element.65.refs_1_, ...), custom_call_target="tpu_custom_call" | custom-call | tf_op jit(solution)/shard_map/finish/pallas_call | solution.py:600
  (24 shorter events, 0.1 us)
Async XLA Ops:
  3.0 18.4 %collective-permute-start.4 = (bf16[256,256]{1,0:T(8,128)(2,1)}, bf16[256,256]{1,0:T(8,128)(2,1)S(1)}, u32[]{:S(2)}, u32[]{:S(2)}) collective-permute-start(bf16[256,256]{1,0:T(8,128)(2,1)} %get-tuple-element.39.sent_ref), channel_id=1, source_target_pairs={{0,8},{8,12},{1,9},{9,13},{2,10},{10,14},{3,11},{11,15},{16,24},{2... | collective-permute-start | bytes 393224 | tf_op jit(solution)/shard_map/ppermute | solution.py:635
  8.9 13.1 %collective-permute-start = (bf16[256,256]{1,0:T(8,128)(2,1)}, bf16[256,256]{1,0:T(8,128)(2,1)S(1)}, u32[]{:S(2)}, u32[]{:S(2)}) collective-permute-start(bf16[256,256]{1,0:T(8,128)(2,1)} %get-tuple-element.44.refs_0_), channel_id=1, source_target_pairs={{0,8},{8,12},{1,9},{9,13},{2,10},{10,14},{3,11},{11,15},{16,24},{2... | collective-permute-start | bytes 393224 | tf_op jit(solution)/shard_map/ppermute | solution.py:635
  12.4 15.1 %collective-permute-start.1 = (bf16[256,512]{1,0:T(8,128)(2,1)}, bf16[256,512]{1,0:T(8,128)(2,1)S(1)}, u32[]{:S(2)}, u32[]{:S(2)}) collective-permute-start(bf16[256,512]{1,0:T(8,128)(2,1)} %get-tuple-element.41.sent_ref), channel_id=1, source_target_pairs={{4,12},{5,13},{6,14},{7,15},{20,28},{21,29},{22,30},{23,31}} | collective-permute-start | bytes 786440 | tf_op jit(solution)/shard_map/ppermute | solution.py:636
  13.1 1.2 %copy-start = (bf16[1,256,2048]{2,1,0:T(8,128)(2,1)S(1)}, bf16[1,256,2048]{2,1,0:T(8,128)(2,1)}, u32[]{:S(2)}) copy-start(bf16[1,256,2048]{2,1,0:T(8,128)(2,1)} %param.9) | copy-start | bytes 3145732
  14.3 0.9 %copy-start.2 = (f32[256,128]{1,0:T(8,128)S(1)}, f32[256,128]{1,0:T(8,128)}, u32[]{:S(2)}) copy-start(f32[256,128]{1,0:T(8,128)} %get-tuple-element.37.cos_ref) | copy-start | bytes 393220
  15.2 0.9 %copy-start.4 = (f32[256,128]{1,0:T(8,128)S(1)}, f32[256,128]{1,0:T(8,128)}, u32[]{:S(2)}) copy-start(f32[256,128]{1,0:T(8,128)} %get-tuple-element.38.sin_ref) | copy-start | bytes 393220
  16.1 1.2 %copy-start.8 = (bf16[1,256,2048]{2,1,0:T(8,128)(2,1)S(1)}, bf16[1,256,2048]{2,1,0:T(8,128)(2,1)}, u32[]{:S(2)}) copy-start(bf16[1,256,2048]{2,1,0:T(8,128)(2,1)} %param.6) | copy-start | bytes 3145732
  17.3 0.9 %copy-start.10 = (bf16[256,256]{1,0:T(8,128)(2,1)S(1)}, bf16[256,256]{1,0:T(8,128)(2,1)}, u32[]{:S(2)}) copy-start(bf16[256,256]{1,0:T(8,128)(2,1)} %get-tuple-element.39.sent_ref) | copy-start | bytes 393220
  18.3 3.8 %copy-start.6 = (bf16[256,512]{1,0:T(8,128)(2,1)S(1)}, bf16[256,512]{1,0:T(8,128)(2,1)}, u32[]{:S(2)}) copy-start(bf16[256,512]{1,0:T(8,128)(2,1)} %get-tuple-element.41.sent_ref) | copy-start | bytes 786436
  18.3 3.8 %copy-start.9 = (bf16[256,256]{1,0:T(8,128)(2,1)S(1)}, bf16[256,256]{1,0:T(8,128)(2,1)}, u32[]{:S(2)}) copy-start(bf16[256,256]{1,0:T(8,128)(2,1)} %get-tuple-element.44.refs_0_) | copy-start | bytes 393220
  19.4 8.1 %collective-permute-start.5 = (bf16[256,256]{1,0:T(8,128)(2,1)S(1)}, bf16[256,256]{1,0:T(8,128)(2,1)S(1)}, u32[]{:S(2)}, u32[]{:S(2)}) collective-permute-start(bf16[256,256]{1,0:T(8,128)(2,1)S(1)} %get-tuple-element.50), channel_id=1, source_target_pairs={{0,4},{4,8},{1,5},{5,9},{2,6},{6,10},{3,7},{7,11},{16,20},{20,24},... | collective-permute-start | bytes 393224 | tf_op jit(solution)/shard_map/ppermute | solution.py:643
  21.3 6.1 %collective-permute-start.6 = (bf16[256,256]{1,0:T(8,128)(2,1)S(1)}, bf16[256,256]{1,0:T(8,128)(2,1)S(1)}, u32[]{:S(2)}, u32[]{:S(2)}) collective-permute-start(bf16[256,256]{1,0:T(8,128)(2,1)S(1)} %collective-permute-done.4.refs_0_), channel_id=1, source_target_pairs={{8,12},{9,13},{10,14},{11,15},{24,28},{25,29},{26,30},{27,31}} | collective-permute-start | bytes 393224 | tf_op jit(solution)/shard_map/ppermute | solution.py:644
  22.0 5.5 %copy-start.1 = (bf16[1,256,2048]{2,1,0:T(8,128)(2,1)S(1)}, bf16[1,256,2048]{2,1,0:T(8,128)(2,1)}, u32[]{:S(2)}) copy-start(bf16[1,256,2048]{2,1,0:T(8,128)(2,1)} %param.9) | copy-start | bytes 3145732
  22.1 5.4 %copy-start.7 = (s32[8]{0:T(128)S(1)}, s32[8]{0:T(128)}, u32[]{:S(2)}) copy-start(s32[8]{0:T(128)} %get-tuple-element.36.meta_ref) | copy-start | bytes 100
  24.3 5.0 %collective-permute-start.2 = (bf16[256,256]{1,0:T(8,128)(2,1)S(1)}, bf16[256,256]{1,0:T(8,128)(2,1)S(1)}, u32[]{:S(2)}, u32[]{:S(2)}) collective-permute-start(bf16[256,256]{1,0:T(8,128)(2,1)S(1)} %get-tuple-element.48), channel_id=1, source_target_pairs={{0,4},{4,8},{1,5},{5,9},{2,6},{6,10},{3,7},{7,11},{16,20},{20,24},... | collective-permute-start | bytes 393224 | tf_op jit(solution)/shard_map/ppermute | solution.py:643
  26.8 2.5 %collective-permute-start.3 = (bf16[256,256]{1,0:T(8,128)(2,1)S(1)}, bf16[256,256]{1,0:T(8,128)(2,1)S(1)}, u32[]{:S(2)}, u32[]{:S(2)}) collective-permute-start(bf16[256,256]{1,0:T(8,128)(2,1)S(1)} %get-tuple-element.49), channel_id=1, source_target_pairs={{8,12},{9,13},{10,14},{11,15},{24,28},{25,29},{26,30},{27,31}} | collective-permute-start | bytes 393224 | tf_op jit(solution)/shard_map/ppermute | solution.py:644
  28.5 3.9 %collective-permute-start.8 = (bf16[256,512]{1,0:T(8,128)(2,1)S(1)}, bf16[256,512]{1,0:T(8,128)(2,1)S(1)}, u32[]{:S(2)}, u32[]{:S(2)}) collective-permute-start(bf16[256,512]{1,0:T(8,128)(2,1)S(1)} %get-tuple-element.61), channel_id=1, source_target_pairs={{12,8},{8,4},{13,9},{9,5},{14,10},{10,6},{15,11},{11,7},{28,24},{2... | collective-permute-start | bytes 786440 | tf_op jit(solution)/shard_map/ppermute | solution.py:672
  29.3 4.5 %copy-start.3 = (f32[256,128]{1,0:T(8,128)S(1)}, f32[256,128]{1,0:T(8,128)}, u32[]{:S(2)}) copy-start(f32[256,128]{1,0:T(8,128)} %get-tuple-element.37.cos_ref) | copy-start | bytes 393220
  29.3 4.5 %copy-start.5 = (f32[256,128]{1,0:T(8,128)S(1)}, f32[256,128]{1,0:T(8,128)}, u32[]{:S(2)}) copy-start(f32[256,128]{1,0:T(8,128)} %get-tuple-element.38.sin_ref) | copy-start | bytes 393220
  30.4 6.1 %collective-permute-start.7 = (bf16[256,256]{1,0:T(8,128)(2,1)S(1)}, bf16[256,256]{1,0:T(8,128)(2,1)S(1)}, u32[]{:S(2)}, u32[]{:S(2)}) collective-permute-start(bf16[256,256]{1,0:T(8,128)(2,1)S(1)} %get-tuple-element.56), channel_id=1, source_target_pairs={{12,8},{8,4},{13,9},{9,5},{14,10},{10,6},{15,11},{11,7},{28,24},{2... | collective-permute-start | bytes 393224 | tf_op jit(solution)/shard_map/ppermute | solution.py:672
  31.1 15.1 %collective-permute-start.11 = (bf16[256,512]{1,0:T(8,128)(2,1)S(1)}, bf16[256,512]{1,0:T(8,128)(2,1)S(1)}, u32[]{:S(2)}, u32[]{:S(2)}) collective-permute-start(bf16[256,512]{1,0:T(8,128)(2,1)S(1)} %get-tuple-element.66), channel_id=1, source_target_pairs={{12,4},{4,0},{13,5},{5,1},{14,6},{6,2},{15,7},{7,3},{28,20},{20,16... | collective-permute-start | bytes 786440 | tf_op jit(solution)/shard_map/ppermute | solution.py:679
  32.5 20.5 %collective-permute-start.9 = (bf16[256,256]{1,0:T(8,128)(2,1)S(1)}, bf16[256,256]{1,0:T(8,128)(2,1)S(1)}, u32[]{:S(2)}, u32[]{:S(2)}) collective-permute-start(bf16[256,256]{1,0:T(8,128)(2,1)S(1)} %add_terms.2.refs_0_), channel_id=1, source_target_pairs={{8,0},{9,1},{10,2},{11,3},{24,16},{25,17},{26,18},{27,19}} | collective-permute-start | bytes 393224 | tf_op jit(solution)/shard_map/ppermute | solution.py:676
  36.6 18.2 %collective-permute-start.10 = (bf16[256,256]{1,0:T(8,128)(2,1)S(1)}, bf16[256,256]{1,0:T(8,128)(2,1)S(1)}, u32[]{:S(2)}, u32[]{:S(2)}) collective-permute-start(bf16[256,256]{1,0:T(8,128)(2,1)S(1)} %add_terms.3.refs_0_), channel_id=1, source_target_pairs={{12,8},{8,0},{13,9},{9,1},{14,10},{10,2},{15,11},{11,3},{28,24},{2... | collective-permute-start | bytes 393224 | tf_op jit(solution)/shard_map/ppermute | solution.py:676

commit v4 on v3

--- a/solution.py
+++ b/solution.py
@@ -74,7 +74,7 @@
 
 
 def prepare_kernel(
-    ctx_size, pos_hbm, keys_hbm, values_hbm, meta_ref, cos_ref, sin_ref, sent_ref, *refs
+    ctx_size, pos_hbm, keys_hbm, values_hbm, meta_ref, table_ref, sent_ref, *refs
 ):
     sent_heads, (pos_ref, keys_ref, values_ref, sems) = refs[:-4], refs[-4:]
     sources = (pos_hbm, keys_hbm, values_hbm)
@@ -96,8 +96,8 @@
     cos_full = jnp.cos(angles)
     front = lax.broadcasted_iota(jnp.int32, angles.shape, 1) < HALF_DIM
     sin_full = jnp.where(front, -jnp.sin(angles), jnp.sin(angles))
-    cos_ref[...] = cos_full
-    sin_ref[...] = sin_full
+    table_ref[:, :HEAD_DIM] = cos_full
+    table_ref[:, HEAD_DIM:] = sin_full
     copies[1].wait()
     copies[2].wait()
     for lane in range(0, keys_ref.shape[1], HEAD_DIM):
@@ -110,7 +110,7 @@
 
 def prepare(positions, keys, values, ctx_size):
     slots, width = keys.shape
-    table = jax.ShapeDtypeStruct((slots, HEAD_DIM), jnp.float32)
+    table = jax.ShapeDtypeStruct((slots, 2 * HEAD_DIM), jnp.float32)
     sent = jax.ShapeDtypeStruct((slots, 2 * width), jnp.bfloat16)
     operands = (positions, keys, values)
     return pl.pallas_call(
@@ -118,12 +118,11 @@
         out_shape=(
             jax.ShapeDtypeStruct((2 * ctx_size,), jnp.int32),
             table,
-            table,
             sent,
             *[jax.ShapeDtypeStruct((slots, 2 * HEAD_DIM), jnp.bfloat16)] * (width // HEAD_DIM),
         ),
         in_specs=[HBM] * 3,
-        out_specs=(SMEM,) + (VMEM,) * (3 + width // HEAD_DIM),
+        out_specs=(SMEM,) + (VMEM,) * (2 + width // HEAD_DIM),
         scratch_shapes=[pltpu.VMEM(operand.shape, operand.dtype) for operand in operands]
         + [pltpu.SemaphoreType.DMA((3,))],
         compiler_params=vmem(positions.shape[1], 54, 60),
@@ -131,41 +130,30 @@
     )(*operands)
 
 
-def queries_kernel(
-    cos_ref,
-    sin_ref,
-    query_ref,
-    grad_ref,
-    sent_ref,
-    turned_ref,
-    turned_t_ref,
-    grad_t_ref,
-    sent_again_ref,
-):
-    sent_again_ref[...] = sent_ref[...]
+def queries_kernel(table_ref, query_ref, grad_ref, turned_ref, turned_t_ref, grad_t_ref):
     for lane in range(0, query_ref.shape[1], HEAD_DIM):
         lanes = slice(lane, lane + HEAD_DIM)
-        query = turn(query_ref[:, lanes].astype(jnp.float32), cos_ref[...], sin_ref[...])
+        query = turn(query_ref[:, lanes].astype(jnp.float32), table_ref[:, :HEAD_DIM], table_ref[:, HEAD_DIM:])
         turned_ref[:, lanes] = query.astype(jnp.bfloat16)
         turned_t_ref[lanes, :] = query.T.astype(jnp.bfloat16)
         grad_t_ref[lanes, :] = grad_ref[:, lanes].astype(jnp.float32).T.astype(jnp.bfloat16)
 
 
-def rotate_queries(cos_full, sin_full, queries, out_grad, sent):
+def rotate_queries(table, queries, out_grad):
     slots, width = queries.shape
     straight = jax.ShapeDtypeStruct((slots, width), jnp.bfloat16)
     across = jax.ShapeDtypeStruct((width, slots), jnp.bfloat16)
     return pl.pallas_call(
         queries_kernel,
-        out_shape=(straight, across, across, jax.ShapeDtypeStruct(sent.shape, sent.dtype)),
-        in_specs=[VMEM] * 5,
-        out_specs=(VMEM,) * 4,
+        out_shape=(straight, across, across),
+        in_specs=[VMEM] * 3,
+        out_specs=(VMEM,) * 3,
         compiler_params=vmem(0, 16, 16),
         cost_estimate=pl.CostEstimate(
             flops=3 * 10**9, bytes_accessed=4 * 1024 * 1024, transcendentals=0
         ),
         name="rotate_queries",
-    )(cos_full, sin_full, queries, out_grad, sent)
+    )(table, queries, out_grad)
 
 
 def stacked(ref, lane, heads, width):
@@ -468,8 +456,7 @@
 def local_kernel(
     key_head,
     meta_ref,
-    cos_ref,
-    sin_ref,
+    table_ref,
     turned_ref,
     grad_ref,
     sent_ref,
@@ -506,7 +493,7 @@
 
     lane = key_head * heads * HEAD_DIM
     for head in range(heads):
-        grad = turn_back((sum_ref[head] * SCORE_SCALE).T, cos_ref[...], sin_ref[...])
+        grad = turn_back((sum_ref[head] * SCORE_SCALE).T, table_ref[:, :HEAD_DIM], table_ref[:, HEAD_DIM:])
         dq_ref[:, head * HEAD_DIM : (head + 1) * HEAD_DIM] = grad.astype(jnp.bfloat16)
     own_ref[...] = terms_of(
         prob_ref[...],
@@ -516,11 +503,11 @@
     )
 
 
-def local_terms(meta, cos_full, sin_full, turned, out_grad, sent, own, key_head, joined, dq, after):
+def local_terms(meta, table, turned, out_grad, sent, own, key_head, joined, dq, after):
     slots = turned.shape[0]
     heads = joined[1].shape[0]
     weight, product, _ = own
-    operands = [meta, cos_full, sin_full, turned, out_grad, sent, weight, product, *joined, *after]
+    operands = [meta, table, turned, out_grad, sent, weight, product, *joined, *after]
     in_specs = [SMEM] + [VMEM] * (len(operands) - 1)
     aliases = {}
     if dq is not None:
@@ -567,10 +554,10 @@
     )(own, arrived, *after)
 
 
-def finish_kernel(ctx_size, key_heads, meta_ref, cos_ref, sin_ref, *refs):
+def finish_kernel(ctx_size, key_heads, meta_ref, table_ref, *refs):
     key_grad_ref, value_grad_ref = refs[-2:]
     owns, terms = refs[:key_heads], list(refs[key_heads:-2])
-    slots = cos_ref.shape[0]
+    slots = table_ref.shape[0]
     live = lax.broadcasted_iota(jnp.int32, (slots, HEAD_DIM), 0) < meta_ref[ctx_size]
     totals = [own[...] for own in owns]
     if relayed(ctx_size):
@@ -588,23 +575,23 @@
             totals[head] += term[:, 2 * head * HEAD_DIM : 2 * (head + 1) * HEAD_DIM]
     for head, total in enumerate(totals):
         lanes = head_lanes(head)
-        key_term = turn_back(total[:, :HEAD_DIM], cos_ref[...], sin_ref[...])
+        key_term = turn_back(total[:, :HEAD_DIM], table_ref[:, :HEAD_DIM], table_ref[:, HEAD_DIM:])
         key_grad_ref[:, lanes] = jnp.where(live, key_term, 0.0).astype(jnp.bfloat16)
         value_grad_ref[:, lanes] = jnp.where(live, total[:, HEAD_DIM:], 0.0).astype(jnp.bfloat16)
 
 
-def finish(meta, cos_full, sin_full, owns, terms, ctx_size):
-    slots = cos_full.shape[0]
+def finish(meta, table, owns, terms, ctx_size):
+    slots = table.shape[0]
     key_heads = len(owns)
     grad = jax.ShapeDtypeStruct((slots, key_heads * HEAD_DIM), jnp.bfloat16)
     return pl.pallas_call(
         functools.partial(finish_kernel, ctx_size, key_heads),
         out_shape=(grad, grad),
-        in_specs=[SMEM] + [VMEM] * (2 + len(owns) + len(terms)),
+        in_specs=[SMEM] + [VMEM] * (1 + len(owns) + len(terms)),
         out_specs=(VMEM, VMEM),
         compiler_params=vmem(0, 16, 16),
         name="finish",
-    )(meta, cos_full, sin_full, *owns, *terms)
+    )(meta, table, *owns, *terms)
 
 
 def climb(sent, ctx_size):
@@ -627,17 +614,15 @@
     ctx_size = lax.axis_size("ctx")
     routed = positions.shape[1]
     key_heads = keys.shape[2] // HEAD_DIM
-    meta, cos_full, sin_full, sent, *sent_heads = prepare(positions, keys[0], values[0], ctx_size)
-    turned, turned_t, grad_t, sent_again = rotate_queries(
-        cos_full, sin_full, queries[0], out_grad[0], sent_heads[0]
-    )
+    meta, table, sent, *sent_heads = prepare(positions, keys[0], values[0], ctx_size)
+    turned, turned_t, grad_t = rotate_queries(table, queries[0], out_grad[0])
     if relayed(ctx_size):
         alphas = [lax.ppermute(part, "ctx", [(0, 2), (2, 3)]) for part in sent_heads]
         beta = lax.ppermute(sent, "ctx", [(1, 3)])
         own, handed = own_scores(sent, turned_t, grad_t, sent_heads[1:] + alphas[1:])
         blocks = []
         for head, alpha in enumerate(alphas):
-            near, far = sent_again, alpha
+            near, far = sent_heads[0], alpha
             if head > 0:
                 near, far = handed[head - 1], handed[head + key_heads - 2]
             gamma = lax.ppermute(near, "ctx", [(0, 1), (1, 2)])
@@ -665,7 +650,7 @@
         terms.append(outs[0])
         joined.append(outs[1])
     local = functools.partial(
-        local_terms, meta, cos_full, sin_full, turned, out_grad[0], sent, own
+        local_terms, meta, table, turned, out_grad[0], sent, own
     )
     dq = None
     if relayed(ctx_size):
@@ -682,7 +667,7 @@
         for head in range(key_heads):
             dq, own_terms = local(head, joined[head], dq, [])
             owns.append(own_terms)
-    key_grad, value_grad = finish(meta, cos_full, sin_full, owns, arrived, ctx_size)
+    key_grad, value_grad = finish(meta, table, owns, arrived, ctx_size)
     return (dq[None], key_grad[None], value_grad[None])
 
 

time: 55.2 us -> 56.4 us (1.022); the launches traced: 56.2 us -> 56.6 us
  waiting for transfers between devices: 14.3 us -> 18.3 us
  starting transfers between devices: 21.1 us -> 19.2 us
  local copies, waits for them, and re-layouts: 5.18 us -> 3.42 us
    ppermute x2, waiting for transfers between devices: 8.51 us -> 14.5 us  [body(): lax.ppermute(total, 'ctx', [(3, 2), (2, 0)] if relays else [(2, 0)])]
    ppermute x2, starting transfers between devices: 9.43 us -> 5.17 us  [body(): lax.ppermute(part, 'ctx', [(0, 2), (2, 3)])]
    ppermute x2, starting transfers between devices: 4.39 us -> 6.84 us  [body(): gamma = lax.ppermute(near, 'ctx', [(0, 1), (1, 2)])]
    ppermute x1, waiting for transfers between devices: 5.67 us -> 3.63 us  [body(): lax.ppermute(terms[-1][1], 'ctx', [(3, 1), (1, 0)])]
    unnamed x22 -> x16, local copies, waits for them, and re-layouts: 5.18 us -> 3.42 us
  transfers between devices with their start and end apart: 12 -> 12, of which waited for: 4 -> 4; matrix products, arithmetic and copies ran while one was open for 0% -> 0% of each run, Pallas kernels for 20% -> 19%
where the time goes in v4:
time: 56.4 us; the launch traced here: 56.6 us
  starting transfers between devices  19.2 us (34%)
  waiting for transfers between devices  18.3 us (32%)
  Pallas kernels  14.8 us (26%)
  local copies, waits for them, and re-layouts  3.42 us (6%)
  between operations  0.89 us (2%)
    ppermute x2, waiting for transfers between devices, body(): lax.ppermute(total, 'ctx', [(3, 2), (2, 0)] if relays else [(2, 0)])  14.5 us
    ppermute x2, starting transfers between devices, body(): gamma = lax.ppermute(near, 'ctx', [(0, 1), (1, 2)])  6.84 us
    pallas_call x2, Pallas kernels, local_terms(): pl.pallas_call(functools.partial(local_kernel, key_head), grid=(1,), out_...  5.45 us
    ppermute x2, starting transfers between devices, body(): lax.ppermute(part, 'ctx', [(0, 2), (2, 3)])  5.17 us
    ppermute x1, waiting for transfers between devices, body(): lax.ppermute(terms[-1][1], 'ctx', [(3, 1), (1, 0)])  3.63 us
    unnamed x16, local copies, waits for them, and re-layouts  3.42 us
    ppermute x2, starting transfers between devices, body(): lax.ppermute(total, 'ctx', [(3, 2), (2, 0)] if relays else [(2, 0)])  2.58 us
    pallas_call x1, Pallas kernels, prepare(): pl.pallas_call(functools.partial(prepare_kernel, ctx_size), out_shape=(ja...  2.34 us
  transfers between devices with their start and end apart: 12, of which 4 were waited for; matrix products, arithmetic and copies ran while one was open for 0% of the time, Pallas kernels for 19%

profile of v4, /device:TPU:0, one launch (start us, length us, event | category | flops | bytes accessed | tf_op | source)
XLA Modules:
  0.0 56.6 jit_solution(7546336793856473481)
XLA Ops:
  0.6 2.3 %prepare.1 = (s32[8]{0:T(128)}, f32[256,256]{1,0:T(8,128)}, bf16[256,512]{1,0:T(8,128)(2,1)}, bf16[256,256]{1,0:T(8,128)(2,1)}, bf16[256,256]{1,0:T(8,128)(2,1)}) custom-call(s32[1,512]{1,0:T(1,128)} %pos_hbm.1, bf16[256,256]{1,0:T(8,128)(2,1)} %bitcast.14, bf16[256,256]{1,0:T(8,128)(2,1)} %bitcast.15), custom_call_target="tpu_custom_call" | custom-call | tf_op jit(solution)/shard_map/prepare/pallas_call | solution.py:116
  3.0 4.9 %collective-permute-start.5 = (bf16[256,256]{1,0:T(8,128)(2,1)}, bf16[256,256]{1,0:T(8,128)(2,1)S(1)}, u32[]{:S(2)}, u32[]{:S(2)}) collective-permute-start(bf16[256,256]{1,0:T(8,128)(2,1)} %get-tuple-element.46), channel_id=1, source_target_pairs={{0,4},{4,8},{1,5},{5,9},{2,6},{6,10},{3,7},{7,11},{16,20},{20,24},... | collective-permute-start | bytes 393224 | tf_op jit(solution)/shard_map/ppermute | solution.py:628
  7.9 2.3 %collective-permute-start.4 = (bf16[256,256]{1,0:T(8,128)(2,1)}, bf16[256,256]{1,0:T(8,128)(2,1)S(1)}, u32[]{:S(2)}, u32[]{:S(2)}) collective-permute-start(bf16[256,256]{1,0:T(8,128)(2,1)} %get-tuple-element.46), channel_id=1, source_target_pairs={{0,8},{8,12},{1,9},{9,13},{2,10},{10,14},{3,11},{11,15},{16,24},{2... | collective-permute-start | bytes 393224 | tf_op jit(solution)/shard_map/ppermute | solution.py:620
  10.2 2.9 %collective-permute-start = (bf16[256,256]{1,0:T(8,128)(2,1)}, bf16[256,256]{1,0:T(8,128)(2,1)S(1)}, u32[]{:S(2)}, u32[]{:S(2)}) collective-permute-start(bf16[256,256]{1,0:T(8,128)(2,1)} %get-tuple-element.40.refs_0_), channel_id=1, source_target_pairs={{0,8},{8,12},{1,9},{9,13},{2,10},{10,14},{3,11},{11,15},{16,24},{2... | collective-permute-start | bytes 393224 | tf_op jit(solution)/shard_map/ppermute | solution.py:620
  13.1 0.7 %collective-permute-start.1 = (bf16[256,512]{1,0:T(8,128)(2,1)}, bf16[256,512]{1,0:T(8,128)(2,1)S(1)}, u32[]{:S(2)}, u32[]{:S(2)}) collective-permute-start(bf16[256,512]{1,0:T(8,128)(2,1)} %get-tuple-element.37.sent_ref), channel_id=1, source_target_pairs={{4,12},{5,13},{6,14},{7,15},{20,28},{21,29},{22,30},{23,31}} | collective-permute-start | bytes 786440 | tf_op jit(solution)/shard_map/ppermute | solution.py:621
  13.8 0.0 copy-start
  13.8 1.2 %copy-done = bf16[1,256,2048]{2,1,0:T(8,128)(2,1)S(1)} copy-done((bf16[1,256,2048]{2,1,0:T(8,128)(2,1)S(1)}, bf16[1,256,2048]{2,1,0:T(8,128)(2,1)}, u32[]{:S(2)}) %copy-start) | copy-done | bytes 1048600
  15.0 0.9 %copy-done.2 = f32[256,256]{1,0:T(8,128)S(1)} copy-done((f32[256,256]{1,0:T(8,128)S(1)}, f32[256,256]{1,0:T(8,128)}, u32[]{:S(2)}) %copy-start.2) | copy-done | bytes 262168
  16.0 1.2 %copy-done.6 = bf16[1,256,2048]{2,1,0:T(8,128)(2,1)S(1)} copy-done((bf16[1,256,2048]{2,1,0:T(8,128)(2,1)S(1)}, bf16[1,256,2048]{2,1,0:T(8,128)(2,1)}, u32[]{:S(2)}) %copy-start.6) | copy-done | bytes 1048600
  17.2 1.1 %rotate_queries.1 = (bf16[256,2048]{1,0:T(8,128)(2,1)S(1)}, bf16[2048,256]{1,0:T(8,128)(2,1)S(1)}, bf16[2048,256]{1,0:T(8,128)(2,1)S(1)}) custom-call(f32[256,256]{1,0:T(8,128)S(1)} %copy-done.2, bf16[256,2048]{1,0:T(8,128)(2,1)S(1)} %bitcast.12, bf16[256,2048]{1,0:T(8,128)(2,1)S(1)} %bitcast.7), custom_call_target="tpu_custom_call" | custom-call | flops 3000000000 | bytes 4194304 | tf_op jit(solution)/shard_map/rotate_queries/pallas_call | solution.py:146
  18.3 0.7 %collective-permute-start.6 = (bf16[256,256]{1,0:T(8,128)(2,1)S(1)}, bf16[256,256]{1,0:T(8,128)(2,1)S(1)}, u32[]{:S(2)}, u32[]{:S(2)}) collective-permute-start(bf16[256,256]{1,0:T(8,128)(2,1)S(1)} %collective-permute-done.4.refs_0_), channel_id=1, source_target_pairs={{8,12},{9,13},{10,14},{11,15},{24,28},{25,29},{26,30},{27,31}} | collective-permute-start | bytes 393224 | tf_op jit(solution)/shard_map/ppermute | solution.py:629
  19.0 0.0 collective-permute-done.refs_1_.refs_0_
  19.1 0.0 copy-start.1
  19.1 2.2 %own_scores.1 = (f32[16,256,256]{2,1,0:T(8,128)S(1)}, f32[16,256,256]{2,1,0:T(8,128)S(1)}, f32[16,8,256]{2,1,0:T(8,128)S(1)}, bf16[256,256]{1,0:T(8,128)(2,1)S(1)}, bf16[256,256]{1,0:T(8,128)(2,1)S(1)}) custom-call(bf16[256,512]{1,0:T(8,128)(2,1)S(1)} %copy-done.4, bf16[2048,256]{1,0:T(8,128)(2,1)S(1)} %get-tuple-element.38.turned_t_ref, ...), custom_call_target="tpu_custom_call" | custom-call | flops 5000000000 | bytes 10485760 | tf_op jit(solution)/shard_map/own_scores/pallas_call | solution.py:231
  21.3 1.9 %collective-permute-start.2 = (bf16[256,256]{1,0:T(8,128)(2,1)S(1)}, bf16[256,256]{1,0:T(8,128)(2,1)S(1)}, u32[]{:S(2)}, u32[]{:S(2)}) collective-permute-start(bf16[256,256]{1,0:T(8,128)(2,1)S(1)} %get-tuple-element.44), channel_id=1, source_target_pairs={{0,4},{4,8},{1,5},{5,9},{2,6},{6,10},{3,7},{7,11},{16,20},{20,24},... | collective-permute-start | bytes 393224 | tf_op jit(solution)/shard_map/ppermute | solution.py:628
  23.2 0.7 %collective-permute-start.3 = (bf16[256,256]{1,0:T(8,128)(2,1)S(1)}, bf16[256,256]{1,0:T(8,128)(2,1)S(1)}, u32[]{:S(2)}, u32[]{:S(2)}) collective-permute-start(bf16[256,256]{1,0:T(8,128)(2,1)S(1)} %get-tuple-element.45), channel_id=1, source_target_pairs={{8,12},{9,13},{10,14},{11,15},{24,28},{25,29},{26,30},{27,31}} | collective-permute-start | bytes 393224 | tf_op jit(solution)/shard_map/ppermute | solution.py:629
  23.9 0.0 collective-permute-done.5.refs_2_
  23.9 0.0 collective-permute-done.6.refs_3_
  24.0 1.0 %scores.2 = (bf16[256,512]{1,0:T(8,128)(2,1)S(1)}, bf16[256,256]{1,0:T(8,128)(2,1)S(1)}, f32[256,256]{1,0:T(8,128)S(1)}, bf16[576,2048]{1,0:T(8,128)(2,1)S(1)}, ...) custom-call(s32[8]{0:T(128)S(1)} %copy-done.5, bf16[256,2048]{1,0:T(8,128)(2,1)S(1)} %get-tuple-element.36.turned_ref, ...), custom_call_target="tpu_custom_call" | custom-call | flops 4000000000 | bytes 6291456 | tf_op jit(solution)/shard_map/scores/pallas_call | solution.py:431
  25.0 0.7 %collective-permute-start.8 = (bf16[256,512]{1,0:T(8,128)(2,1)S(1)}, bf16[256,512]{1,0:T(8,128)(2,1)S(1)}, u32[]{:S(2)}, u32[]{:S(2)}) collective-permute-start(bf16[256,512]{1,0:T(8,128)(2,1)S(1)} %get-tuple-element.57), channel_id=1, source_target_pairs={{12,8},{8,4},{13,9},{9,5},{14,10},{10,6},{15,11},{11,7},{28,24},{2... | collective-permute-start | bytes 786440 | tf_op jit(solution)/shard_map/ppermute | solution.py:657
  25.6 0.1 collective-permute-done.2.refs_2_
  25.7 1.1 %scores.3 = (bf16[256,256]{1,0:T(8,128)(2,1)S(1)}, bf16[256,512]{1,0:T(8,128)(2,1)S(1)}, f32[256,256]{1,0:T(8,128)S(1)}, bf16[576,2048]{1,0:T(8,128)(2,1)S(1)}, ...) custom-call(s32[8]{0:T(128)S(1)} %copy-done.5, bf16[256,2048]{1,0:T(8,128)(2,1)S(1)} %get-tuple-element.36.turned_ref, ...), custom_call_target="tpu_custom_call" | custom-call | flops 4000000000 | bytes 6291456 | tf_op jit(solution)/shard_map/scores/pallas_call | solution.py:431
  26.9 0.7 %collective-permute-start.7 = (bf16[256,256]{1,0:T(8,128)(2,1)S(1)}, bf16[256,256]{1,0:T(8,128)(2,1)S(1)}, u32[]{:S(2)}, u32[]{:S(2)}) collective-permute-start(bf16[256,256]{1,0:T(8,128)(2,1)S(1)} %get-tuple-element.52), channel_id=1, source_target_pairs={{12,8},{8,4},{13,9},{9,5},{14,10},{10,6},{15,11},{11,7},{28,24},{2... | collective-permute-start | bytes 393224 | tf_op jit(solution)/shard_map/ppermute | solution.py:657
  27.6 1.3 %collective-permute-start.11 = (bf16[256,512]{1,0:T(8,128)(2,1)S(1)}, bf16[256,512]{1,0:T(8,128)(2,1)S(1)}, u32[]{:S(2)}, u32[]{:S(2)}) collective-permute-start(bf16[256,512]{1,0:T(8,128)(2,1)S(1)} %get-tuple-element.62), channel_id=1, source_target_pairs={{12,4},{4,0},{13,5},{5,1},{14,6},{6,2},{15,7},{7,3},{28,20},{20,16... | collective-permute-start | bytes 786440 | tf_op jit(solution)/shard_map/ppermute | solution.py:664
  28.9 1.3 %collective-permute-start.9 = (bf16[256,256]{1,0:T(8,128)(2,1)S(1)}, bf16[256,256]{1,0:T(8,128)(2,1)S(1)}, u32[]{:S(2)}, u32[]{:S(2)}) collective-permute-start(bf16[256,256]{1,0:T(8,128)(2,1)S(1)} %add_terms.2.refs_0_), channel_id=1, source_target_pairs={{8,0},{9,1},{10,2},{11,3},{24,16},{25,17},{26,18},{27,19}} | collective-permute-start | bytes 393224 | tf_op jit(solution)/shard_map/ppermute | solution.py:661
  30.2 2.7 %local_terms.2 = (bf16[256,2048]{1,0:T(8,128)(2,1)}, f32[256,256]{1,0:T(8,128)S(1)}) custom-call(s32[8]{0:T(128)S(1)} %copy-done.5, f32[256,256]{1,0:T(8,128)S(1)} %copy-done.3, bf16[256,2048]{1,0:T(8,128)(2,1)S(1)} %get-tuple-element.36.turned_ref, bf16[256,2048]{1,0:T(8,128)(2,1)S(1)} %bitcast.10, bf16[256,512]{1,0:T(8,128)(2,1)S(1)} %copy-done.4, ...), custom_call_target="tpu_custom_call" | custom-call | flops 4000000000 | bytes 10485760 | tf_op jit(solution)/shard_map/local_terms/pallas_call | solution.py:517
  33.0 1.3 %collective-permute-start.10 = (bf16[256,256]{1,0:T(8,128)(2,1)S(1)}, bf16[256,256]{1,0:T(8,128)(2,1)S(1)}, u32[]{:S(2)}, u32[]{:S(2)}) collective-permute-start(bf16[256,256]{1,0:T(8,128)(2,1)S(1)} %add_terms.3.refs_0_), channel_id=1, source_target_pairs={{12,8},{8,0},{13,9},{9,1},{14,10},{10,2},{15,11},{11,3},{28,24},{2... | collective-permute-start | bytes 393224 | tf_op jit(solution)/shard_map/ppermute | solution.py:661
  34.3 2.7 %local_terms.3 = (bf16[256,2048]{1,0:T(8,128)(2,1)}, f32[256,256]{1,0:T(8,128)S(1)}) custom-call(s32[8]{0:T(128)S(1)} %copy-done.5, f32[256,256]{1,0:T(8,128)S(1)} %copy-done.3, bf16[256,2048]{1,0:T(8,128)(2,1)S(1)} %get-tuple-element.36.turned_ref, bf16[256,2048]{1,0:T(8,128)(2,1)S(1)} %bitcast.11, ...), custom_call_target="tpu_custom_call", output_to_operand_aliasing={{0}: (11, {})} | custom-call | flops 4000000000 | bytes 10485760 | tf_op jit(solution)/shard_map/local_terms/pallas_call | solution.py:517
  37.0 3.6 %collective-permute-done.11.refs_6_ = bf16[256,512]{1,0:T(8,128)(2,1)S(1)} collective-permute-done((bf16[256,512]{1,0:T(8,128)(2,1)S(1)}, bf16[256,512]{1,0:T(8,128)(2,1)S(1)}, u32[]{:S(2)}, u32[]{:S(2)}) %collective-permute-start.11) | collective-permute-done | bytes 262176 | tf_op jit(solution)/shard_map/ppermute | solution.py:664
  40.6 12.7 %collective-permute-done.9.refs_4_ = bf16[256,256]{1,0:T(8,128)(2,1)S(1)} collective-permute-done((bf16[256,256]{1,0:T(8,128)(2,1)S(1)}, bf16[256,256]{1,0:T(8,128)(2,1)S(1)}, u32[]{:S(2)}, u32[]{:S(2)}) %collective-permute-start.9) | collective-permute-done | bytes 131104 | tf_op jit(solution)/shard_map/ppermute | solution.py:661
  53.4 1.8 %collective-permute-done.10.refs_5_ = bf16[256,256]{1,0:T(8,128)(2,1)S(1)} collective-permute-done((bf16[256,256]{1,0:T(8,128)(2,1)S(1)}, bf16[256,256]{1,0:T(8,128)(2,1)S(1)}, u32[]{:S(2)}, u32[]{:S(2)}) %collective-permute-start.10) | collective-permute-done | bytes 131104 | tf_op jit(solution)/shard_map/ppermute | solution.py:661
  55.2 1.4 %finish.1 = (bf16[256,256]{1,0:T(8,128)(2,1)}, bf16[256,256]{1,0:T(8,128)(2,1)}) custom-call(s32[8]{0:T(128)S(1)} %copy-done.5, f32[256,256]{1,0:T(8,128)S(1)} %copy-done.3, f32[256,256]{1,0:T(8,128)S(1)} %get-tuple-element.58.refs_0_, f32[256,256]{1,0:T(8,128)S(1)} %get-tuple-element.61.refs_1_, ...), custom_call_target="tpu_custom_call" | custom-call | tf_op jit(solution)/shard_map/finish/pallas_call | solution.py:587
  (18 shorter events, 0.1 us)
Async XLA Ops:
  3.0 20.9 %collective-permute-start.5 = (bf16[256,256]{1,0:T(8,128)(2,1)}, bf16[256,256]{1,0:T(8,128)(2,1)S(1)}, u32[]{:S(2)}, u32[]{:S(2)}) collective-permute-start(bf16[256,256]{1,0:T(8,128)(2,1)} %get-tuple-element.46), channel_id=1, source_target_pairs={{0,4},{4,8},{1,5},{5,9},{2,6},{6,10},{3,7},{7,11},{16,20},{20,24},... | collective-permute-start | bytes 393224 | tf_op jit(solution)/shard_map/ppermute | solution.py:628
  7.9 10.4 %collective-permute-start.4 = (bf16[256,256]{1,0:T(8,128)(2,1)}, bf16[256,256]{1,0:T(8,128)(2,1)S(1)}, u32[]{:S(2)}, u32[]{:S(2)}) collective-permute-start(bf16[256,256]{1,0:T(8,128)(2,1)} %get-tuple-element.46), channel_id=1, source_target_pairs={{0,8},{8,12},{1,9},{9,13},{2,10},{10,14},{3,11},{11,15},{16,24},{2... | collective-permute-start | bytes 393224 | tf_op jit(solution)/shard_map/ppermute | solution.py:620
  10.2 8.8 %collective-permute-start = (bf16[256,256]{1,0:T(8,128)(2,1)}, bf16[256,256]{1,0:T(8,128)(2,1)S(1)}, u32[]{:S(2)}, u32[]{:S(2)}) collective-permute-start(bf16[256,256]{1,0:T(8,128)(2,1)} %get-tuple-element.40.refs_0_), channel_id=1, source_target_pairs={{0,8},{8,12},{1,9},{9,13},{2,10},{10,14},{3,11},{11,15},{16,24},{2... | collective-permute-start | bytes 393224 | tf_op jit(solution)/shard_map/ppermute | solution.py:620
  13.1 10.8 %collective-permute-start.1 = (bf16[256,512]{1,0:T(8,128)(2,1)}, bf16[256,512]{1,0:T(8,128)(2,1)S(1)}, u32[]{:S(2)}, u32[]{:S(2)}) collective-permute-start(bf16[256,512]{1,0:T(8,128)(2,1)} %get-tuple-element.37.sent_ref), channel_id=1, source_target_pairs={{4,12},{5,13},{6,14},{7,15},{20,28},{21,29},{22,30},{23,31}} | collective-permute-start | bytes 786440 | tf_op jit(solution)/shard_map/ppermute | solution.py:621
  13.8 1.2 %copy-start = (bf16[1,256,2048]{2,1,0:T(8,128)(2,1)S(1)}, bf16[1,256,2048]{2,1,0:T(8,128)(2,1)}, u32[]{:S(2)}) copy-start(bf16[1,256,2048]{2,1,0:T(8,128)(2,1)} %param.9) | copy-start | bytes 3145732
  15.0 0.9 %copy-start.2 = (f32[256,256]{1,0:T(8,128)S(1)}, f32[256,256]{1,0:T(8,128)}, u32[]{:S(2)}) copy-start(f32[256,256]{1,0:T(8,128)} %get-tuple-element.35.table_ref) | copy-start | bytes 786436
  16.0 1.2 %copy-start.6 = (bf16[1,256,2048]{2,1,0:T(8,128)(2,1)S(1)}, bf16[1,256,2048]{2,1,0:T(8,128)(2,1)}, u32[]{:S(2)}) copy-start(bf16[1,256,2048]{2,1,0:T(8,128)(2,1)} %param.6) | copy-start | bytes 3145732
  17.2 1.8 %copy-start.4 = (bf16[256,512]{1,0:T(8,128)(2,1)S(1)}, bf16[256,512]{1,0:T(8,128)(2,1)}, u32[]{:S(2)}) copy-start(bf16[256,512]{1,0:T(8,128)(2,1)} %get-tuple-element.37.sent_ref) | copy-start | bytes 786436
  17.2 1.9 %copy-start.7 = (bf16[256,256]{1,0:T(8,128)(2,1)S(1)}, bf16[256,256]{1,0:T(8,128)(2,1)}, u32[]{:S(2)}) copy-start(bf16[256,256]{1,0:T(8,128)(2,1)} %get-tuple-element.40.refs_0_) | copy-start | bytes 393220
  18.3 5.6 %collective-permute-start.6 = (bf16[256,256]{1,0:T(8,128)(2,1)S(1)}, bf16[256,256]{1,0:T(8,128)(2,1)S(1)}, u32[]{:S(2)}, u32[]{:S(2)}) collective-permute-start(bf16[256,256]{1,0:T(8,128)(2,1)S(1)} %collective-permute-done.4.refs_0_), channel_id=1, source_target_pairs={{8,12},{9,13},{10,14},{11,15},{24,28},{25,29},{26,30},{27,31}} | collective-permute-start | bytes 393224 | tf_op jit(solution)/shard_map/ppermute | solution.py:629
  19.1 4.9 %copy-start.1 = (bf16[1,256,2048]{2,1,0:T(8,128)(2,1)S(1)}, bf16[1,256,2048]{2,1,0:T(8,128)(2,1)}, u32[]{:S(2)}) copy-start(bf16[1,256,2048]{2,1,0:T(8,128)(2,1)} %param.9) | copy-start | bytes 3145732
  19.1 4.9 %copy-start.5 = (s32[8]{0:T(128)S(1)}, s32[8]{0:T(128)}, u32[]{:S(2)}) copy-start(s32[8]{0:T(128)} %get-tuple-element.34.meta_ref) | copy-start | bytes 100
  21.3 4.4 %collective-permute-start.2 = (bf16[256,256]{1,0:T(8,128)(2,1)S(1)}, bf16[256,256]{1,0:T(8,128)(2,1)S(1)}, u32[]{:S(2)}, u32[]{:S(2)}) collective-permute-start(bf16[256,256]{1,0:T(8,128)(2,1)S(1)} %get-tuple-element.44), channel_id=1, source_target_pairs={{0,4},{4,8},{1,5},{5,9},{2,6},{6,10},{3,7},{7,11},{16,20},{20,24},... | collective-permute-start | bytes 393224 | tf_op jit(solution)/shard_map/ppermute | solution.py:628
  23.2 2.5 %collective-permute-start.3 = (bf16[256,256]{1,0:T(8,128)(2,1)S(1)}, bf16[256,256]{1,0:T(8,128)(2,1)S(1)}, u32[]{:S(2)}, u32[]{:S(2)}) collective-permute-start(bf16[256,256]{1,0:T(8,128)(2,1)S(1)} %get-tuple-element.45), channel_id=1, source_target_pairs={{8,12},{9,13},{10,14},{11,15},{24,28},{25,29},{26,30},{27,31}} | collective-permute-start | bytes 393224 | tf_op jit(solution)/shard_map/ppermute | solution.py:629
  25.0 3.9 %collective-permute-start.8 = (bf16[256,512]{1,0:T(8,128)(2,1)S(1)}, bf16[256,512]{1,0:T(8,128)(2,1)S(1)}, u32[]{:S(2)}, u32[]{:S(2)}) collective-permute-start(bf16[256,512]{1,0:T(8,128)(2,1)S(1)} %get-tuple-element.57), channel_id=1, source_target_pairs={{12,8},{8,4},{13,9},{9,5},{14,10},{10,6},{15,11},{11,7},{28,24},{2... | collective-permute-start | bytes 786440 | tf_op jit(solution)/shard_map/ppermute | solution.py:657
  25.7 4.5 %copy-start.3 = (f32[256,256]{1,0:T(8,128)S(1)}, f32[256,256]{1,0:T(8,128)}, u32[]{:S(2)}) copy-start(f32[256,256]{1,0:T(8,128)} %get-tuple-element.35.table_ref) | copy-start | bytes 786436
  26.9 6.1 %collective-permute-start.7 = (bf16[256,256]{1,0:T(8,128)(2,1)S(1)}, bf16[256,256]{1,0:T(8,128)(2,1)S(1)}, u32[]{:S(2)}, u32[]{:S(2)}) collective-permute-start(bf16[256,256]{1,0:T(8,128)(2,1)S(1)} %get-tuple-element.52), channel_id=1, source_target_pairs={{12,8},{8,4},{13,9},{9,5},{14,10},{10,6},{15,11},{11,7},{28,24},{2... | collective-permute-start | bytes 393224 | tf_op jit(solution)/shard_map/ppermute | solution.py:657
  27.6 13.1 %collective-permute-start.11 = (bf16[256,512]{1,0:T(8,128)(2,1)S(1)}, bf16[256,512]{1,0:T(8,128)(2,1)S(1)}, u32[]{:S(2)}, u32[]{:S(2)}) collective-permute-start(bf16[256,512]{1,0:T(8,128)(2,1)S(1)} %get-tuple-element.62), channel_id=1, source_target_pairs={{12,4},{4,0},{13,5},{5,1},{14,6},{6,2},{15,7},{7,3},{28,20},{20,16... | collective-permute-start | bytes 786440 | tf_op jit(solution)/shard_map/ppermute | solution.py:664
  28.9 24.4 %collective-permute-start.9 = (bf16[256,256]{1,0:T(8,128)(2,1)S(1)}, bf16[256,256]{1,0:T(8,128)(2,1)S(1)}, u32[]{:S(2)}, u32[]{:S(2)}) collective-permute-start(bf16[256,256]{1,0:T(8,128)(2,1)S(1)} %add_terms.2.refs_0_), channel_id=1, source_target_pairs={{8,0},{9,1},{10,2},{11,3},{24,16},{25,17},{26,18},{27,19}} | collective-permute-start | bytes 393224 | tf_op jit(solution)/shard_map/ppermute | solution.py:661
  33.0 22.2 %collective-permute-start.10 = (bf16[256,256]{1,0:T(8,128)(2,1)S(1)}, bf16[256,256]{1,0:T(8,128)(2,1)S(1)}, u32[]{:S(2)}, u32[]{:S(2)}) collective-permute-start(bf16[256,256]{1,0:T(8,128)(2,1)S(1)} %add_terms.3.refs_0_), channel_id=1, source_target_pairs={{12,8},{8,0},{13,9},{9,1},{14,10},{10,2},{15,11},{11,3},{28,24},{2... | collective-permute-start | bytes 393224 | tf_op jit(solution)/shard_map/ppermute | solution.py:661
